TPU v7x, 256 devices: a whole 4x4x8 slice. The times are simulated.
256 devices in a mesh: tmpl: 64 (over x_hi, y, z), chan: 4 (over x_lo, core).
Axes of the slice: x: 4 (x_hi: 2, x_lo: 2; x = x_hi * 2 + x_lo), y: 4, z: 8, core: 2. Of those that a mesh axis runs over, the one named last changes fastest.
Arguments:
- data_spec: float32 [2, 600, 1024], P(None, 'chan', 'tmpl')
- tmpl_spec: float32 [2, 256, 600, 1024], P(None, 'tmpl', 'chan'), may hold values from -6 to 6
- shifts: int32 [256, 600], P('tmpl', 'chan'), may hold values from 0 to 255
- mask: int32 [256, 600], P('tmpl', 'chan'), may hold values 0 or 1
Outputs:
- stack: float32 [256, 3072], P('tmpl', 'chan')
All inputs are finite; a program needn't handle non-finite values. No bound on the sum of `mask` on one device may be relied on, other than what follows from the above.
Results may differ from a plain program's by a relative error of at most 0.0003.
Values sent between devices are 32-bit elements; how exact they have to be, the bound alone decides.
No kernel may reach another device: no remote copies, remote signals or barrier semaphores. Data moves between devices by JAX's collectives and lax.ppermute only.
A program may use at most 64 MiB of HBM per device.

v0:
```python
import math

import jax
import jax.numpy as jnp
from jax import lax
from jax.sharding import PartitionSpec as P

FREQS = 1024
FIRST = 128
NFFT = 4096
LAGS = 3072


full_turn = 2.0 * math.pi


def network_piece(piece, start, data_scale, tmpl_spec, shifts, weight):
    count = piece.shape[2]
    data_re = piece[0] * data_scale[:, None]
    data_im = piece[1] * data_scale[:, None]
    bins = FIRST + start + jnp.arange(count, dtype=jnp.int32)
    turns = bins[None, None, :] * shifts[:, :, None] % NFFT
    phase = full_turn * turns.astype(jnp.float32) / NFFT
    cosine = jnp.cos(phase)
    sine = jnp.sin(phase)
    prod_re = tmpl_spec[0] * data_re[None] + tmpl_spec[1] * data_im[None]
    prod_im = tmpl_spec[0] * data_im[None] - tmpl_spec[1] * data_re[None]
    shift_re = prod_re * cosine - prod_im * sine
    shift_im = prod_re * sine + prod_im * cosine
    out_re = jnp.sum(weight[:, :, None] * shift_re, axis=1)
    out_im = jnp.sum(weight[:, :, None] * shift_im, axis=1)
    return jnp.stack([out_re, out_im])


def to_lags(spectra, lags, bins):
    turns = bins[:, None] * lags[None, :] % NFFT
    angle = full_turn * turns.astype(jnp.float32) / NFFT
    high = lax.Precision.HIGHEST
    result = jnp.dot(spectra[0], jnp.cos(angle), precision=high) - jnp.dot(
        spectra[1], jnp.sin(angle), precision=high
    )
    return result / FREQS


def on_device(data_spec, tmpl_spec, shifts, mask):
    spec_power = jnp.sum(tmpl_spec[0] * tmpl_spec[0] + tmpl_spec[1] * tmpl_spec[1], axis=2) / FREQS
    weight = mask.astype(jnp.float32) / jnp.sqrt(spec_power + 1e-06)
    whole = lax.all_gather(data_spec, "tmpl", axis=2, tiled=True)
    power = jnp.sum(whole[0] * whole[0] + whole[1] * whole[1], axis=1)
    data_scale = 1.0 / jnp.sqrt(power / FREQS + 1e-06)
    network = network_piece(whole, 0, data_scale, tmpl_spec, shifts, weight)
    lag_dev = LAGS // lax.axis_size("chan")
    bins = FIRST + jnp.arange(FREQS, dtype=jnp.int32)
    summed = lax.psum(network, "chan")
    lags = lax.axis_index("chan") * lag_dev + jnp.arange(lag_dev, dtype=jnp.int32)
    stack = to_lags(summed, lags, bins)
    return stack


def solution(mesh):
    return jax.shard_map(
        on_device,
        mesh=mesh,
        in_specs=(
            P(None, "chan", "tmpl"),
            P(None, "tmpl", "chan", None),
            P("tmpl", "chan"),
            P("tmpl", "chan"),
        ),
        out_specs=P("tmpl", "chan"),
        check_vma=False,
    )
```

profile of v0, /device:TPU:1, one launch (start us, length us, event | category | flops | bytes accessed | tf_op | source)
XLA Modules:
  0.0 204.6 jit_solution(15871767320276072342)
XLA Ops:
  6.5 0.0 all-gather.2.cloned.1.call-start
  6.5 0.7 all-gather.2.cloned.1.call-update
  7.3 0.0 copy-start.1
  7.3 0.0 copy-start.2
  7.3 3.3 %fusion.11 = f32[4,150]{0,1:T(8,128)S(1)} fusion(f32[2,4,150,1024]{3,1,2,0:T(4,128)} %param.5), kind=kLoop, calls=%fused_computation.24 | loop fusion | flops 2457000 | bytes 4917600 | tf_op jit(solution)/shard_map/reduce_sum | solution.py:46
  10.6 0.1 copy.15
  10.7 0.0 copy-done.1
  10.7 0.1 copy.16
  10.8 0.0 copy-done.2
  10.8 0.1 copy.19
  11.0 118.4 %all-gather.2.cloned.1.call-done = f32[2,150,1024]{1,2,0:T(8,128)} async-done(((f32[2,150,16]{1,2,0:T(8,128)}), f32[2,150,1024]{1,2,0:T(8,128)}) %all-gather.2.cloned.1.call-update) | async-done | bytes 1228816 | tf_op jit(solution)/shard_map/all_gather | solution.py:48
  129.4 0.0 copy-start
  129.4 1.9 add_reduce_fusion
  131.3 0.3 copy-done
  131.6 0.1 multiply_bitcast_fusion
  131.7 0.3 copy.17
  132.0 0.3 copy.18
  132.3 24.6 %multiply_reduce_fusion.1 = (f32[4,1024]{1,0:T(4,128)S(1)}, f32[4,1024]{1,0:T(4,128)S(1)}) fusion(s32[4,150]{0,1:T(8,128)S(1)} %copy.19, s32[1024]{0:T(1024)S(1)} %iota_add_fusion.1, f32[4,150]{0,1:T(8,128)S(1)} %copy.16, f32[150,1024]{1,0:T(8,128)S(1)} %copy.17, f32[2,4,150,1024]{3,1,2,0:T(4,128)} %param.5, f32[150,1024]{1,0:T(8,128)S(1)} %copy.18), kind=kLoop, calls=%fused_computation.31 | loop fusion | flops 18423808 | bytes 6185664 | tf_op jit(solution)/shard_map/reduce_sum | solution.py:30
  157.0 13.4 %psum.7 = f32[2,4,1024]{2,1,0:T(4,128)S(1)} all-reduce(f32[2,4,1024]{2,1,0:T(4,128)S(1)} %pad_maximum_fusion), channel_id=1, replica_groups=mesh['tmpl'=64,'chan'=4] {'chan'}, use_global_device_ids=true, to_apply=%region_4.5 | all-reduce | flops 8192 | bytes 65536 | tf_op jit(solution)/shard_map/psum | solution.py:54
  170.4 13.4 %fusion.3 = f32[4,768]{1,0:T(4,128)S(1)} fusion(s32[768]{0:T(1024)S(1)} %iota_add_fusion, s32[1024]{0:T(1024)S(1)} %iota_add_fusion.1, f32[2,4,1024]{2,1,0:T(4,128)S(1)} %psum.7), kind=kOutput, calls=%fused_computation.13 | convolution fusion | flops 48758784 | bytes 36864 | tf_op jit(solution)/shard_map/dot_general | solution.py:39
  183.8 14.0 %fusion.21 = f32[4,768]{1,0:T(4,128)} fusion(f32[4,768]{1,0:T(4,128)S(1)} %fusion.3, s32[768]{0:T(1024)S(1)} %iota_add_fusion, s32[1024]{0:T(1024)S(1)} %iota_add_fusion.1, f32[2,4,1024]{2,1,0:T(4,128)S(1)} %psum.7), kind=kOutput, calls=%fused_computation.35 | convolution fusion | flops 48764928 | bytes 49152 | tf_op jit(solution)/shard_map/dot_general | solution.py:39
  (5 shorter events, 0.0 us)
Async XLA Ops:
  6.5 122.8 %all-gather.2.cloned.1.call-start = ((), (), s32[]{:S(2)}) async-start(), calls=%async_computation | async-start | bytes 2129920 | tf_op jit(solution)/shard_map/all_gather | solution.py:48
  7.3 3.4 %copy-start.1 = (s32[4,150]{1,0:T(4,128)S(1)}, s32[4,150]{1,0:T(4,128)}, u32[]{:S(2)}) copy-start(s32[4,150]{1,0:T(4,128)} %param.7) | copy-start | bytes 7204
  7.3 3.5 %copy-start.2 = (s32[4,150]{1,0:T(4,128)S(1)}, s32[4,150]{1,0:T(4,128)}, u32[]{:S(2)}) copy-start(s32[4,150]{1,0:T(4,128)} %param.6) | copy-start | bytes 7204
  129.4 2.2 %copy-start = (f32[2,150,1024]{1,2,0:T(8,128)S(1)}, f32[2,150,1024]{1,2,0:T(8,128)}, u32[]{:S(2)}) copy-start(f32[2,150,1024]{1,2,0:T(8,128)} %all-gather.2.cloned.1.call-done) | copy-start | bytes 3686404
Sparse Core Ops, SparseCore 0:
  10.9 118.4 all-gather.1
where the time goes:
time: 205 us
  waiting for transfers between devices  119 us (58%)
  other arithmetic  30 us (15%)
  matrix products  27.4 us (13%)
  between operations  13.5 us (7%)
  blocking collectives  13.4 us (7%)
    all_gather x1, waiting for transfers between devices, on_device(): whole = lax.all_gather(data_spec, 'tmpl', axis=2, tiled=True)  118 us
    reduce_sum x1, other arithmetic, network_piece(): out_re = jnp.sum(weight[:, :, None] * shift_re, axis=1)  24.6 us
    dot_general x1, matrix products, to_lags(): jnp.dot(spectra[0], jnp.cos(angle), precision=high)  14 us
    psum x1, blocking collectives, on_device(): summed = lax.psum(network, 'chan')  13.4 us
    dot_general x1, matrix products, to_lags(): jnp.dot(spectra[1], jnp.sin(angle), precision=high)  13.4 us
  transfers between devices with their start and end apart: 1, of which 1 were waited for; matrix products, arithmetic and copies ran while one was open for 2% of the time, Pallas kernels for 0%

commit v1 on v0

v1 whole, which is shorter than its diff:
```python
import math

import jax
import jax.numpy as jnp
import numpy as np
from jax import lax
from jax.experimental import pallas as pl
from jax.experimental.pallas import tpu as pltpu
from jax.sharding import PartitionSpec as P

FREQS = 1024
FIRST = 128
NFFT = 4096
LAGS = 3072
CHANS = 150
ROWS = 152
TMPL = 4
XH, YS, ZS = 2, 4, 8

VMEM = pl.BlockSpec(memory_space=pltpu.VMEM)
HIGH = lax.Precision.HIGHEST
PARAMS = pltpu.CompilerParams(vmem_limit_bytes=48 << 20)


def from_offset(x, dx=0, dy=0, dz=0):
    pairs = []
    for i in range(XH * YS * ZS):
        a, b, c = i // (YS * ZS), i // ZS % YS, i % ZS
        src = (a + dx) % XH * (YS * ZS) + (b + dy) % YS * ZS + (c + dz) % ZS
        pairs.append((src, i))
    return lax.ppermute(x, "tmpl", pairs)


def sincos(turns):
    moved = turns + 512
    quad = moved >> 10
    theta = ((moved & 1023) - 512).astype(jnp.float32) * (2.0 * math.pi / NFFT)
    sq = theta * theta
    sin = theta * (1.0 + sq * (-1.0 / 6 + sq * (1.0 / 120 + sq * (-1.0 / 5040))))
    cos = 1.0 + sq * (-0.5 + sq * (1.0 / 24 + sq * (-1.0 / 720 + sq * (1.0 / 40320))))
    odd = (quad & 1) != 0
    c = jnp.where(odd, sin, cos)
    s = jnp.where(odd, cos, sin)
    c = jnp.where(((quad + 1) & 2) != 0, -c, c)
    s = jnp.where((quad & 2) != 0, -s, s)
    return c, s


def template_kernel(spec_ref, shift_ref, mask_ref, out_ref, code_ref):
    code = shift_ref[...] + 256 * mask_ref[...]
    code_ref[0:4, 0:CHANS] = code
    code_ref[4:8, 0:CHANS] = code
    row = lax.broadcasted_iota(jnp.int32, (8, 128), 0)
    lane = lax.broadcasted_iota(jnp.int32, (8, 128), 1)
    first_bin = FIRST * (row // 4 + 1) + lane

    def channel(c, codes, at):
        col = jnp.broadcast_to(pltpu.roll(codes, (128 - at) % 128, 1)[:, 0:1], (8, 128))
        move = col & 255
        used = (col >> 8).astype(jnp.float32)
        er, ei = sincos((first_bin * move) & (NFFT - 1))
        wr, wi = sincos((256 * move) & (NFFT - 1))
        re = [spec_ref[0, c, m] for m in range(4)]
        im = [spec_ref[1, c, m] for m in range(4)]
        power = sum(a * a + b * b for a, b in zip(re, im))
        power = jnp.broadcast_to(jnp.sum(power, axis=1, keepdims=True), (8, 128))
        power = power + pltpu.roll(power, 4, 0)
        weight = used / jnp.sqrt(power * (1.0 / FREQS) + 1e-06)
        er, ei = er * weight, ei * weight
        for m in range(4):
            out_ref[c, 0, m] = re[m] * er + im[m] * ei
            out_ref[c, 1, m] = re[m] * ei - im[m] * er
            if m < 3:
                er, ei = er * wr - ei * wi, er * wi + ei * wr

    for start, count, unroll in ((0, 128, 4), (128, CHANS - 128, 2)):
        codes = code_ref[:, start : start + 128]

        def step(i, carry, start=start, unroll=unroll, codes=codes):
            for j in range(unroll):
                at = i * unroll + j
                channel(start + at, codes, at)
            return carry

        lax.fori_loop(0, count // unroll, step, 0)


def template_part(tmpl_spec, shifts, mask):
    view = tmpl_spec.reshape(2, TMPL, CHANS, 4, 2, 128).transpose(0, 2, 3, 4, 1, 5)
    view = view.reshape(2, CHANS, 4, 8, 128)
    return pl.pallas_call(
        template_kernel,
        out_shape=jax.ShapeDtypeStruct((CHANS, 2, 4, 8, 128), jnp.float32),
        in_specs=[VMEM] * 3,
        out_specs=VMEM,
        scratch_shapes=[pltpu.VMEM((8, 256), jnp.int32)],
        compiler_params=PARAMS,
    )(view, shifts, mask)


Z_ORDER = (0, 1, -1, 2, -2, 3, 4, -3)


def pack_kernel(*refs):
    parts, out_ref, held = refs[:8], refs[8], refs[9]
    z = lax.axis_index("tmpl") % ZS
    for part, dz in zip(parts, Z_ORDER):
        at = pl.multiple_of(lax.rem(z + dz + ZS, ZS) * 16, 16)
        for k in range(2):
            held[k, pl.ds(at, 16), 0:CHANS] = part[k]
    for k in range(2):
        out_ref[k, 0:128, :] = held[k, :, 0:128].T
        out_ref[k, 128:ROWS, :] = held[k, :, 128:256].T[0 : ROWS - 128]


def gather_z(data_spec):
    own = data_spec.transpose(0, 2, 1)
    up = from_offset(own, dz=1)
    down = from_offset(own, dz=-1)
    up2 = from_offset(own, dz=2)
    down2 = from_offset(own, dz=-2)
    up3 = from_offset(up2, dz=1)
    up4 = from_offset(up2, dz=2)
    down3 = from_offset(down2, dz=-1)
    return pl.pallas_call(
        pack_kernel,
        out_shape=jax.ShapeDtypeStruct((2, ROWS, 128), jnp.float32),
        in_specs=[VMEM] * 8,
        out_specs=VMEM,
        scratch_shapes=[pltpu.VMEM((2, 128, 256), jnp.float32)],
        compiler_params=PARAMS,
    )(own, up, down, up2, down2, up3, up4, down3)


XY_ORDER = ((0, 0), (1, 0), (0, 1), (0, -1), (1, 1), (1, -1), (1, 2), (0, 2))


def gather_xy(own):
    ax = from_offset(own, dx=1)
    up = from_offset(own, dy=1)
    down = from_offset(own, dy=-1)
    far = from_offset(ax, dy=2)
    xup = from_offset(up, dx=1)
    xdown = from_offset(down, dx=1)
    re2 = from_offset(up[0], dy=1)
    im2 = from_offset(down[1], dy=-1)
    return own, ax, up, down, xup, xdown, far, re2, im2


def tables():
    kl = np.arange(32)
    fh = np.arange(8)
    a = 2 * np.pi * (np.outer(kl, fh + 1) % 32) / 32
    first = np.zeros((2, TMPL, 32, 2, 4, 2, TMPL))
    for t in range(TMPL):
        c, s = np.cos(a).reshape(32, 4, 2), np.sin(a).reshape(32, 4, 2)
        first[0, t, :, 0, :, :, t] = c
        first[0, t, :, 1, :, :, t] = -s
        first[1, t, :, 0, :, :, t] = s
        first[1, t, :, 1, :, :, t] = c
    fl = np.arange(128)
    b = np.tile(2 * np.pi * np.outer(kl, fl) / NFFT, (TMPL, 1))
    kh = (4 * np.arange(24)[None, :] + np.arange(4)[:, None]).reshape(96)
    g = 2 * np.pi * (np.outer(kh, fl) % 128) / 128
    rows = [first.reshape(256, 64)]
    twist = np.stack([np.cos(b), np.sin(b)])
    last = np.stack([np.cos(g), -np.sin(g)]) / FREQS
    return tuple(np.asarray(v, np.float32) for v in (rows[0], twist, last))


def network_kernel(*refs):
    spec_ref = refs[0]
    blocks = refs[1:8]
    re2_ref, im2_ref, first_ref, twist_ref, last_ref = refs[8:13]
    keep_ref, send_ref, data_ref, piece_ref = refs[13:]
    me = lax.axis_index("tmpl")
    x, y = me // (YS * ZS), me // ZS % YS

    def block(q, k):
        if q < 7:
            return blocks[q][k]
        return (re2_ref, im2_ref)[k][...]

    power = None
    for q in range(8):
        re, im = block(q, 0), block(q, 1)
        one = re * re + im * im
        power = one if power is None else power + one
    power = jnp.sum(power, axis=1, keepdims=True)
    scale = jnp.broadcast_to(1.0 / jnp.sqrt(power * (1.0 / FREQS) + 1e-06), (ROWS, 128))
    for q, (dx, dy) in enumerate(XY_ORDER):
        group = lax.rem(x + dx, XH) * YS + lax.rem(y + dy + YS, YS)
        for k in range(2):
            data_ref[group, k] = block(q, k) * scale

    lower = lax.broadcasted_iota(jnp.int32, (8, 128), 0) < 4

    def channel(c, acc):
        acc = list(acc)
        for m in range(4):
            d = []
            for k in range(2):
                one = jnp.broadcast_to(data_ref[2 * m, k, pl.ds(c, 1), :], (8, 128))
                two = jnp.broadcast_to(data_ref[2 * m + 1, k, pl.ds(c, 1), :], (8, 128))
                d.append(jnp.where(lower, one, two))
            tr, ti = spec_ref[c, 0, m], spec_ref[c, 1, m]
            acc[m] = acc[m] + (tr * d[0] - ti * d[1])
            acc[4 + m] = acc[4 + m] + (tr * d[1] + ti * d[0])
        return tuple(acc)

    zero = jnp.zeros((8, 128), jnp.float32)
    acc = lax.fori_loop(0, CHANS, channel, (zero,) * 8, unroll=5)
    spectra = jnp.concatenate(acc, axis=0)
    mixed = jnp.dot(first_ref[...], spectra, precision=HIGH, preferred_element_type=jnp.float32)
    yr, yi = mixed[0:128], mixed[128:256]
    tc, ts = twist_ref[0], twist_ref[1]
    zr, zi = yr * tc - yi * ts, yr * ts + yi * tc
    dims = (((1,), (1,)), ((), ()))
    lags = lax.dot_general(last_ref[0], zr, dims, precision=HIGH, preferred_element_type=jnp.float32)
    lags = lags + lax.dot_general(last_ref[1], zi, dims, precision=HIGH, preferred_element_type=jnp.float32)
    lane = lax.broadcasted_iota(jnp.int32, (24, 128), 1) // 32
    chan = lax.axis_index("chan")
    for t in range(TMPL):
        out = None
        for r in range(4):
            part = lags[24 * r : 24 * r + 24]
            if (r - t) % 4:
                part = pltpu.roll(part, (r - t) % 4 * 32, 1)
            out = part if out is None else jnp.where(lane == r, part, out)
        for j in range(4):
            for g in range(6):
                piece_ref[j ^ chan, t : t + 1, g * 128 : (g + 1) * 128] = out[6 * j + g : 6 * j + g + 1]
    keep_ref[0] = piece_ref[0]
    keep_ref[1] = piece_ref[2]
    send_ref[0] = piece_ref[1]
    send_ref[1] = piece_ref[3]


def network_part(spectra, blocks):
    lag_dev = LAGS // 4
    shape = jax.ShapeDtypeStruct((2, TMPL, lag_dev), jnp.float32)
    return pl.pallas_call(
        network_kernel,
        out_shape=(shape, shape),
        in_specs=[VMEM] * 13,
        out_specs=(VMEM, VMEM),
        scratch_shapes=[
            pltpu.VMEM((8, 2, ROWS, 128), jnp.float32),
            pltpu.VMEM((4, TMPL, lag_dev), jnp.float32),
        ],
        compiler_params=PARAMS,
    )(spectra, *blocks, *tables())


def on_device(data_spec, tmpl_spec, shifts, mask):
    spectra = template_part(tmpl_spec, shifts, mask)
    blocks = gather_xy(gather_z(data_spec))
    keep, send = network_part(spectra, blocks)
    got = lax.ppermute(send, "chan", [(i, i ^ 1) for i in range(4)])
    other = lax.ppermute(keep[1] + got[1], "chan", [(i, i ^ 2) for i in range(4)])
    return keep[0] + got[0] + other


def solution(mesh):
    return jax.shard_map(
        on_device,
        mesh=mesh,
        in_specs=(
            P(None, "chan", "tmpl"),
            P(None, "tmpl", "chan", None),
            P("tmpl", "chan"),
            P("tmpl", "chan"),
        ),
        out_specs=P("tmpl", "chan"),
        check_vma=False,
    )
```

time: 205 us -> 58.7 us (0.29)
  waiting for transfers between devices: 119 us -> 4.68 us
  starting transfers between devices: 0.01 us -> 32 us
  other arithmetic: 30 us -> 0.61 us
  matrix products: 27.4 us -> 0 us
  Pallas kernels: 0 us -> 16.2 us
  blocking collectives: 13.4 us -> 0 us
  between operations: 13.5 us -> 0.1 us
  local copies, waits for them, and re-layouts: 1.23 us -> 4.35 us
    all_gather x1 -> x0, waiting for transfers between devices: 118 us -> none  [on_device(): whole = lax.all_gather(data_spec, 'tmpl', axis=2, tiled=True)]
    ppermute x0 -> x17, starting transfers between devices: none -> 32 us  [the longest x15 25 us: from_offset(): return lax.ppermute(x, 'tmpl', pairs)]
    reduce_sum x3 -> x0, other arithmetic: 29.8 us -> none  [the longest x1 24.6 us: network_piece(): out_re = jnp.sum(weight[:, :, None] * shift_re, axis=1)]
    dot_general x2 -> x0, matrix products: 27.4 us -> none  [the longest x1 14 us: to_lags(): jnp.dot(spectra[0], jnp.cos(angle), precision=high)]
    pallas_call x0 -> x3, Pallas kernels: none -> 16.2 us  [the longest x1 11.4 us: template_part(): pl.pallas_call(template_kernel, out_shape=jax.ShapeDtypeStruct((CHANS, 2,...]
    psum x1 -> x0, blocking collectives: 13.4 us -> none  [on_device(): summed = lax.psum(network, 'chan')]
    ppermute x0 -> x17, waiting for transfers between devices: none -> 4.68 us  [the longest x15 2.74 us: from_offset(): return lax.ppermute(x, 'tmpl', pairs)]
    unnamed x7 -> x14, local copies, waits for them, and re-layouts: 0.43 us -> 4.33 us
  transfers between devices with their start and end apart: 1 -> 17, of which waited for: 1 -> 5; matrix products, arithmetic and copies ran while one was open for 2% -> 0% of each run, Pallas kernels for 0% -> 20%
where the time goes in v1:
time: 58.7 us; the launch traced here: 58 us
  starting transfers between devices  32 us (55%)
  Pallas kernels  16.2 us (28%)
  waiting for transfers between devices  4.68 us (8%)
  local copies, waits for them, and re-layouts  4.35 us (7%)
  other arithmetic  0.61 us (1%)
    ppermute x15, starting transfers between devices, from_offset(): return lax.ppermute(x, 'tmpl', pairs)  25 us
    pallas_call x1, Pallas kernels, template_part(): pl.pallas_call(template_kernel, out_shape=jax.ShapeDtypeStruct((CHANS, 2,...  11.4 us
    ppermute x1, starting transfers between devices, on_device(): got = lax.ppermute(send, 'chan', [(i, i ^ 1) for i in range(4)])  5.59 us
    pallas_call x1, Pallas kernels, network_part(): pl.pallas_call(network_kernel, out_shape=(shape, shape), in_specs=[VMEM]...  4.66 us
    unnamed x14, local copies, waits for them, and re-layouts  4.33 us
    ppermute x15, waiting for transfers between devices, from_offset(): return lax.ppermute(x, 'tmpl', pairs)  2.74 us
    ppermute x1, starting transfers between devices, on_device(): lax.ppermute(keep[1] + got[1], 'chan', [(i, i ^ 2) for i in range(4)])  1.45 us
  transfers between devices with their start and end apart: 17, of which 5 were waited for; matrix products, arithmetic and copies ran while one was open for 0% of the time, Pallas kernels for 20%

profile of v1, /device:TPU:1, one launch (start us, length us, event | category | flops | bytes accessed | tf_op | source)
XLA Modules:
  0.0 58.0 jit_solution(17602387704196591346)
XLA Ops:
  0.0 3.8 %collective-permute-start.3 = (f32[2,16,150]{2,1,0:T(8,128)}, f32[2,16,150]{2,1,0:T(8,128)S(1)}, u32[]{:S(2)}, u32[]{:S(2)}) collective-permute-start(f32[2,16,150]{2,1,0:T(8,128)} %bitcast.16), channel_id=1, source_target_pairs={{24,0},{28,4},{0,8},{4,12},{8,16},{12,20},{16,24},{20,28},{56,32},... | collective-permute-start | bytes 57608 | tf_op jit(solution)/shard_map/ppermute | solution.py:31
  3.8 3.0 %collective-permute-start.2 = (f32[2,16,150]{2,1,0:T(8,128)}, f32[2,16,150]{2,1,0:T(8,128)S(1)}, u32[]{:S(2)}, u32[]{:S(2)}) collective-permute-start(f32[2,16,150]{2,1,0:T(8,128)} %bitcast.17), channel_id=1, source_target_pairs={{8,0},{12,4},{16,8},{20,12},{24,16},{28,20},{0,24},{4,28},{40,32},... | collective-permute-start | bytes 57608 | tf_op jit(solution)/shard_map/ppermute | solution.py:31
  6.9 0.7 %collective-permute-start.1 = (f32[2,16,150]{2,1,0:T(8,128)}, f32[2,16,150]{2,1,0:T(8,128)S(1)}, u32[]{:S(2)}, u32[]{:S(2)}) collective-permute-start(f32[2,16,150]{2,1,0:T(8,128)} %bitcast.18), channel_id=1, source_target_pairs={{28,0},{0,4},{4,8},{8,12},{12,16},{16,20},{20,24},{24,28},{60,32},... | collective-permute-start | bytes 57608 | tf_op jit(solution)/shard_map/ppermute | solution.py:31
  7.6 1.9 %collective-permute-start = (f32[2,16,150]{2,1,0:T(8,128)}, f32[2,16,150]{2,1,0:T(8,128)S(1)}, u32[]{:S(2)}, u32[]{:S(2)}) collective-permute-start(f32[2,16,150]{2,1,0:T(8,128)} %bitcast.19), channel_id=1, source_target_pairs={{4,0},{8,4},{12,8},{16,12},{20,16},{24,20},{28,24},{0,28},{36,32},... | collective-permute-start | bytes 57608 | tf_op jit(solution)/shard_map/ppermute | solution.py:31
  9.5 0.0 collective-permute-done.3.refs_4_
  9.5 0.0 collective-permute-done.2.refs_3_
  9.6 2.4 %collective-permute-start.5 = (f32[2,16,150]{2,1,0:T(8,128)S(1)}, f32[2,16,150]{2,1,0:T(8,128)S(1)}, u32[]{:S(2)}, u32[]{:S(2)}) collective-permute-start(f32[2,16,150]{2,1,0:T(8,128)S(1)} %collective-permute-done.2.refs_3_), channel_id=1, source_target_pairs={{8,0},{12,4},{16,8},{20,12},{24,16},{28,20},{0,24},{4,28},{40,32},... | collective-permute-start | bytes 57608 | tf_op jit(solution)/shard_map/ppermute | solution.py:31
  11.9 0.8 %collective-permute-start.4 = (f32[2,16,150]{2,1,0:T(8,128)S(1)}, f32[2,16,150]{2,1,0:T(8,128)S(1)}, u32[]{:S(2)}, u32[]{:S(2)}) collective-permute-start(f32[2,16,150]{2,1,0:T(8,128)S(1)} %collective-permute-done.2.refs_3_), channel_id=1, source_target_pairs={{4,0},{8,4},{12,8},{16,12},{20,16},{24,20},{28,24},{0,28},{36,32},... | collective-permute-start | bytes 57608 | tf_op jit(solution)/shard_map/ppermute | solution.py:31
  12.7 0.0 collective-permute-done.1.refs_2_
  12.7 0.8 %collective-permute-done.6.refs_7_ = f32[2,16,150]{2,1,0:T(8,128)S(1)} collective-permute-done((f32[2,16,150]{2,1,0:T(8,128)S(1)}, f32[2,16,150]{2,1,0:T(8,128)S(1)}, u32[]{:S(2)}, u32[]{:S(2)}) %collective-permute-start.6) | collective-permute-done | bytes 19232 | tf_op jit(solution)/shard_map/ppermute | solution.py:31
  13.5 0.9 %collective-permute-done.5.refs_6_ = f32[2,16,150]{2,1,0:T(8,128)S(1)} collective-permute-done((f32[2,16,150]{2,1,0:T(8,128)S(1)}, f32[2,16,150]{2,1,0:T(8,128)S(1)}, u32[]{:S(2)}, u32[]{:S(2)}) %collective-permute-start.5) | collective-permute-done | bytes 19232 | tf_op jit(solution)/shard_map/ppermute | solution.py:31
  14.4 1.0 %collective-permute-done.4.refs_5_ = f32[2,16,150]{2,1,0:T(8,128)S(1)} collective-permute-done((f32[2,16,150]{2,1,0:T(8,128)S(1)}, f32[2,16,150]{2,1,0:T(8,128)S(1)}, u32[]{:S(2)}, u32[]{:S(2)}) %collective-permute-start.4) | collective-permute-done | bytes 19232 | tf_op jit(solution)/shard_map/ppermute | solution.py:31
  15.4 0.8 %copy-done.4 = f32[2,150,16]{1,2,0:T(8,128)S(1)} copy-done((f32[2,150,16]{1,2,0:T(8,128)S(1)}, f32[2,150,16]{1,2,0:T(8,128)}, u32[]{:S(2)}) %copy-start.4) | copy-done | bytes 19224
  16.2 0.2 shard_map.74.refs_1_
  16.3 1.4 %collective-permute-start.9 = (f32[2,152,128]{2,1,0:T(8,128)S(1)}, f32[2,152,128]{2,1,0:T(8,128)S(1)}, u32[]{:S(2)}, u32[]{:S(2)}) collective-permute-start(f32[2,152,128]{2,1,0:T(8,128)S(1)} %shard_map.74.refs_1_), channel_id=1, source_target_pairs={{96,0},{100,4},{104,8},{108,12},{112,16},{116,20},{120,24},{124,28... | collective-permute-start | bytes 466952 | tf_op jit(solution)/shard_map/ppermute | solution.py:31
  17.7 1.5 %collective-permute-start.8 = (f32[2,152,128]{2,1,0:T(8,128)S(1)}, f32[2,152,128]{2,1,0:T(8,128)S(1)}, u32[]{:S(2)}, u32[]{:S(2)}) collective-permute-start(f32[2,152,128]{2,1,0:T(8,128)S(1)} %shard_map.74.refs_1_), channel_id=1, source_target_pairs={{32,0},{36,4},{40,8},{44,12},{48,16},{52,20},{56,24},{60,28},{64,3... | collective-permute-start | bytes 466952 | tf_op jit(solution)/shard_map/ppermute | solution.py:31
  19.2 2.7 %collective-permute-start.7 = (f32[2,152,128]{2,1,0:T(8,128)S(1)}, f32[2,152,128]{2,1,0:T(8,128)S(1)}, u32[]{:S(2)}, u32[]{:S(2)}) collective-permute-start(f32[2,152,128]{2,1,0:T(8,128)S(1)} %shard_map.74.refs_1_), channel_id=1, source_target_pairs={{128,0},{132,4},{136,8},{140,12},{144,16},{148,20},{152,24},{156,2... | collective-permute-start | bytes 466952 | tf_op jit(solution)/shard_map/ppermute | solution.py:31
  22.0 0.1 collective-permute-start.14
  22.1 2.5 %collective-permute-start.11 = (f32[2,152,128]{2,1,0:T(8,128)S(1)}, f32[2,152,128]{2,1,0:T(8,128)S(1)}, u32[]{:S(2)}, u32[]{:S(2)}) collective-permute-start(f32[2,152,128]{2,1,0:T(8,128)S(1)} %collective-permute-done.9.refs_4_), channel_id=1, source_target_pairs={{128,0},{132,4},{136,8},{140,12},{144,16},{148,20},{152,24},{156,2... | collective-permute-start | bytes 466952 | tf_op jit(solution)/shard_map/ppermute | solution.py:31
  24.6 0.5 collective-permute-start.10
  25.1 2.5 %collective-permute-start.12 = (f32[2,152,128]{2,1,0:T(8,128)S(1)}, f32[2,152,128]{2,1,0:T(8,128)S(1)}, u32[]{:S(2)}, u32[]{:S(2)}) collective-permute-start(f32[2,152,128]{2,1,0:T(8,128)S(1)} %collective-permute-done.7.refs_2_), channel_id=1, source_target_pairs={{64,0},{68,4},{72,8},{76,12},{80,16},{84,20},{88,24},{92,28},{96,3... | collective-permute-start | bytes 466952 | tf_op jit(solution)/shard_map/ppermute | solution.py:31
  27.6 1.1 %collective-permute-start.13 = (f32[152,128]{1,0:T(8,128)S(1)}, f32[152,128]{1,0:T(8,128)S(1)}, u32[]{:S(2)}, u32[]{:S(2)}) collective-permute-start(f32[152,128]{1,0:T(8,128)S(1)} %slice_bitcast_fusion.1), channel_id=1, source_target_pairs={{32,0},{36,4},{40,8},{44,12},{48,16},{52,20},{56,24},{60,28},{64,3... | collective-permute-start | bytes 233480 | tf_op jit(solution)/shard_map/ppermute | solution.py:31
  28.7 0.7 %copy-done.5 = s32[4,150]{1,0:T(4,128)S(1)} copy-done((s32[4,150]{1,0:T(4,128)S(1)}, s32[4,150]{1,0:T(4,128)}, u32[]{:S(2)}) %copy-start.5) | copy-done | bytes 2424
  29.4 0.7 %copy-done.6 = s32[4,150]{1,0:T(4,128)S(1)} copy-done((s32[4,150]{1,0:T(4,128)S(1)}, s32[4,150]{1,0:T(4,128)}, u32[]{:S(2)}) %copy-start.6) | copy-done | bytes 2424
  30.1 11.4 %shard_map.73.refs_0_ = f32[150,2,4,8,128]{4,3,2,1,0:T(8,128)S(1)} custom-call(f32[2,150,4,8,128]{4,3,2,1,0:T(8,128)} %bitcast.21, s32[4,150]{1,0:T(4,128)S(1)} %copy-done.5, s32[4,150]{1,0:T(4,128)S(1)} %copy-done.6), custom_call_target="tpu_custom_call" | custom-call | tf_op jit(solution)/shard_map/pallas_call | solution.py:91
  41.5 2.2 %copy-done = f32[150,2,4,8,128]{4,3,2,1,0:T(8,128)} copy-done((f32[150,2,4,8,128]{4,3,2,1,0:T(8,128)}, f32[150,2,4,8,128]{4,3,2,1,0:T(8,128)S(1)}, u32[]{:S(2)}) %copy-start) | copy-done | bytes 4915224
  43.7 4.7 %shard_map.75 = (f32[2,4,768]{2,1,0:T(4,128)S(1)}, f32[2,4,768]{2,1,0:T(4,128)S(1)}) custom-call(f32[150,2,4,8,128]{4,3,2,1,0:T(8,128)} %copy-done, f32[2,152,128]{2,1,0:T(8,128)S(1)} %shard_map.74.refs_1_, f32[2,152,128]{2,1,0:T(8,128)S(1)} %collective-permute-done.7.refs_2_, f32[2,152,128]{2,1,0:T(8,128)S(1)} %collective-permute-done.8.refs_3_, ...), custom_call_target="tpu_custom_call" | custom-call | tf_op jit(solution)/shard_map/pallas_call | solution.py:242
  48.4 5.6 %collective-permute-start.15 = (f32[2,4,768]{2,1,0:T(4,128)S(1)}, f32[2,4,768]{2,1,0:T(4,128)S(1)}, u32[]{:S(2)}, u32[]{:S(2)}) collective-permute-start(f32[2,4,768]{2,1,0:T(4,128)S(1)} %get-tuple-element.8), channel_id=1, source_target_pairs={{0,1},{1,0},{2,3},{3,2},{4,5},{5,4},{6,7},{7,6},{8,9},{9,8},{10,11... | collective-permute-start | bytes 73736 | tf_op jit(solution)/shard_map/ppermute | solution.py:259
  54.0 0.8 %collective-permute-done.15 = f32[2,4,768]{2,1,0:T(4,128)S(1)} collective-permute-done((f32[2,4,768]{2,1,0:T(4,128)S(1)}, f32[2,4,768]{2,1,0:T(4,128)S(1)}, u32[]{:S(2)}, u32[]{:S(2)}) %collective-permute-start.15) | collective-permute-done | bytes 24608 | tf_op jit(solution)/shard_map/ppermute | solution.py:259
  54.8 1.5 %collective-permute-start.16 = (f32[4,768]{1,0:T(4,128)S(1)}, f32[4,768]{1,0:T(4,128)S(1)}, u32[]{:S(2)}, u32[]{:S(2)}) collective-permute-start(f32[4,768]{1,0:T(4,128)S(1)} %fusion), channel_id=1, source_target_pairs={{0,2},{1,3},{2,0},{3,1},{4,6},{5,7},{6,4},{7,5},{8,10},{9,11},{10,... | collective-permute-start | bytes 36872 | tf_op jit(solution)/shard_map/ppermute | solution.py:260
  56.3 1.1 %collective-permute-done.16 = f32[4,768]{1,0:T(4,128)S(1)} collective-permute-done((f32[4,768]{1,0:T(4,128)S(1)}, f32[4,768]{1,0:T(4,128)S(1)}, u32[]{:S(2)}, u32[]{:S(2)}) %collective-permute-start.16) | collective-permute-done | bytes 12320 | tf_op jit(solution)/shard_map/ppermute | solution.py:260
  57.4 0.6 %fusion.2 = f32[4,768]{1,0:T(4,128)} fusion(f32[4,768]{1,0:T(4,128)S(1)} %collective-permute-done.16, f32[2,4,768]{2,1,0:T(4,128)S(1)} %collective-permute-done.15, f32[2,4,768]{2,1,0:T(4,128)S(1)} %get-tuple-element.7), kind=kLoop, calls=%fused_computation.6 | loop fusion | flops 6144 | bytes 49152 | tf_op jit(solution)/shard_map/add | solution.py:261
  (23 shorter events, 0.1 us)
Async XLA Ops:
  0.0 9.5 %collective-permute-start.3 = (f32[2,16,150]{2,1,0:T(8,128)}, f32[2,16,150]{2,1,0:T(8,128)S(1)}, u32[]{:S(2)}, u32[]{:S(2)}) collective-permute-start(f32[2,16,150]{2,1,0:T(8,128)} %bitcast.16), channel_id=1, source_target_pairs={{24,0},{28,4},{0,8},{4,12},{8,16},{12,20},{16,24},{20,28},{56,32},... | collective-permute-start | bytes 57608 | tf_op jit(solution)/shard_map/ppermute | solution.py:31
  3.8 5.7 %collective-permute-start.2 = (f32[2,16,150]{2,1,0:T(8,128)}, f32[2,16,150]{2,1,0:T(8,128)S(1)}, u32[]{:S(2)}, u32[]{:S(2)}) collective-permute-start(f32[2,16,150]{2,1,0:T(8,128)} %bitcast.17), channel_id=1, source_target_pairs={{8,0},{12,4},{16,8},{20,12},{24,16},{28,20},{0,24},{4,28},{40,32},... | collective-permute-start | bytes 57608 | tf_op jit(solution)/shard_map/ppermute | solution.py:31
  6.9 5.9 %collective-permute-start.1 = (f32[2,16,150]{2,1,0:T(8,128)}, f32[2,16,150]{2,1,0:T(8,128)S(1)}, u32[]{:S(2)}, u32[]{:S(2)}) collective-permute-start(f32[2,16,150]{2,1,0:T(8,128)} %bitcast.18), channel_id=1, source_target_pairs={{28,0},{0,4},{4,8},{8,12},{12,16},{16,20},{20,24},{24,28},{60,32},... | collective-permute-start | bytes 57608 | tf_op jit(solution)/shard_map/ppermute | solution.py:31
  7.6 5.1 %collective-permute-start = (f32[2,16,150]{2,1,0:T(8,128)}, f32[2,16,150]{2,1,0:T(8,128)S(1)}, u32[]{:S(2)}, u32[]{:S(2)}) collective-permute-start(f32[2,16,150]{2,1,0:T(8,128)} %bitcast.19), channel_id=1, source_target_pairs={{4,0},{8,4},{12,8},{16,12},{20,16},{24,20},{28,24},{0,28},{36,32},... | collective-permute-start | bytes 57608 | tf_op jit(solution)/shard_map/ppermute | solution.py:31
  9.5 4.0 %collective-permute-start.6 = (f32[2,16,150]{2,1,0:T(8,128)S(1)}, f32[2,16,150]{2,1,0:T(8,128)S(1)}, u32[]{:S(2)}, u32[]{:S(2)}) collective-permute-start(f32[2,16,150]{2,1,0:T(8,128)S(1)} %collective-permute-done.3.refs_4_), channel_id=1, source_target_pairs={{28,0},{0,4},{4,8},{8,12},{12,16},{16,20},{20,24},{24,28},{60,32},... | collective-permute-start | bytes 57608 | tf_op jit(solution)/shard_map/ppermute | solution.py:31
  9.6 4.8 %collective-permute-start.5 = (f32[2,16,150]{2,1,0:T(8,128)S(1)}, f32[2,16,150]{2,1,0:T(8,128)S(1)}, u32[]{:S(2)}, u32[]{:S(2)}) collective-permute-start(f32[2,16,150]{2,1,0:T(8,128)S(1)} %collective-permute-done.2.refs_3_), channel_id=1, source_target_pairs={{8,0},{12,4},{16,8},{20,12},{24,16},{28,20},{0,24},{4,28},{40,32},... | collective-permute-start | bytes 57608 | tf_op jit(solution)/shard_map/ppermute | solution.py:31
  11.9 3.5 %collective-permute-start.4 = (f32[2,16,150]{2,1,0:T(8,128)S(1)}, f32[2,16,150]{2,1,0:T(8,128)S(1)}, u32[]{:S(2)}, u32[]{:S(2)}) collective-permute-start(f32[2,16,150]{2,1,0:T(8,128)S(1)} %collective-permute-done.2.refs_3_), channel_id=1, source_target_pairs={{4,0},{8,4},{12,8},{16,12},{20,16},{24,20},{28,24},{0,28},{36,32},... | collective-permute-start | bytes 57608 | tf_op jit(solution)/shard_map/ppermute | solution.py:31
  15.4 0.8 %copy-start.4 = (f32[2,150,16]{1,2,0:T(8,128)S(1)}, f32[2,150,16]{1,2,0:T(8,128)}, u32[]{:S(2)}) copy-start(f32[2,150,16]{1,2,0:T(8,128)} %param.7) | copy-start | bytes 57604
  16.3 5.7 %collective-permute-start.9 = (f32[2,152,128]{2,1,0:T(8,128)S(1)}, f32[2,152,128]{2,1,0:T(8,128)S(1)}, u32[]{:S(2)}, u32[]{:S(2)}) collective-permute-start(f32[2,152,128]{2,1,0:T(8,128)S(1)} %shard_map.74.refs_1_), channel_id=1, source_target_pairs={{96,0},{100,4},{104,8},{108,12},{112,16},{116,20},{120,24},{124,28... | collective-permute-start | bytes 466952 | tf_op jit(solution)/shard_map/ppermute | solution.py:31
  17.7 6.9 %collective-permute-start.8 = (f32[2,152,128]{2,1,0:T(8,128)S(1)}, f32[2,152,128]{2,1,0:T(8,128)S(1)}, u32[]{:S(2)}, u32[]{:S(2)}) collective-permute-start(f32[2,152,128]{2,1,0:T(8,128)S(1)} %shard_map.74.refs_1_), channel_id=1, source_target_pairs={{32,0},{36,4},{40,8},{44,12},{48,16},{52,20},{56,24},{60,28},{64,3... | collective-permute-start | bytes 466952 | tf_op jit(solution)/shard_map/ppermute | solution.py:31
  19.2 5.9 %collective-permute-start.7 = (f32[2,152,128]{2,1,0:T(8,128)S(1)}, f32[2,152,128]{2,1,0:T(8,128)S(1)}, u32[]{:S(2)}, u32[]{:S(2)}) collective-permute-start(f32[2,152,128]{2,1,0:T(8,128)S(1)} %shard_map.74.refs_1_), channel_id=1, source_target_pairs={{128,0},{132,4},{136,8},{140,12},{144,16},{148,20},{152,24},{156,2... | collective-permute-start | bytes 466952 | tf_op jit(solution)/shard_map/ppermute | solution.py:31
  22.0 21.7 %collective-permute-start.14 = (f32[152,128]{1,0:T(8,128)S(1)}, f32[152,128]{1,0:T(8,128)S(1)}, u32[]{:S(2)}, u32[]{:S(2)}) collective-permute-start(f32[152,128]{1,0:T(8,128)S(1)} %slice_bitcast_fusion), channel_id=1, source_target_pairs={{96,0},{100,4},{104,8},{108,12},{112,16},{116,20},{120,24},{124,28... | collective-permute-start | bytes 233480 | tf_op jit(solution)/shard_map/ppermute | solution.py:31
  22.1 21.6 %collective-permute-start.11 = (f32[2,152,128]{2,1,0:T(8,128)S(1)}, f32[2,152,128]{2,1,0:T(8,128)S(1)}, u32[]{:S(2)}, u32[]{:S(2)}) collective-permute-start(f32[2,152,128]{2,1,0:T(8,128)S(1)} %collective-permute-done.9.refs_4_), channel_id=1, source_target_pairs={{128,0},{132,4},{136,8},{140,12},{144,16},{148,20},{152,24},{156,2... | collective-permute-start | bytes 466952 | tf_op jit(solution)/shard_map/ppermute | solution.py:31
  24.6 19.1 %collective-permute-start.10 = (f32[2,152,128]{2,1,0:T(8,128)S(1)}, f32[2,152,128]{2,1,0:T(8,128)S(1)}, u32[]{:S(2)}, u32[]{:S(2)}) collective-permute-start(f32[2,152,128]{2,1,0:T(8,128)S(1)} %collective-permute-done.8.refs_3_), channel_id=1, source_target_pairs={{128,0},{132,4},{136,8},{140,12},{144,16},{148,20},{152,24},{156,2... | collective-permute-start | bytes 466952 | tf_op jit(solution)/shard_map/ppermute | solution.py:31
  25.1 18.5 %collective-permute-start.12 = (f32[2,152,128]{2,1,0:T(8,128)S(1)}, f32[2,152,128]{2,1,0:T(8,128)S(1)}, u32[]{:S(2)}, u32[]{:S(2)}) collective-permute-start(f32[2,152,128]{2,1,0:T(8,128)S(1)} %collective-permute-done.7.refs_2_), channel_id=1, source_target_pairs={{64,0},{68,4},{72,8},{76,12},{80,16},{84,20},{88,24},{92,28},{96,3... | collective-permute-start | bytes 466952 | tf_op jit(solution)/shard_map/ppermute | solution.py:31
  27.6 16.1 %collective-permute-start.13 = (f32[152,128]{1,0:T(8,128)S(1)}, f32[152,128]{1,0:T(8,128)S(1)}, u32[]{:S(2)}, u32[]{:S(2)}) collective-permute-start(f32[152,128]{1,0:T(8,128)S(1)} %slice_bitcast_fusion.1), channel_id=1, source_target_pairs={{32,0},{36,4},{40,8},{44,12},{48,16},{52,20},{56,24},{60,28},{64,3... | collective-permute-start | bytes 233480 | tf_op jit(solution)/shard_map/ppermute | solution.py:31
  28.7 0.7 %copy-start.5 = (s32[4,150]{1,0:T(4,128)S(1)}, s32[4,150]{1,0:T(4,128)}, u32[]{:S(2)}) copy-start(s32[4,150]{1,0:T(4,128)} %shift_ref.1) | copy-start | bytes 7204
  29.4 0.7 %copy-start.6 = (s32[4,150]{1,0:T(4,128)S(1)}, s32[4,150]{1,0:T(4,128)}, u32[]{:S(2)}) copy-start(s32[4,150]{1,0:T(4,128)} %mask_ref.1) | copy-start | bytes 7204
  30.1 13.6 %copy-start.1 = (f32[2,128,128]{2,1,0:T(8,128)S(1)}, f32[2,128,128]{2,1,0:T(8,128)}, u32[]{:S(2)}) copy-start(f32[2,128,128]{2,1,0:T(8,128)} %constant.7.clone.refs_11_) | copy-start | bytes 393220
  30.1 13.6 %copy-start.2 = (f32[256,64]{1,0:T(8,128)S(1)}, f32[256,64]{1,0:T(8,128)}, u32[]{:S(2)}) copy-start(f32[256,64]{1,0:T(8,128)} %constant.6.clone.refs_10_) | copy-start | bytes 196612
  30.1 13.7 %copy-start.3 = (f32[2,96,128]{2,1,0:T(8,128)S(1)}, f32[2,96,128]{2,1,0:T(8,128)}, u32[]{:S(2)}) copy-start(f32[2,96,128]{2,1,0:T(8,128)} %constant.8.clone.refs_12_) | copy-start | bytes 294916
  41.5 2.2 %copy-start = (f32[150,2,4,8,128]{4,3,2,1,0:T(8,128)}, f32[150,2,4,8,128]{4,3,2,1,0:T(8,128)S(1)}, u32[]{:S(2)}) copy-start(f32[150,2,4,8,128]{4,3,2,1,0:T(8,128)S(1)} %shard_map.73.refs_0_) | copy-start | bytes 14745604
  48.4 6.4 %collective-permute-start.15 = (f32[2,4,768]{2,1,0:T(4,128)S(1)}, f32[2,4,768]{2,1,0:T(4,128)S(1)}, u32[]{:S(2)}, u32[]{:S(2)}) collective-permute-start(f32[2,4,768]{2,1,0:T(4,128)S(1)} %get-tuple-element.8), channel_id=1, source_target_pairs={{0,1},{1,0},{2,3},{3,2},{4,5},{5,4},{6,7},{7,6},{8,9},{9,8},{10,11... | collective-permute-start | bytes 73736 | tf_op jit(solution)/shard_map/ppermute | solution.py:259
  54.8 2.5 %collective-permute-start.16 = (f32[4,768]{1,0:T(4,128)S(1)}, f32[4,768]{1,0:T(4,128)S(1)}, u32[]{:S(2)}, u32[]{:S(2)}) collective-permute-start(f32[4,768]{1,0:T(4,128)S(1)} %fusion), channel_id=1, source_target_pairs={{0,2},{1,3},{2,0},{3,1},{4,6},{5,7},{6,4},{7,5},{8,10},{9,11},{10,... | collective-permute-start | bytes 36872 | tf_op jit(solution)/shard_map/ppermute | solution.py:260

commit v2 on v1

v2 whole, which is shorter than its diff:
```python
import functools
import math

import jax
import jax.numpy as jnp
import numpy as np
from jax import lax
from jax.experimental import pallas as pl
from jax.experimental.pallas import tpu as pltpu
from jax.sharding import PartitionSpec as P

FREQS = 1024
FIRST = 128
NFFT = 4096
LAGS = 3072
CHANS = 150
ROWS = 152
TMPL = 4
XH, YS, ZS = 2, 4, 8

VMEM = pl.BlockSpec(memory_space=pltpu.VMEM)
HIGH = lax.Precision.HIGHEST
PARAMS = pltpu.CompilerParams(vmem_limit_bytes=16 << 20)
LARGE = pltpu.CompilerParams(vmem_limit_bytes=40 << 20)


def from_offset(x, dx=0, dy=0, dz=0):
    pairs = []
    for i in range(XH * YS * ZS):
        a, b, c = i // (YS * ZS), i // ZS % YS, i % ZS
        src = (a + dx) % XH * (YS * ZS) + (b + dy) % YS * ZS + (c + dz) % ZS
        pairs.append((src, i))
    return lax.ppermute(x, "tmpl", pairs)


def half_turn_fit():
    x = np.cos(np.pi * (np.arange(400) + 0.5) / 400) * 0.25 + 0.25
    r = np.sqrt(x)
    even = np.polynomial.Chebyshev.fit(x, np.cos(np.pi * r), 5, domain=[0, 0.5])
    odd = np.polynomial.Chebyshev.fit(x, np.sin(np.pi * r) / r, 5, domain=[0, 0.5])
    return [[float(v) for v in p.convert(kind=np.polynomial.Polynomial).coef] for p in (even, odd)]


COS_FIT, SIN_FIT = half_turn_fit()


def sincos(turns):
    near = jnp.floor(turns + 0.5)
    r = turns - near
    half = near * 0.5
    sign = 1.0 - 4.0 * (half - jnp.floor(half))
    sq = r * r
    c, s = COS_FIT[-1], SIN_FIT[-1]
    for a, b in zip(COS_FIT[-2::-1], SIN_FIT[-2::-1]):
        c, s = c * sq + a, s * sq + b
    return sign, c, s * r


STEP = 30
STEPS = CHANS // STEP


def template_kernel(spec_ref, code_ref, after_hbm, out_ref, pair_ref, wide_ref, weight_ref):
    row = lax.broadcasted_iota(jnp.int32, (8, 128), 0)
    lane = lax.broadcasted_iota(jnp.int32, (8, 128), 1)
    first_bin = (FIRST * (row // 4 + 1) + lane).astype(jnp.float32) * (2.0 / NFFT)

    base = pl.program_id(0) * STEP

    @pl.when(pl.program_id(0) == 0)
    def _():
        pair_ref[0:4, 0:CHANS] = code_ref[...]
        pair_ref[4:8, 0:CHANS] = code_ref[...]
        for start in (0, 128):
            codes = pair_ref[:, start : start + 128]
            sign, wr, wi = sincos(codes * (2.0 * 2 * FIRST / NFFT))
            wr, wi = wr * sign, wi * sign
            for at in range(min(128, CHANS - start)):
                for k, part in enumerate((codes, wr, wi)):
                    wide_ref[start + at, k] = jnp.broadcast_to(part[:, at : at + 1], (8, 128))

    def weigh(c):
        power = None
        for m in range(4):
            re, im = spec_ref[0, c, m], spec_ref[1, c, m]
            one = re * re + im * im
            power = one if power is None else power + one
        power = jnp.broadcast_to(jnp.sum(power, axis=1, keepdims=True), (8, 128))
        power = power + pltpu.roll(power, 4, 0)
        weight = lax.rsqrt(power * (1.0 / FREQS) + 1e-06)
        weight_ref[c] = jnp.where(wide_ref[base + c, 0] >= NFFT, weight, 0.0)

    def phase(c):
        sign, er, ei = sincos(first_bin * wide_ref[base + c, 0])
        wr, wi = wide_ref[base + c, 1], wide_ref[base + c, 2]
        weight = weight_ref[c] * sign
        er, ei = er * weight, ei * weight
        for m in range(4):
            re, im = spec_ref[0, c, m], spec_ref[1, c, m]
            out_ref[c, 0, m] = re * er + im * ei
            out_ref[c, 1, m] = re * ei - im * er
            if m < 3:
                er, ei = er * wr - ei * wi, er * wi + ei * wr

    for body, unroll in ((weigh, 10), (phase, 5)):

        def step(j, carry, body=body, unroll=unroll):
            for k in range(unroll):
                body(j * unroll + k)
            return carry

        lax.fori_loop(0, STEP // unroll, step, 0)


def template_view(tmpl_spec):
    view = tmpl_spec.reshape(2, TMPL, CHANS, 4, 2, 128).transpose(0, 2, 3, 4, 1, 5)
    return view.reshape(2, CHANS, 4, 8, 128)


def template_part(tmpl_spec, code, after):
    return pl.pallas_call(
        template_kernel,
        grid=(STEPS,),
        out_shape=jax.ShapeDtypeStruct((CHANS, 2, 4, 8, 128), jnp.float32),
        in_specs=[
            pl.BlockSpec((2, STEP, 4, 8, 128), lambda i: (0, i, 0, 0, 0)),
            VMEM,
            pl.BlockSpec(memory_space=pl.ANY),
        ],
        out_specs=pl.BlockSpec((STEP, 2, 4, 8, 128), lambda i: (i, 0, 0, 0, 0)),
        scratch_shapes=[
            pltpu.VMEM((8, 256), jnp.float32),
            pltpu.VMEM((CHANS, 3, 8, 128), jnp.float32),
            pltpu.VMEM((STEP, 8, 128), jnp.float32),
        ],
        compiler_params=LARGE,
    )(template_view(tmpl_spec), code, after)


REST = CHANS - 128
DENSE = 80


def dense_kernel(own_ref, other_ref, out_ref):
    out_ref[64:DENSE, :] = jnp.zeros((DENSE - 64, 128), jnp.float32)
    for j in range(4):
        ref = (own_ref, other_ref)[j // 2]
        out_ref[16 * j : 16 * j + 16, :] = ref[j % 2, :, 0:128]
        out_ref[64:DENSE, 32 * j : 32 * j + REST] = ref[j % 2, :, 128:CHANS]


Z_ORDER = (0, 1, -1, 2, -2, 3, 4, -3)


def pack_kernel(*refs):
    parts, out_ref, held = refs[:8], refs[8], refs[9]
    z = lax.axis_index("tmpl") % ZS
    for part, dz in zip(parts, Z_ORDER):
        at = pl.multiple_of(lax.rem(z + dz + ZS, ZS) * 16, 16)
        for j in range(5):
            held[j, pl.ds(at, 16), :] = part[16 * j : 16 * j + 16, :]
    rest = held[4].T
    for j in range(4):
        out_ref[j // 2, j % 2, 0:128, :] = held[j].T
        out_ref[j // 2, j % 2, 128:ROWS, :] = rest[32 * j : 32 * j + ROWS - 128]


def gather_xz(data_spec):
    raw = data_spec.transpose(0, 2, 1)
    own = pl.pallas_call(
        dense_kernel,
        out_shape=jax.ShapeDtypeStruct((DENSE, 128), jnp.float32),
        in_specs=[VMEM] * 2,
        out_specs=VMEM,
        compiler_params=PARAMS,
    )(raw, from_offset(raw, dx=1))
    up = from_offset(own, dz=1)
    down = from_offset(own, dz=-1)
    up2 = from_offset(own, dz=2)
    down2 = from_offset(own, dz=-2)
    up3 = from_offset(up2, dz=1)
    up4 = from_offset(up2, dz=2)
    down3 = from_offset(down2, dz=-1)
    return pl.pallas_call(
        pack_kernel,
        out_shape=jax.ShapeDtypeStruct((2, 2, ROWS, 128), jnp.float32),
        in_specs=[VMEM] * 8,
        out_specs=VMEM,
        scratch_shapes=[pltpu.VMEM((5, 128, 128), jnp.float32)],
        compiler_params=PARAMS,
    )(own, up, down, up2, down2, up3, up4, down3)


Y_ORDER = (0, 1, -1, 2)


def gather_y(own):
    return (own,) + tuple(from_offset(own, dy=dy) for dy in Y_ORDER[1:])


def tables():
    kl = np.arange(32)
    fh = np.arange(8)
    a = 2 * np.pi * (np.outer(kl, fh + 1) % 32) / 32
    first = np.zeros((2, TMPL, 32, 2, 4, 2, TMPL))
    for t in range(TMPL):
        c, s = np.cos(a).reshape(32, 4, 2), np.sin(a).reshape(32, 4, 2)
        first[0, t, :, 0, :, :, t] = c
        first[0, t, :, 1, :, :, t] = -s
        first[1, t, :, 0, :, :, t] = s
        first[1, t, :, 1, :, :, t] = c
    fl = np.arange(128)
    b = np.tile(2 * np.pi * np.outer(kl, fl) / NFFT, (TMPL, 1))
    kh = (4 * np.arange(24)[None, :] + np.arange(4)[:, None]).reshape(96)
    g = 2 * np.pi * (np.outer(kh, fl) % 128) / 128
    rows = [first.reshape(256, 64)]
    twist = np.stack([np.cos(b), np.sin(b)])
    last = np.stack([np.cos(g), -np.sin(g)]) / FREQS
    return tuple(np.asarray(v, np.float32) for v in (rows[0], twist, last))


def network_kernel(*refs):
    spec_ref, blocks = refs[0], refs[1:5]
    first_ref, twist_ref, last_ref, keep_ref, send_ref, data_ref, piece_ref, acc_ref = refs[5:]
    pl.when(pl.program_id(0) == 0)(functools.partial(scale_data, blocks, data_ref, acc_ref))
    base = pl.program_id(0) * STEP
    lower = lax.broadcasted_iota(jnp.int32, (8, 128), 0) < 4

    def channel(c, acc):
        acc = list(acc)
        for m in range(4):
            d = []
            for k in range(2):
                one = jnp.broadcast_to(data_ref[2 * m, k, pl.ds(base + c, 1), :], (8, 128))
                two = jnp.broadcast_to(data_ref[2 * m + 1, k, pl.ds(base + c, 1), :], (8, 128))
                d.append(jnp.where(lower, one, two))
            tr, ti = spec_ref[c, 0, m], spec_ref[c, 1, m]
            acc[m] = acc[m] + (tr * d[0] - ti * d[1])
            acc[4 + m] = acc[4 + m] + (tr * d[1] + ti * d[0])
        return tuple(acc)

    acc = lax.fori_loop(0, STEP, channel, tuple(acc_ref[i] for i in range(8)), unroll=5)
    for i in range(8):
        acc_ref[i] = acc[i]

    @pl.when(pl.program_id(0) == STEPS - 1)
    def _():
        to_lags(acc, first_ref, twist_ref, last_ref, piece_ref)
        keep_ref[0] = piece_ref[0]
        keep_ref[1] = piece_ref[2]
        send_ref[0] = piece_ref[1]
        send_ref[1] = piece_ref[3]


def scale_data(blocks, data_ref, acc_ref):
    acc_ref[...] = jnp.zeros_like(acc_ref)
    me = lax.axis_index("tmpl")
    x, y = me // (YS * ZS), me // ZS % YS

    power = None
    for block in blocks:
        for dx in range(XH):
            re, im = block[dx, 0], block[dx, 1]
            one = re * re + im * im
            power = one if power is None else power + one
    power = jnp.sum(power, axis=1, keepdims=True)
    scale = jnp.broadcast_to(lax.rsqrt(power * (1.0 / FREQS) + 1e-06), (ROWS, 128))
    for block, dy in zip(blocks, Y_ORDER):
        for dx in range(XH):
            group = lax.rem(x + dx, XH) * YS + lax.rem(y + dy + YS, YS)
            for k in range(2):
                data_ref[group, k] = block[dx, k] * scale


def to_lags(acc, first_ref, twist_ref, last_ref, piece_ref):
    spectra = jnp.concatenate(acc, axis=0)
    mixed = jnp.dot(first_ref[...], spectra, precision=HIGH, preferred_element_type=jnp.float32)
    yr, yi = mixed[0:128], mixed[128:256]
    tc, ts = twist_ref[0], twist_ref[1]
    zr, zi = yr * tc - yi * ts, yr * ts + yi * tc
    dims = (((1,), (1,)), ((), ()))
    lags = lax.dot_general(last_ref[0], zr, dims, precision=HIGH, preferred_element_type=jnp.float32)
    lags = lags + lax.dot_general(last_ref[1], zi, dims, precision=HIGH, preferred_element_type=jnp.float32)
    lane = lax.broadcasted_iota(jnp.int32, (24, 128), 1) // 32
    chan = lax.axis_index("chan")
    for t in range(TMPL):
        out = None
        for r in range(4):
            part = lags[24 * r : 24 * r + 24]
            if (r - t) % 4:
                part = pltpu.roll(part, (r - t) % 4 * 32, 1)
            out = part if out is None else jnp.where(lane == r, part, out)
        for j in range(4):
            for g in range(6):
                piece_ref[j ^ chan, t : t + 1, g * 128 : (g + 1) * 128] = out[6 * j + g : 6 * j + g + 1]


def network_part(spectra, blocks):
    lag_dev = LAGS // 4
    shape = jax.ShapeDtypeStruct((2, TMPL, lag_dev), jnp.float32)
    return pl.pallas_call(
        network_kernel,
        grid=(STEPS,),
        out_shape=(shape, shape),
        in_specs=[pl.BlockSpec((STEP, 2, 4, 8, 128), lambda i: (i, 0, 0, 0, 0))] + [VMEM] * 7,
        out_specs=(VMEM, VMEM),
        scratch_shapes=[
            pltpu.VMEM((8, 2, ROWS, 128), jnp.float32),
            pltpu.VMEM((4, TMPL, lag_dev), jnp.float32),
            pltpu.VMEM((8, 8, 128), jnp.float32),
        ],
        compiler_params=PARAMS,
    )(spectra, *blocks, *tables())


def on_device(data_spec, tmpl_spec, shifts, mask):
    own = gather_xz(data_spec)
    blocks = gather_y(own)
    code = (shifts + NFFT * mask).astype(jnp.float32)
    spectra = template_part(tmpl_spec, code, own)
    keep, send = network_part(spectra, blocks)
    got = lax.ppermute(send, "chan", [(i, i ^ 1) for i in range(4)])
    other = lax.ppermute(keep[1] + got[1], "chan", [(i, i ^ 2) for i in range(4)])
    return keep[0] + got[0] + other


def solution(mesh):
    return jax.shard_map(
        on_device,
        mesh=mesh,
        in_specs=(
            P(None, "chan", "tmpl"),
            P(None, "tmpl", "chan", None),
            P("tmpl", "chan"),
            P("tmpl", "chan"),
        ),
        out_specs=P("tmpl", "chan"),
        check_vma=False,
    )
```

time: 58.7 us -> 46.8 us (0.80)
  Pallas kernels: 16.2 us -> 7.46 us
  starting transfers between devices: 32 us -> 27.2 us
  waiting for transfers between devices: 4.68 us -> 7.17 us
  local copies, waits for them, and re-layouts: 4.35 us -> 3.16 us
  other arithmetic: 0.61 us -> 1.32 us
    pallas_call x3 -> x4, Pallas kernels: 16.2 us -> 7.46 us  [the longest x1 4.76 us: template_part(): pl.pallas_call(template_kernel, grid=(STEPS,), out_shape=jax.ShapeDtypeSt...]
    ppermute x15 -> x11, starting transfers between devices: 25 us -> 21.4 us  [from_offset(): return lax.ppermute(x, 'tmpl', pairs)]
    ppermute x15 -> x11, waiting for transfers between devices: 2.74 us -> 4.99 us  [from_offset(): return lax.ppermute(x, 'tmpl', pairs)]
    unnamed x14 -> x10, local copies, waits for them, and re-layouts: 4.33 us -> 3.16 us
    ppermute x1, starting transfers between devices: 5.59 us -> 4.62 us  [on_device(): got = lax.ppermute(send, 'chan', [(i, i ^ 1) for i in range(4)])]
    convert_element_type x0 -> x1, other arithmetic: none -> 0.71 us  [on_device(): code = (shifts + NFFT * mask).astype(jnp.float32)]
  transfers between devices with their start and end apart: 17 -> 13, of which waited for: 5 -> 7; matrix products, arithmetic and copies ran while one was open for 0% -> 2% of each run, Pallas kernels for 20% -> 10%
where the time goes in v2:
time: 46.8 us; the launch traced here: 46.4 us
  starting transfers between devices  27.2 us (58%)
  Pallas kernels  7.46 us (16%)
  waiting for transfers between devices  7.17 us (15%)
  local copies, waits for them, and re-layouts  3.16 us (7%)
  other arithmetic  1.32 us (3%)
    ppermute x11, starting transfers between devices, from_offset(): return lax.ppermute(x, 'tmpl', pairs)  21.4 us
    ppermute x11, waiting for transfers between devices, from_offset(): return lax.ppermute(x, 'tmpl', pairs)  4.99 us
    pallas_call x1, Pallas kernels, template_part(): pl.pallas_call(template_kernel, grid=(STEPS,), out_shape=jax.ShapeDtypeSt...  4.76 us
    ppermute x1, starting transfers between devices, on_device(): got = lax.ppermute(send, 'chan', [(i, i ^ 1) for i in range(4)])  4.62 us
    unnamed x10, local copies, waits for them, and re-layouts  3.16 us
    pallas_call x1, Pallas kernels, network_part(): pl.pallas_call(network_kernel, grid=(STEPS,), out_shape=(shape, shape), i...  2.44 us
    ppermute x1, waiting for transfers between devices, on_device(): lax.ppermute(keep[1] + got[1], 'chan', [(i, i ^ 2) for i in range(4)])  1.34 us
    ppermute x1, starting transfers between devices, on_device(): lax.ppermute(keep[1] + got[1], 'chan', [(i, i ^ 2) for i in range(4)])  1.21 us
  transfers between devices with their start and end apart: 13, of which 7 were waited for; matrix products, arithmetic and copies ran while one was open for 2% of the time, Pallas kernels for 10%

profile of v2, /device:TPU:1, one launch (start us, length us, event | category | flops | bytes accessed | tf_op | source)
XLA Modules:
  0.0 46.4 jit_solution(16387847611395939182)
XLA Ops:
  0.0 3.6 %collective-permute-start = (f32[2,16,150]{2,1,0:T(8,128)}, f32[2,16,150]{2,1,0:T(8,128)S(1)}, u32[]{:S(2)}, u32[]{:S(2)}) collective-permute-start(f32[2,16,150]{2,1,0:T(8,128)} %bitcast.13), channel_id=1, source_target_pairs={{128,0},{132,4},{136,8},{140,12},{144,16},{148,20},{152,24},{156,2... | collective-permute-start | bytes 57608 | tf_op jit(solution)/shard_map/ppermute | solution.py:33
  3.6 1.5 %collective-permute-done.other_ref = f32[2,16,150]{2,1,0:T(8,128)S(1)} collective-permute-done((f32[2,16,150]{2,1,0:T(8,128)}, f32[2,16,150]{2,1,0:T(8,128)S(1)}, u32[]{:S(2)}, u32[]{:S(2)}) %collective-permute-start) | collective-permute-done | bytes 19232 | tf_op jit(solution)/shard_map/ppermute | solution.py:33
  5.1 0.8 %copy-done.4 = f32[2,150,16]{1,2,0:T(8,128)S(1)} copy-done((f32[2,150,16]{1,2,0:T(8,128)S(1)}, f32[2,150,16]{1,2,0:T(8,128)}, u32[]{:S(2)}) %copy-start.4) | copy-done | bytes 19224
  5.8 0.1 shard_map.73.refs_0_
  5.9 3.2 %collective-permute-start.4 = (f32[80,128]{1,0:T(8,128)S(1)}, f32[80,128]{1,0:T(8,128)S(1)}, u32[]{:S(2)}, u32[]{:S(2)}) collective-permute-start(f32[80,128]{1,0:T(8,128)S(1)} %shard_map.73.refs_0_), channel_id=1, source_target_pairs={{24,0},{28,4},{0,8},{4,12},{8,16},{12,20},{16,24},{20,28},{56,32},... | collective-permute-start | bytes 122888 | tf_op jit(solution)/shard_map/ppermute | solution.py:33
  9.2 3.1 %collective-permute-start.3 = (f32[80,128]{1,0:T(8,128)S(1)}, f32[80,128]{1,0:T(8,128)S(1)}, u32[]{:S(2)}, u32[]{:S(2)}) collective-permute-start(f32[80,128]{1,0:T(8,128)S(1)} %shard_map.73.refs_0_), channel_id=1, source_target_pairs={{8,0},{12,4},{16,8},{20,12},{24,16},{28,20},{0,24},{4,28},{40,32},... | collective-permute-start | bytes 122888 | tf_op jit(solution)/shard_map/ppermute | solution.py:33
  12.3 0.7 %collective-permute-start.2 = (f32[80,128]{1,0:T(8,128)S(1)}, f32[80,128]{1,0:T(8,128)S(1)}, u32[]{:S(2)}, u32[]{:S(2)}) collective-permute-start(f32[80,128]{1,0:T(8,128)S(1)} %shard_map.73.refs_0_), channel_id=1, source_target_pairs={{28,0},{0,4},{4,8},{8,12},{12,16},{16,20},{20,24},{24,28},{60,32},... | collective-permute-start | bytes 122888 | tf_op jit(solution)/shard_map/ppermute | solution.py:33
  13.0 1.9 %collective-permute-start.1 = (f32[80,128]{1,0:T(8,128)S(1)}, f32[80,128]{1,0:T(8,128)S(1)}, u32[]{:S(2)}, u32[]{:S(2)}) collective-permute-start(f32[80,128]{1,0:T(8,128)S(1)} %shard_map.73.refs_0_), channel_id=1, source_target_pairs={{4,0},{8,4},{12,8},{16,12},{20,16},{24,20},{28,24},{0,28},{36,32},... | collective-permute-start | bytes 122888 | tf_op jit(solution)/shard_map/ppermute | solution.py:33
  15.0 0.0 collective-permute-start.7
  15.0 0.0 collective-permute-done.3.refs_3_
  15.0 2.3 %collective-permute-start.6 = (f32[80,128]{1,0:T(8,128)S(1)}, f32[80,128]{1,0:T(8,128)S(1)}, u32[]{:S(2)}, u32[]{:S(2)}) collective-permute-start(f32[80,128]{1,0:T(8,128)S(1)} %collective-permute-done.3.refs_3_), channel_id=1, source_target_pairs={{8,0},{12,4},{16,8},{20,12},{24,16},{28,20},{0,24},{4,28},{40,32},... | collective-permute-start | bytes 122888 | tf_op jit(solution)/shard_map/ppermute | solution.py:33
  17.2 0.8 %collective-permute-start.5 = (f32[80,128]{1,0:T(8,128)S(1)}, f32[80,128]{1,0:T(8,128)S(1)}, u32[]{:S(2)}, u32[]{:S(2)}) collective-permute-start(f32[80,128]{1,0:T(8,128)S(1)} %collective-permute-done.3.refs_3_), channel_id=1, source_target_pairs={{4,0},{8,4},{12,8},{16,12},{20,16},{24,20},{28,24},{0,28},{36,32},... | collective-permute-start | bytes 122888 | tf_op jit(solution)/shard_map/ppermute | solution.py:33
  18.0 0.0 collective-permute-done.2.refs_2_
  18.0 0.0 collective-permute-done.1.refs_1_
  18.1 1.5 %collective-permute-done.7.refs_7_ = f32[80,128]{1,0:T(8,128)S(1)} collective-permute-done((f32[80,128]{1,0:T(8,128)S(1)}, f32[80,128]{1,0:T(8,128)S(1)}, u32[]{:S(2)}, u32[]{:S(2)}) %collective-permute-start.7) | collective-permute-done | bytes 40992 | tf_op jit(solution)/shard_map/ppermute | solution.py:33
  19.5 0.2 collective-permute-done.6.refs_6_
  19.7 0.9 %collective-permute-done.5.refs_5_ = f32[80,128]{1,0:T(8,128)S(1)} collective-permute-done((f32[80,128]{1,0:T(8,128)S(1)}, f32[80,128]{1,0:T(8,128)S(1)}, u32[]{:S(2)}, u32[]{:S(2)}) %collective-permute-start.5) | collective-permute-done | bytes 40992 | tf_op jit(solution)/shard_map/ppermute | solution.py:33
  20.6 0.2 shard_map.74.after_hbm.refs_1_
  20.8 3.0 %collective-permute-start.10 = (f32[2,2,152,128]{3,2,1,0:T(8,128)S(1)}, f32[2,2,152,128]{3,2,1,0:T(8,128)S(1)}, u32[]{:S(2)}, u32[]{:S(2)}) collective-permute-start(f32[2,2,152,128]{3,2,1,0:T(8,128)S(1)} %shard_map.74.after_hbm.refs_1_), channel_id=1, source_target_pairs={{64,0},{68,4},{72,8},{76,12},{80,16},{84,20},{88,24},{92,28},{96,3... | collective-permute-start | bytes 933896 | tf_op jit(solution)/shard_map/ppermute | solution.py:33
  23.8 0.4 collective-permute-start.9
  24.2 2.3 %collective-permute-start.8 = (f32[2,2,152,128]{3,2,1,0:T(8,128)S(1)}, f32[2,2,152,128]{3,2,1,0:T(8,128)S(1)}, u32[]{:S(2)}, u32[]{:S(2)}) collective-permute-start(f32[2,2,152,128]{3,2,1,0:T(8,128)S(1)} %shard_map.74.after_hbm.refs_1_), channel_id=1, source_target_pairs={{32,0},{36,4},{40,8},{44,12},{48,16},{52,20},{56,24},{60,28},{64,3... | collective-permute-start | bytes 933896 | tf_op jit(solution)/shard_map/ppermute | solution.py:33
  26.5 0.7 %add_convert_fusion.code_ref = f32[4,150]{1,0:T(4,128)S(1)} fusion(s32[4,150]{1,0:T(4,128)} %param.9, s32[4,150]{1,0:T(4,128)} %param.10), kind=kLoop, calls=%fused_computation.5 | loop fusion | flops 1800 | bytes 7200 | tf_op jit(solution)/shard_map/convert_element_type | solution.py:319
  27.2 2.4 %copy-done = f32[2,4,150,1024]{3,1,2,0:T(4,128)S(1)} copy-done((f32[2,4,150,1024]{3,1,2,0:T(4,128)S(1)}, f32[2,4,150,1024]{3,1,2,0:T(4,128)}, u32[]{:S(2)}) %copy-start) | copy-done | bytes 4915224
  29.6 4.8 %shard_map.75.refs_0_ = f32[150,2,4,8,128]{4,3,2,1,0:T(8,128)S(1)} custom-call(f32[2,150,4,8,128]{4,3,2,1,0:T(8,128)S(1)} %bitcast.12, f32[4,150]{1,0:T(4,128)S(1)} %add_convert_fusion.code_ref, f32[2,2,152,128]{3,2,1,0:T(8,128)S(1)} %shard_map.74.after_hbm.refs_1_), custom_call_target="tpu_custom_call" | custom-call | tf_op jit(solution)/shard_map/pallas_call | solution.py:121
  34.4 0.0 collective-permute-done.10.refs_4_
  34.4 0.9 %collective-permute-done.9.refs_3_ = f32[2,2,152,128]{3,2,1,0:T(8,128)S(1)} collective-permute-done((f32[2,2,152,128]{3,2,1,0:T(8,128)S(1)}, f32[2,2,152,128]{3,2,1,0:T(8,128)S(1)}, u32[]{:S(2)}, u32[]{:S(2)}) %collective-permute-start.9) | collective-permute-done | bytes 311328 | tf_op jit(solution)/shard_map/ppermute | solution.py:33
  35.3 2.4 %shard_map.76 = (f32[2,4,768]{2,1,0:T(4,128)S(1)}, f32[2,4,768]{2,1,0:T(4,128)S(1)}) custom-call(f32[150,2,4,8,128]{4,3,2,1,0:T(8,128)S(1)} %shard_map.75.refs_0_, f32[2,2,152,128]{3,2,1,0:T(8,128)S(1)} %shard_map.74.after_hbm.refs_1_, f32[2,2,152,128]{3,2,1,0:T(8,128)S(1)} %collective-permute-done.8.refs_2_, ...), custom_call_target="tpu_custom_call" | custom-call | tf_op jit(solution)/shard_map/pallas_call | solution.py:301
  37.7 4.6 %collective-permute-start.11 = (f32[2,4,768]{2,1,0:T(4,128)S(1)}, f32[2,4,768]{2,1,0:T(4,128)S(1)}, u32[]{:S(2)}, u32[]{:S(2)}) collective-permute-start(f32[2,4,768]{2,1,0:T(4,128)S(1)} %get-tuple-element.8), channel_id=1, source_target_pairs={{0,1},{1,0},{2,3},{3,2},{4,5},{5,4},{6,7},{7,6},{8,9},{9,8},{10,11... | collective-permute-start | bytes 73736 | tf_op jit(solution)/shard_map/ppermute | solution.py:322
  42.4 0.8 %collective-permute-done.11 = f32[2,4,768]{2,1,0:T(4,128)S(1)} collective-permute-done((f32[2,4,768]{2,1,0:T(4,128)S(1)}, f32[2,4,768]{2,1,0:T(4,128)S(1)}, u32[]{:S(2)}, u32[]{:S(2)}) %collective-permute-start.11) | collective-permute-done | bytes 24608 | tf_op jit(solution)/shard_map/ppermute | solution.py:322
  43.2 1.2 %collective-permute-start.12 = (f32[4,768]{1,0:T(4,128)S(1)}, f32[4,768]{1,0:T(4,128)S(1)}, u32[]{:S(2)}, u32[]{:S(2)}) collective-permute-start(f32[4,768]{1,0:T(4,128)S(1)} %fusion), channel_id=1, source_target_pairs={{0,2},{1,3},{2,0},{3,1},{4,6},{5,7},{6,4},{7,5},{8,10},{9,11},{10,... | collective-permute-start | bytes 36872 | tf_op jit(solution)/shard_map/ppermute | solution.py:323
  44.4 1.3 %collective-permute-done.12 = f32[4,768]{1,0:T(4,128)S(1)} collective-permute-done((f32[4,768]{1,0:T(4,128)S(1)}, f32[4,768]{1,0:T(4,128)S(1)}, u32[]{:S(2)}, u32[]{:S(2)}) %collective-permute-start.12) | collective-permute-done | bytes 12320 | tf_op jit(solution)/shard_map/ppermute | solution.py:323
  45.8 0.6 %fusion.2 = f32[4,768]{1,0:T(4,128)} fusion(f32[4,768]{1,0:T(4,128)S(1)} %collective-permute-done.12, f32[2,4,768]{2,1,0:T(4,128)S(1)} %collective-permute-done.11, f32[2,4,768]{2,1,0:T(4,128)S(1)} %get-tuple-element.7), kind=kLoop, calls=%fused_computation.4 | loop fusion | flops 6144 | bytes 49152 | tf_op jit(solution)/shard_map/add | solution.py:324
  (11 shorter events, 0.0 us)
Async XLA Ops:
  0.0 5.1 %collective-permute-start = (f32[2,16,150]{2,1,0:T(8,128)}, f32[2,16,150]{2,1,0:T(8,128)S(1)}, u32[]{:S(2)}, u32[]{:S(2)}) collective-permute-start(f32[2,16,150]{2,1,0:T(8,128)} %bitcast.13), channel_id=1, source_target_pairs={{128,0},{132,4},{136,8},{140,12},{144,16},{148,20},{152,24},{156,2... | collective-permute-start | bytes 57608 | tf_op jit(solution)/shard_map/ppermute | solution.py:33
  5.1 0.8 %copy-start.4 = (f32[2,150,16]{1,2,0:T(8,128)S(1)}, f32[2,150,16]{1,2,0:T(8,128)}, u32[]{:S(2)}) copy-start(f32[2,150,16]{1,2,0:T(8,128)} %param.7) | copy-start | bytes 57604
  5.9 9.0 %collective-permute-start.4 = (f32[80,128]{1,0:T(8,128)S(1)}, f32[80,128]{1,0:T(8,128)S(1)}, u32[]{:S(2)}, u32[]{:S(2)}) collective-permute-start(f32[80,128]{1,0:T(8,128)S(1)} %shard_map.73.refs_0_), channel_id=1, source_target_pairs={{24,0},{28,4},{0,8},{4,12},{8,16},{12,20},{16,24},{20,28},{56,32},... | collective-permute-start | bytes 122888 | tf_op jit(solution)/shard_map/ppermute | solution.py:33
  9.2 5.8 %collective-permute-start.3 = (f32[80,128]{1,0:T(8,128)S(1)}, f32[80,128]{1,0:T(8,128)S(1)}, u32[]{:S(2)}, u32[]{:S(2)}) collective-permute-start(f32[80,128]{1,0:T(8,128)S(1)} %shard_map.73.refs_0_), channel_id=1, source_target_pairs={{8,0},{12,4},{16,8},{20,12},{24,16},{28,20},{0,24},{4,28},{40,32},... | collective-permute-start | bytes 122888 | tf_op jit(solution)/shard_map/ppermute | solution.py:33
  12.3 5.8 %collective-permute-start.2 = (f32[80,128]{1,0:T(8,128)S(1)}, f32[80,128]{1,0:T(8,128)S(1)}, u32[]{:S(2)}, u32[]{:S(2)}) collective-permute-start(f32[80,128]{1,0:T(8,128)S(1)} %shard_map.73.refs_0_), channel_id=1, source_target_pairs={{28,0},{0,4},{4,8},{8,12},{12,16},{16,20},{20,24},{24,28},{60,32},... | collective-permute-start | bytes 122888 | tf_op jit(solution)/shard_map/ppermute | solution.py:33
  13.0 5.0 %collective-permute-start.1 = (f32[80,128]{1,0:T(8,128)S(1)}, f32[80,128]{1,0:T(8,128)S(1)}, u32[]{:S(2)}, u32[]{:S(2)}) collective-permute-start(f32[80,128]{1,0:T(8,128)S(1)} %shard_map.73.refs_0_), channel_id=1, source_target_pairs={{4,0},{8,4},{12,8},{16,12},{20,16},{24,20},{28,24},{0,28},{36,32},... | collective-permute-start | bytes 122888 | tf_op jit(solution)/shard_map/ppermute | solution.py:33
  15.0 4.6 %collective-permute-start.7 = (f32[80,128]{1,0:T(8,128)S(1)}, f32[80,128]{1,0:T(8,128)S(1)}, u32[]{:S(2)}, u32[]{:S(2)}) collective-permute-start(f32[80,128]{1,0:T(8,128)S(1)} %collective-permute-done.4.refs_4_), channel_id=1, source_target_pairs={{28,0},{0,4},{4,8},{8,12},{12,16},{16,20},{20,24},{24,28},{60,32},... | collective-permute-start | bytes 122888 | tf_op jit(solution)/shard_map/ppermute | solution.py:33
  15.0 4.8 %collective-permute-start.6 = (f32[80,128]{1,0:T(8,128)S(1)}, f32[80,128]{1,0:T(8,128)S(1)}, u32[]{:S(2)}, u32[]{:S(2)}) collective-permute-start(f32[80,128]{1,0:T(8,128)S(1)} %collective-permute-done.3.refs_3_), channel_id=1, source_target_pairs={{8,0},{12,4},{16,8},{20,12},{24,16},{28,20},{0,24},{4,28},{40,32},... | collective-permute-start | bytes 122888 | tf_op jit(solution)/shard_map/ppermute | solution.py:33
  17.2 3.4 %collective-permute-start.5 = (f32[80,128]{1,0:T(8,128)S(1)}, f32[80,128]{1,0:T(8,128)S(1)}, u32[]{:S(2)}, u32[]{:S(2)}) collective-permute-start(f32[80,128]{1,0:T(8,128)S(1)} %collective-permute-done.3.refs_3_), channel_id=1, source_target_pairs={{4,0},{8,4},{12,8},{16,12},{20,16},{24,20},{28,24},{0,28},{36,32},... | collective-permute-start | bytes 122888 | tf_op jit(solution)/shard_map/ppermute | solution.py:33
  20.8 13.6 %collective-permute-start.10 = (f32[2,2,152,128]{3,2,1,0:T(8,128)S(1)}, f32[2,2,152,128]{3,2,1,0:T(8,128)S(1)}, u32[]{:S(2)}, u32[]{:S(2)}) collective-permute-start(f32[2,2,152,128]{3,2,1,0:T(8,128)S(1)} %shard_map.74.after_hbm.refs_1_), channel_id=1, source_target_pairs={{64,0},{68,4},{72,8},{76,12},{80,16},{84,20},{88,24},{92,28},{96,3... | collective-permute-start | bytes 933896 | tf_op jit(solution)/shard_map/ppermute | solution.py:33
  23.8 11.4 %collective-permute-start.9 = (f32[2,2,152,128]{3,2,1,0:T(8,128)S(1)}, f32[2,2,152,128]{3,2,1,0:T(8,128)S(1)}, u32[]{:S(2)}, u32[]{:S(2)}) collective-permute-start(f32[2,2,152,128]{3,2,1,0:T(8,128)S(1)} %shard_map.74.after_hbm.refs_1_), channel_id=1, source_target_pairs={{96,0},{100,4},{104,8},{108,12},{112,16},{116,20},{120,24},{124,28... | collective-permute-start | bytes 933896 | tf_op jit(solution)/shard_map/ppermute | solution.py:33
  24.2 11.0 %collective-permute-start.8 = (f32[2,2,152,128]{3,2,1,0:T(8,128)S(1)}, f32[2,2,152,128]{3,2,1,0:T(8,128)S(1)}, u32[]{:S(2)}, u32[]{:S(2)}) collective-permute-start(f32[2,2,152,128]{3,2,1,0:T(8,128)S(1)} %shard_map.74.after_hbm.refs_1_), channel_id=1, source_target_pairs={{32,0},{36,4},{40,8},{44,12},{48,16},{52,20},{56,24},{60,28},{64,3... | collective-permute-start | bytes 933896 | tf_op jit(solution)/shard_map/ppermute | solution.py:33
  27.2 2.4 %copy-start = (f32[2,4,150,1024]{3,1,2,0:T(4,128)S(1)}, f32[2,4,150,1024]{3,1,2,0:T(4,128)}, u32[]{:S(2)}) copy-start(f32[2,4,150,1024]{3,1,2,0:T(4,128)} %param.8) | copy-start | bytes 14745604
  29.6 5.7 %copy-start.1 = (f32[2,128,128]{2,1,0:T(8,128)S(1)}, f32[2,128,128]{2,1,0:T(8,128)}, u32[]{:S(2)}) copy-start(f32[2,128,128]{2,1,0:T(8,128)} %constant.9.clone.refs_6_) | copy-start | bytes 393220
  29.6 5.7 %copy-start.2 = (f32[256,64]{1,0:T(8,128)S(1)}, f32[256,64]{1,0:T(8,128)}, u32[]{:S(2)}) copy-start(f32[256,64]{1,0:T(8,128)} %constant.8.clone.refs_5_) | copy-start | bytes 196612
  29.6 5.7 %copy-start.3 = (f32[2,96,128]{2,1,0:T(8,128)S(1)}, f32[2,96,128]{2,1,0:T(8,128)}, u32[]{:S(2)}) copy-start(f32[2,96,128]{2,1,0:T(8,128)} %constant.10.clone.refs_7_) | copy-start | bytes 294916
  37.7 5.5 %collective-permute-start.11 = (f32[2,4,768]{2,1,0:T(4,128)S(1)}, f32[2,4,768]{2,1,0:T(4,128)S(1)}, u32[]{:S(2)}, u32[]{:S(2)}) collective-permute-start(f32[2,4,768]{2,1,0:T(4,128)S(1)} %get-tuple-element.8), channel_id=1, source_target_pairs={{0,1},{1,0},{2,3},{3,2},{4,5},{5,4},{6,7},{7,6},{8,9},{9,8},{10,11... | collective-permute-start | bytes 73736 | tf_op jit(solution)/shard_map/ppermute | solution.py:322
  43.2 2.5 %collective-permute-start.12 = (f32[4,768]{1,0:T(4,128)S(1)}, f32[4,768]{1,0:T(4,128)S(1)}, u32[]{:S(2)}, u32[]{:S(2)}) collective-permute-start(f32[4,768]{1,0:T(4,128)S(1)} %fusion), channel_id=1, source_target_pairs={{0,2},{1,3},{2,0},{3,1},{4,6},{5,7},{6,4},{7,5},{8,10},{9,11},{10,... | collective-permute-start | bytes 36872 | tf_op jit(solution)/shard_map/ppermute | solution.py:323

commit v3 on v2

v3 whole, which is shorter than its diff:
```python
import functools
import math

import jax
import jax.numpy as jnp
import numpy as np
from jax import lax
from jax.experimental import pallas as pl
from jax.experimental.pallas import tpu as pltpu
from jax.sharding import PartitionSpec as P

FREQS = 1024
FIRST = 128
NFFT = 4096
LAGS = 3072
CHANS = 150
ROWS = 152
TMPL = 4
XH, YS, ZS = 2, 4, 8

VMEM = pl.BlockSpec(memory_space=pltpu.VMEM)
HIGH = lax.Precision.HIGHEST
PARAMS = pltpu.CompilerParams(vmem_limit_bytes=16 << 20)
LARGE = pltpu.CompilerParams(vmem_limit_bytes=45 << 20)


def from_offset(x, dx=0, dy=0, dz=0):
    pairs = []
    for i in range(XH * YS * ZS):
        a, b, c = i // (YS * ZS), i // ZS % YS, i % ZS
        src = (a + dx) % XH * (YS * ZS) + (b + dy) % YS * ZS + (c + dz) % ZS
        pairs.append((src, i))
    return lax.ppermute(x, "tmpl", pairs)


def half_turn_fit():
    x = np.cos(np.pi * (np.arange(400) + 0.5) / 400) * 0.25 + 0.25
    r = np.sqrt(x)
    even = np.polynomial.Chebyshev.fit(x, np.cos(np.pi * r), 5, domain=[0, 0.5])
    odd = np.polynomial.Chebyshev.fit(x, np.sin(np.pi * r) / r, 5, domain=[0, 0.5])
    return [[float(v) for v in p.convert(kind=np.polynomial.Polynomial).coef] for p in (even, odd)]


COS_FIT, SIN_FIT = half_turn_fit()


def sincos(turns):
    near = jnp.floor(turns + 0.5)
    r = turns - near
    half = near * 0.5
    sign = 1.0 - 4.0 * (half - jnp.floor(half))
    sq = r * r
    c, s = COS_FIT[-1], SIN_FIT[-1]
    for a, b in zip(COS_FIT[-2::-1], SIN_FIT[-2::-1]):
        c, s = c * sq + a, s * sq + b
    return sign, c, s * r


STEP = 50
STEPS = CHANS // STEP


def template_kernel(spec_hbm, wide_ref, after_hbm, out_ref, spec_ref, weight_ref, sems):
    def part(i):
        at = pl.ds(i * STEP, STEP)
        return [pltpu.make_async_copy(spec_hbm.at[k, at], spec_ref.at[k, at], sems.at[i, k]) for k in range(2)]

    for copy in part(0) + part(1):
        copy.start()
    row = lax.broadcasted_iota(jnp.int32, (8, 128), 0)
    lane = lax.broadcasted_iota(jnp.int32, (8, 128), 1)
    first_bin = (FIRST * (row // 4 + 1) + lane).astype(jnp.float32) * (2.0 / NFFT)

    def weigh(c):
        power = None
        for m in range(4):
            re, im = spec_ref[0, c, m], spec_ref[1, c, m]
            one = re * re + im * im
            power = one if power is None else power + one
        power = power + pltpu.roll(power, 4, 0)
        power = jnp.broadcast_to(jnp.sum(power, axis=1, keepdims=True), (8, 128))
        weight = lax.rsqrt(power * (1.0 / FREQS) + 1e-06)
        weight_ref[c] = jnp.where(wide_ref[c, 0] >= NFFT, weight, 0.0)

    def phase(c):
        sign, er, ei = sincos(first_bin * wide_ref[c, 0])
        wr, wi = wide_ref[c, 1], wide_ref[c, 2]
        weight = weight_ref[c] * sign
        er, ei = er * weight, ei * weight
        for m in range(4):
            re, im = spec_ref[0, c, m], spec_ref[1, c, m]
            out_ref[c, 0, m] = re * er + im * ei
            out_ref[c, 1, m] = re * ei - im * er
            if m < 3:
                er, ei = er * wr - ei * wi, er * wi + ei * wr

    for i in range(STEPS):
        for copy in part(i):
            copy.wait()
        if i + 2 < STEPS:
            for copy in part(i + 2):
                copy.start()
        for body, unroll in ((weigh, 25), (phase, 10)):

            def step(j, carry, body=body, unroll=unroll, i=i):
                for k in range(unroll):
                    body(i * STEP + j * unroll + k)
                return carry

            lax.fori_loop(0, STEP // unroll, step, 0)


def template_view(tmpl_spec):
    view = tmpl_spec.reshape(2, TMPL, CHANS, 4, 2, 128).transpose(0, 2, 3, 4, 1, 5)
    return view.reshape(2, CHANS, 4, 8, 128)


def template_part(tmpl_spec, wide, after):
    return pl.pallas_call(
        template_kernel,
        out_shape=jax.ShapeDtypeStruct((CHANS, 2, 4, 8, 128), jnp.float32),
        in_specs=[pl.BlockSpec(memory_space=pl.ANY), VMEM, pl.BlockSpec(memory_space=pl.ANY)],
        out_specs=VMEM,
        scratch_shapes=[
            pltpu.VMEM((2, CHANS, 4, 8, 128), jnp.float32),
            pltpu.VMEM((CHANS, 8, 128), jnp.float32),
            pltpu.SemaphoreType.DMA((STEPS, 2)),
        ],
        compiler_params=LARGE,
    )(template_view(tmpl_spec), wide, after)


REST = CHANS - 128
HELD = 3
REST_AT = HELD * 32
DENSE = REST_AT + 32


def put(j, ref, k, out_ref):
    out_ref[16 * j : 16 * j + 16, :] = ref[k, :, 0:128]
    at = REST_AT + j // 4 * 16
    out_ref[at : at + 16, 32 * (j % 4) : 32 * (j % 4) + REST] = ref[k, :, 128:CHANS]


def early_kernel(raw_ref, code_ref, own_ref, wide_ref, pair_ref):
    own_ref[...] = jnp.zeros((DENSE, 128), jnp.float32)
    for k in range(2):
        put(k, raw_ref, k, own_ref)
    pair_ref[0:4, 0:CHANS] = code_ref[...]
    pair_ref[4:8, 0:CHANS] = code_ref[...]
    for start in (0, 128):
        codes = pair_ref[:, start : start + 128]
        sign, wr, wi = sincos(codes * (2.0 * 2 * FIRST / NFFT))
        wr, wi = wr * sign, wi * sign
        for at in range(min(128, CHANS - start)):
            for k, part in enumerate((codes, wr, wi)):
                wide_ref[start + at, k] = jnp.broadcast_to(part[:, at : at + 1], (8, 128))


def early_part(raw, code):
    return pl.pallas_call(
        early_kernel,
        out_shape=(
            jax.ShapeDtypeStruct((DENSE, 128), jnp.float32),
            jax.ShapeDtypeStruct((CHANS, 3, 8, 128), jnp.float32),
        ),
        in_specs=[VMEM] * 2,
        out_specs=(VMEM, VMEM),
        scratch_shapes=[pltpu.VMEM((8, 256), jnp.float32)],
        compiler_params=PARAMS,
    )(raw, code)


def dense_kernel(own_ref, other_ref, far_ref, out_ref):
    out_ref[...] = own_ref[...]
    for k in range(2):
        put(2 + k, other_ref, k, out_ref)
        put(4 + k, far_ref, k, out_ref)


Z_ORDER = (0, 1, -1, 2, -2, 3, 4, -3)


def pack_kernel(*refs):
    parts, one_ref, far_ref, held = refs[:8], refs[8], refs[9], refs[10]
    z = lax.axis_index("tmpl") % ZS
    for part, dz in zip(parts, Z_ORDER):
        at = pl.multiple_of(lax.rem(z + dz + ZS, ZS) * 16, 16)
        for j in range(DENSE // 16):
            held[j, pl.ds(at, 16), :] = part[16 * j : 16 * j + 16, :]
    rest = [held[j].T for j in range(REST_AT // 16, DENSE // 16)]
    for j in range(2 * HELD):
        out = one_ref.at[j // 2, j % 2] if j < 4 else far_ref.at[j % 2]
        out[0:128, :] = held[j].T
        out[128:ROWS, :] = rest[j // 4][32 * (j % 4) : 32 * (j % 4) + ROWS - 128]


def gather_xz(dense, other, far):
    own = pl.pallas_call(
        dense_kernel,
        out_shape=jax.ShapeDtypeStruct((DENSE, 128), jnp.float32),
        in_specs=[VMEM] * 3,
        out_specs=VMEM,
        compiler_params=PARAMS,
    )(dense, other, far)
    up = from_offset(own, dz=1)
    down = from_offset(own, dz=-1)
    up2 = from_offset(own, dz=2)
    down2 = from_offset(own, dz=-2)
    up3 = from_offset(up2, dz=1)
    up4 = from_offset(up2, dz=2)
    down3 = from_offset(down2, dz=-1)
    return pl.pallas_call(
        pack_kernel,
        out_shape=(
            jax.ShapeDtypeStruct((2, 2, ROWS, 128), jnp.float32),
            jax.ShapeDtypeStruct((2, ROWS, 128), jnp.float32),
        ),
        in_specs=[VMEM] * 8,
        out_specs=(VMEM, VMEM),
        scratch_shapes=[pltpu.VMEM((DENSE // 16, 128, 128), jnp.float32)],
        compiler_params=PARAMS,
    )(own, up, down, up2, down2, up3, up4, down3)


def gather_xy(one, far):
    return one, from_offset(one, dy=1), from_offset(one, dy=-1), far, from_offset(far, dx=1)


def tables():
    kl = np.arange(32)
    fh = np.arange(8)
    a = 2 * np.pi * (np.outer(kl, fh + 1) % 32) / 32
    first = np.zeros((2, TMPL, 32, 2, 4, 2, TMPL))
    for t in range(TMPL):
        c, s = np.cos(a).reshape(32, 4, 2), np.sin(a).reshape(32, 4, 2)
        first[0, t, :, 0, :, :, t] = c
        first[0, t, :, 1, :, :, t] = -s
        first[1, t, :, 0, :, :, t] = s
        first[1, t, :, 1, :, :, t] = c
    fl = np.arange(128)
    b = np.tile(2 * np.pi * np.outer(kl, fl) / NFFT, (TMPL, 1))
    kh = (4 * np.arange(24)[None, :] + np.arange(4)[:, None]).reshape(96)
    g = 2 * np.pi * (np.outer(kh, fl) % 128) / 128
    rows = [first.reshape(256, 64)]
    twist = np.stack([np.cos(b), np.sin(b)])
    last = np.stack([np.cos(g), -np.sin(g)]) / FREQS
    return tuple(np.asarray(v, np.float32) for v in (rows[0], twist, last))


def network_kernel(*refs):
    spec_ref, (one_ref, up_ref, down_ref, far_ref, other_far_ref) = refs[0], refs[1:6]
    first_ref, twist_ref, last_ref, keep_ref, send_ref, data_ref, piece_ref = refs[6:]
    me = lax.axis_index("tmpl")
    x, y = me // (YS * ZS), me // ZS % YS

    views = [(ref.at[dx], dx, dy) for ref, dy in ((one_ref, 0), (up_ref, 1), (down_ref, YS - 1)) for dx in range(XH)]
    views += [(far_ref, 0, 2), (other_far_ref, 1, 2)]
    power = None
    for block, _, _ in views:
        re, im = block[0], block[1]
        part = re * re + im * im
        power = part if power is None else power + part
    power = jnp.sum(power, axis=1, keepdims=True)
    scale = jnp.broadcast_to(lax.rsqrt(power * (1.0 / FREQS) + 1e-06), (ROWS, 128))
    for block, dx, dy in views:
        group = lax.rem(x + dx, XH) * YS + lax.rem(y + dy, YS)
        for k in range(2):
            data_ref[group, k] = block[k] * scale

    lower = lax.broadcasted_iota(jnp.int32, (8, 128), 0) < 4

    def channel(c, acc):
        acc = list(acc)
        for m in range(4):
            d = []
            for k in range(2):
                one = jnp.broadcast_to(data_ref[2 * m, k, pl.ds(c, 1), :], (8, 128))
                two = jnp.broadcast_to(data_ref[2 * m + 1, k, pl.ds(c, 1), :], (8, 128))
                d.append(jnp.where(lower, one, two))
            tr, ti = spec_ref[c, 0, m], spec_ref[c, 1, m]
            acc[m] = acc[m] + (tr * d[0] - ti * d[1])
            acc[4 + m] = acc[4 + m] + (tr * d[1] + ti * d[0])
        return tuple(acc)

    acc = lax.fori_loop(0, CHANS, channel, (jnp.zeros((8, 128), jnp.float32),) * 8, unroll=5)
    to_lags(acc, first_ref, twist_ref, last_ref, piece_ref)
    keep_ref[0] = piece_ref[0]
    keep_ref[1] = piece_ref[2]
    send_ref[0] = piece_ref[1]
    send_ref[1] = piece_ref[3]


def to_lags(acc, first_ref, twist_ref, last_ref, piece_ref):
    spectra = jnp.concatenate(acc, axis=0)
    mixed = jnp.dot(first_ref[...], spectra, precision=HIGH, preferred_element_type=jnp.float32)
    yr, yi = mixed[0:128], mixed[128:256]
    tc, ts = twist_ref[0], twist_ref[1]
    zr, zi = yr * tc - yi * ts, yr * ts + yi * tc
    dims = (((1,), (1,)), ((), ()))
    lags = lax.dot_general(last_ref[0], zr, dims, precision=HIGH, preferred_element_type=jnp.float32)
    lags = lags + lax.dot_general(last_ref[1], zi, dims, precision=HIGH, preferred_element_type=jnp.float32)
    lane = lax.broadcasted_iota(jnp.int32, (24, 128), 1) // 32
    chan = lax.axis_index("chan")
    for t in range(TMPL):
        out = None
        for r in range(4):
            part = lags[24 * r : 24 * r + 24]
            if (r - t) % 4:
                part = pltpu.roll(part, (r - t) % 4 * 32, 1)
            out = part if out is None else jnp.where(lane == r, part, out)
        for j in range(4):
            for g in range(6):
                piece_ref[j ^ chan, t : t + 1, g * 128 : (g + 1) * 128] = out[6 * j + g : 6 * j + g + 1]


def network_part(spectra, blocks):
    lag_dev = LAGS // 4
    shape = jax.ShapeDtypeStruct((2, TMPL, lag_dev), jnp.float32)
    return pl.pallas_call(
        network_kernel,
        out_shape=(shape, shape),
        in_specs=[VMEM] * 9,
        out_specs=(VMEM, VMEM),
        scratch_shapes=[
            pltpu.VMEM((8, 2, ROWS, 128), jnp.float32),
            pltpu.VMEM((4, TMPL, lag_dev), jnp.float32),
        ],
        compiler_params=PARAMS,
    )(spectra, *blocks, *tables())


def on_device(data_spec, tmpl_spec, shifts, mask):
    raw = data_spec.transpose(0, 2, 1)
    code = (shifts + NFFT * mask).astype(jnp.float32)
    dense, wide = early_part(raw, code)
    one, far = gather_xz(dense, from_offset(raw, dx=1), from_offset(raw, dy=2))
    blocks = gather_xy(one, far)
    spectra = template_part(tmpl_spec, wide, one)
    keep, send = network_part(spectra, blocks)
    got = lax.ppermute(send, "chan", [(i, i ^ 1) for i in range(4)])
    other = lax.ppermute(keep[1] + got[1], "chan", [(i, i ^ 2) for i in range(4)])
    return keep[0] + got[0] + other


def solution(mesh):
    return jax.shard_map(
        on_device,
        mesh=mesh,
        in_specs=(
            P(None, "chan", "tmpl"),
            P(None, "tmpl", "chan", None),
            P("tmpl", "chan"),
            P("tmpl", "chan"),
        ),
        out_specs=P("tmpl", "chan"),
        check_vma=False,
    )
```

time: 46.8 us -> 46.1 us (0.985)
  local copies, waits for them, and re-layouts: 3.16 us -> 0.77 us
  starting transfers between devices: 27.2 us -> 28.4 us
  waiting for transfers between devices: 7.17 us -> 7.92 us
    unnamed x10 -> x8, local copies, waits for them, and re-layouts: 3.16 us -> 0.77 us
    ppermute x11 -> x12, starting transfers between devices: 21.4 us -> 23 us  [from_offset(): return lax.ppermute(x, 'tmpl', pairs)]
    ppermute x1, waiting for transfers between devices: 1.34 us -> 2.23 us  [on_device(): lax.ppermute(keep[1] + got[1], 'chan', [(i, i ^ 2) for i in range(4)])]
    ppermute x1, starting transfers between devices: 1.21 us -> 0.31 us  [on_device(): lax.ppermute(keep[1] + got[1], 'chan', [(i, i ^ 2) for i in range(4)])]
    ppermute x11 -> x12, waiting for transfers between devices: 4.99 us -> 4.84 us  [from_offset(): return lax.ppermute(x, 'tmpl', pairs)]
    pallas_call x3 -> x4, Pallas kernels: 7.39 us -> 7.36 us  [the longest x1 4.07 us: template_part(): pl.pallas_call(template_kernel, out_shape=jax.ShapeDtypeStruct((CHANS, 2,...]
  transfers between devices with their start and end apart: 13 -> 14, of which waited for: 7 -> 6; matrix products, arithmetic and copies ran while one was open for 2% -> 2% of each run, Pallas kernels for 10% -> 11%
where the time goes in v3:
time: 46.1 us; the launch traced here: 45.9 us
  starting transfers between devices  28.4 us (62%)
  waiting for transfers between devices  7.92 us (17%)
  Pallas kernels  7.44 us (16%)
  other arithmetic  1.32 us (3%)
  local copies, waits for them, and re-layouts  0.77 us (2%)
    ppermute x12, starting transfers between devices, from_offset(): return lax.ppermute(x, 'tmpl', pairs)  23 us
    ppermute x1, starting transfers between devices, on_device(): got = lax.ppermute(send, 'chan', [(i, i ^ 1) for i in range(4)])  5.08 us
    ppermute x12, waiting for transfers between devices, from_offset(): return lax.ppermute(x, 'tmpl', pairs)  4.84 us
    pallas_call x1, Pallas kernels, template_part(): pl.pallas_call(template_kernel, out_shape=jax.ShapeDtypeStruct((CHANS, 2,...  4.07 us
    pallas_call x1, Pallas kernels, network_part(): pl.pallas_call(network_kernel, out_shape=(shape, shape), in_specs=[VMEM]...  2.26 us
    ppermute x1, waiting for transfers between devices, on_device(): lax.ppermute(keep[1] + got[1], 'chan', [(i, i ^ 2) for i in range(4)])  2.23 us
  transfers between devices with their start and end apart: 14, of which 6 were waited for; matrix products, arithmetic and copies ran while one was open for 2% of the time, Pallas kernels for 11%

profile of v3, /device:TPU:1, one launch (start us, length us, event | category | flops | bytes accessed | tf_op | source)
XLA Modules:
  0.0 45.9 jit_solution(2303423916937830344)
XLA Ops:
  0.0 3.6 %collective-permute-start = (f32[2,16,150]{2,1,0:T(8,128)}, f32[2,16,150]{2,1,0:T(8,128)S(1)}, u32[]{:S(2)}, u32[]{:S(2)}) collective-permute-start(f32[2,16,150]{2,1,0:T(8,128)} %bitcast.12), channel_id=1, source_target_pairs={{128,0},{132,4},{136,8},{140,12},{144,16},{148,20},{152,24},{156,2... | collective-permute-start | bytes 57608 | tf_op jit(solution)/shard_map/ppermute | solution.py:33
  3.6 2.9 %collective-permute-start.1 = (f32[2,16,150]{2,1,0:T(8,128)}, f32[2,16,150]{2,1,0:T(8,128)S(1)}, u32[]{:S(2)}, u32[]{:S(2)}) collective-permute-start(f32[2,16,150]{2,1,0:T(8,128)} %bitcast.13), channel_id=1, source_target_pairs={{64,0},{68,4},{72,8},{76,12},{80,16},{84,20},{88,24},{92,28},{96,3... | collective-permute-start | bytes 57608 | tf_op jit(solution)/shard_map/ppermute | solution.py:33
  6.5 0.7 %add_convert_fusion.code_ref = f32[4,150]{1,0:T(4,128)S(1)} fusion(s32[4,150]{1,0:T(4,128)} %param.9, s32[4,150]{1,0:T(4,128)} %param.10), kind=kLoop, calls=%fused_computation.5 | loop fusion | flops 1800 | bytes 7200 | tf_op jit(solution)/shard_map/convert_element_type | solution.py:335
  7.2 0.8 %copy-done.3 = f32[2,150,16]{1,2,0:T(8,128)S(1)} copy-done((f32[2,150,16]{1,2,0:T(8,128)S(1)}, f32[2,150,16]{1,2,0:T(8,128)}, u32[]{:S(2)}) %copy-start.3) | copy-done | bytes 19224
  8.0 0.8 %shard_map.73 = (f32[128,128]{1,0:T(8,128)S(1)}, f32[150,3,8,128]{3,2,1,0:T(8,128)S(1)}) custom-call(f32[2,16,150]{2,1,0:T(8,128)S(1)} %bitcast.14, f32[4,150]{1,0:T(4,128)S(1)} %add_convert_fusion.code_ref), custom_call_target="tpu_custom_call" | custom-call | tf_op jit(solution)/shard_map/pallas_call | solution.py:161
  8.7 0.0 collective-permute-done.other_ref
  8.7 0.0 collective-permute-done.1.far_ref
  8.8 0.1 shard_map.74.refs_0_
  8.8 6.0 %collective-permute-start.4 = (f32[128,128]{1,0:T(8,128)S(1)}, f32[128,128]{1,0:T(8,128)S(1)}, u32[]{:S(2)}, u32[]{:S(2)}) collective-permute-start(f32[128,128]{1,0:T(8,128)S(1)} %shard_map.74.refs_0_), channel_id=1, source_target_pairs={{8,0},{12,4},{16,8},{20,12},{24,16},{28,20},{0,24},{4,28},{40,32},... | collective-permute-start | bytes 196616 | tf_op jit(solution)/shard_map/ppermute | solution.py:33
  14.9 0.0 collective-permute-start.5
  14.9 3.1 %collective-permute-start.2 = (f32[128,128]{1,0:T(8,128)S(1)}, f32[128,128]{1,0:T(8,128)S(1)}, u32[]{:S(2)}, u32[]{:S(2)}) collective-permute-start(f32[128,128]{1,0:T(8,128)S(1)} %shard_map.74.refs_0_), channel_id=1, source_target_pairs={{4,0},{8,4},{12,8},{16,12},{20,16},{24,20},{28,24},{0,28},{36,32},... | collective-permute-start | bytes 196616 | tf_op jit(solution)/shard_map/ppermute | solution.py:33
  18.0 0.0 collective-permute-done.4.refs_3_
  18.0 2.7 %collective-permute-start.6 = (f32[128,128]{1,0:T(8,128)S(1)}, f32[128,128]{1,0:T(8,128)S(1)}, u32[]{:S(2)}, u32[]{:S(2)}) collective-permute-start(f32[128,128]{1,0:T(8,128)S(1)} %collective-permute-done.4.refs_3_), channel_id=1, source_target_pairs={{4,0},{8,4},{12,8},{16,12},{20,16},{24,20},{28,24},{0,28},{36,32},... | collective-permute-start | bytes 196616 | tf_op jit(solution)/shard_map/ppermute | solution.py:33
  20.7 0.1 collective-permute-start.7
  20.8 1.5 %collective-permute-start.8 = (f32[128,128]{1,0:T(8,128)S(1)}, f32[128,128]{1,0:T(8,128)S(1)}, u32[]{:S(2)}, u32[]{:S(2)}) collective-permute-start(f32[128,128]{1,0:T(8,128)S(1)} %collective-permute-done.5.refs_4_), channel_id=1, source_target_pairs={{28,0},{0,4},{4,8},{8,12},{12,16},{16,20},{20,24},{24,28},{60,32},... | collective-permute-start | bytes 196616 | tf_op jit(solution)/shard_map/ppermute | solution.py:33
  22.3 0.9 %collective-permute-done.3.refs_2_ = f32[128,128]{1,0:T(8,128)S(1)} collective-permute-done((f32[128,128]{1,0:T(8,128)S(1)}, f32[128,128]{1,0:T(8,128)S(1)}, u32[]{:S(2)}, u32[]{:S(2)}) %collective-permute-start.3) | collective-permute-done | bytes 65568 | tf_op jit(solution)/shard_map/ppermute | solution.py:33
  23.2 1.8 %collective-permute-done.7.refs_6_ = f32[128,128]{1,0:T(8,128)S(1)} collective-permute-done((f32[128,128]{1,0:T(8,128)S(1)}, f32[128,128]{1,0:T(8,128)S(1)}, u32[]{:S(2)}, u32[]{:S(2)}) %collective-permute-start.7) | collective-permute-done | bytes 65568 | tf_op jit(solution)/shard_map/ppermute | solution.py:33
  25.0 0.9 %collective-permute-done.8.refs_7_ = f32[128,128]{1,0:T(8,128)S(1)} collective-permute-done((f32[128,128]{1,0:T(8,128)S(1)}, f32[128,128]{1,0:T(8,128)S(1)}, u32[]{:S(2)}, u32[]{:S(2)}) %collective-permute-start.8) | collective-permute-done | bytes 65568 | tf_op jit(solution)/shard_map/ppermute | solution.py:33
  25.9 0.2 shard_map.75
  26.2 0.6 %collective-permute-start.10 = (f32[2,2,152,128]{3,2,1,0:T(8,128)S(1)}, f32[2,2,152,128]{3,2,1,0:T(8,128)S(1)}, u32[]{:S(2)}, u32[]{:S(2)}) collective-permute-start(f32[2,2,152,128]{3,2,1,0:T(8,128)S(1)} %get-tuple-element.13.after_hbm.refs_1_), channel_id=1, source_target_pairs={{96,0},{100,4},{104,8},{108,12},{112,16},{116,20},{120,24},{124,28... | collective-permute-start | bytes 933896 | tf_op jit(solution)/shard_map/ppermute | solution.py:33
  26.7 2.2 %collective-permute-start.9 = (f32[2,2,152,128]{3,2,1,0:T(8,128)S(1)}, f32[2,2,152,128]{3,2,1,0:T(8,128)S(1)}, u32[]{:S(2)}, u32[]{:S(2)}) collective-permute-start(f32[2,2,152,128]{3,2,1,0:T(8,128)S(1)} %get-tuple-element.13.after_hbm.refs_1_), channel_id=1, source_target_pairs={{32,0},{36,4},{40,8},{44,12},{48,16},{52,20},{56,24},{60,28},{64,3... | collective-permute-start | bytes 933896 | tf_op jit(solution)/shard_map/ppermute | solution.py:33
  28.9 0.3 collective-permute-start.11
  29.3 4.1 %shard_map.76.refs_0_ = f32[150,2,4,8,128]{4,3,2,1,0:T(8,128)S(1)} custom-call(f32[2,150,4,8,128]{4,3,2,1,0:T(8,128)} %bitcast.15, f32[150,3,8,128]{3,2,1,0:T(8,128)S(1)} %get-tuple-element.11.wide_ref, f32[2,2,152,128]{3,2,1,0:T(8,128)S(1)} %get-tuple-element.13.after_hbm.refs_1_), custom_call_target="tpu_custom_call" | custom-call | tf_op jit(solution)/shard_map/pallas_call | solution.py:119
  33.3 1.2 %collective-permute-done.11.refs_5_ = f32[2,152,128]{2,1,0:T(8,128)S(1)} collective-permute-done((f32[2,152,128]{2,1,0:T(8,128)S(1)}, f32[2,152,128]{2,1,0:T(8,128)S(1)}, u32[]{:S(2)}, u32[]{:S(2)}) %collective-permute-start.11) | collective-permute-done | bytes 155680 | tf_op jit(solution)/shard_map/ppermute | solution.py:33
  34.5 0.0 collective-permute-done.10.refs_3_
  34.5 0.0 collective-permute-done.9.refs_2_
  34.5 2.3 %shard_map.77 = (f32[2,4,768]{2,1,0:T(4,128)S(1)}, f32[2,4,768]{2,1,0:T(4,128)S(1)}) custom-call(f32[150,2,4,8,128]{4,3,2,1,0:T(8,128)S(1)} %shard_map.76.refs_0_, f32[2,2,152,128]{3,2,1,0:T(8,128)S(1)} %get-tuple-element.13.after_hbm.refs_1_, f32[2,2,152,128]{3,2,1,0:T(8,128)S(1)} %collective-permute-done.9.refs_2_, ...), custom_call_target="tpu_custom_call" | custom-call | tf_op jit(solution)/shard_map/pallas_call | solution.py:320
  36.8 5.1 %collective-permute-start.12 = (f32[2,4,768]{2,1,0:T(4,128)S(1)}, f32[2,4,768]{2,1,0:T(4,128)S(1)}, u32[]{:S(2)}, u32[]{:S(2)}) collective-permute-start(f32[2,4,768]{2,1,0:T(4,128)S(1)} %get-tuple-element.16), channel_id=1, source_target_pairs={{0,1},{1,0},{2,3},{3,2},{4,5},{5,4},{6,7},{7,6},{8,9},{9,8},{10,11... | collective-permute-start | bytes 73736 | tf_op jit(solution)/shard_map/ppermute | solution.py:341
  41.9 0.8 %collective-permute-done.12 = f32[2,4,768]{2,1,0:T(4,128)S(1)} collective-permute-done((f32[2,4,768]{2,1,0:T(4,128)S(1)}, f32[2,4,768]{2,1,0:T(4,128)S(1)}, u32[]{:S(2)}, u32[]{:S(2)}) %collective-permute-start.12) | collective-permute-done | bytes 24608 | tf_op jit(solution)/shard_map/ppermute | solution.py:341
  42.8 0.3 collective-permute-start.13
  43.1 2.2 %collective-permute-done.13 = f32[4,768]{1,0:T(4,128)S(1)} collective-permute-done((f32[4,768]{1,0:T(4,128)S(1)}, f32[4,768]{1,0:T(4,128)S(1)}, u32[]{:S(2)}, u32[]{:S(2)}) %collective-permute-start.13) | collective-permute-done | bytes 12320 | tf_op jit(solution)/shard_map/ppermute | solution.py:342
  45.3 0.6 %fusion.2 = f32[4,768]{1,0:T(4,128)} fusion(f32[4,768]{1,0:T(4,128)S(1)} %collective-permute-done.13, f32[2,4,768]{2,1,0:T(4,128)S(1)} %collective-permute-done.12, f32[2,4,768]{2,1,0:T(4,128)S(1)} %get-tuple-element.15), kind=kLoop, calls=%fused_computation.4 | loop fusion | flops 6144 | bytes 49152 | tf_op jit(solution)/shard_map/add | solution.py:343
  (12 shorter events, 0.0 us)
Async XLA Ops:
  0.0 8.7 %collective-permute-start = (f32[2,16,150]{2,1,0:T(8,128)}, f32[2,16,150]{2,1,0:T(8,128)S(1)}, u32[]{:S(2)}, u32[]{:S(2)}) collective-permute-start(f32[2,16,150]{2,1,0:T(8,128)} %bitcast.12), channel_id=1, source_target_pairs={{128,0},{132,4},{136,8},{140,12},{144,16},{148,20},{152,24},{156,2... | collective-permute-start | bytes 57608 | tf_op jit(solution)/shard_map/ppermute | solution.py:33
  3.6 5.2 %collective-permute-start.1 = (f32[2,16,150]{2,1,0:T(8,128)}, f32[2,16,150]{2,1,0:T(8,128)S(1)}, u32[]{:S(2)}, u32[]{:S(2)}) collective-permute-start(f32[2,16,150]{2,1,0:T(8,128)} %bitcast.13), channel_id=1, source_target_pairs={{64,0},{68,4},{72,8},{76,12},{80,16},{84,20},{88,24},{92,28},{96,3... | collective-permute-start | bytes 57608 | tf_op jit(solution)/shard_map/ppermute | solution.py:33
  7.2 0.8 %copy-start.3 = (f32[2,150,16]{1,2,0:T(8,128)S(1)}, f32[2,150,16]{1,2,0:T(8,128)}, u32[]{:S(2)}) copy-start(f32[2,150,16]{1,2,0:T(8,128)} %param.7) | copy-start | bytes 57604
  8.8 9.2 %collective-permute-start.4 = (f32[128,128]{1,0:T(8,128)S(1)}, f32[128,128]{1,0:T(8,128)S(1)}, u32[]{:S(2)}, u32[]{:S(2)}) collective-permute-start(f32[128,128]{1,0:T(8,128)S(1)} %shard_map.74.refs_0_), channel_id=1, source_target_pairs={{8,0},{12,4},{16,8},{20,12},{24,16},{28,20},{0,24},{4,28},{40,32},... | collective-permute-start | bytes 196616 | tf_op jit(solution)/shard_map/ppermute | solution.py:33
  14.9 5.9 %collective-permute-start.5 = (f32[128,128]{1,0:T(8,128)S(1)}, f32[128,128]{1,0:T(8,128)S(1)}, u32[]{:S(2)}, u32[]{:S(2)}) collective-permute-start(f32[128,128]{1,0:T(8,128)S(1)} %shard_map.74.refs_0_), channel_id=1, source_target_pairs={{24,0},{28,4},{0,8},{4,12},{8,16},{12,20},{16,24},{20,28},{56,32},... | collective-permute-start | bytes 196616 | tf_op jit(solution)/shard_map/ppermute | solution.py:33
  14.9 7.4 %collective-permute-start.2 = (f32[128,128]{1,0:T(8,128)S(1)}, f32[128,128]{1,0:T(8,128)S(1)}, u32[]{:S(2)}, u32[]{:S(2)}) collective-permute-start(f32[128,128]{1,0:T(8,128)S(1)} %shard_map.74.refs_0_), channel_id=1, source_target_pairs={{4,0},{8,4},{12,8},{16,12},{20,16},{24,20},{28,24},{0,28},{36,32},... | collective-permute-start | bytes 196616 | tf_op jit(solution)/shard_map/ppermute | solution.py:33
  18.0 5.2 %collective-permute-start.3 = (f32[128,128]{1,0:T(8,128)S(1)}, f32[128,128]{1,0:T(8,128)S(1)}, u32[]{:S(2)}, u32[]{:S(2)}) collective-permute-start(f32[128,128]{1,0:T(8,128)S(1)} %shard_map.74.refs_0_), channel_id=1, source_target_pairs={{28,0},{0,4},{4,8},{8,12},{12,16},{16,20},{20,24},{24,28},{60,32},... | collective-permute-start | bytes 196616 | tf_op jit(solution)/shard_map/ppermute | solution.py:33
  18.0 5.2 %collective-permute-start.6 = (f32[128,128]{1,0:T(8,128)S(1)}, f32[128,128]{1,0:T(8,128)S(1)}, u32[]{:S(2)}, u32[]{:S(2)}) collective-permute-start(f32[128,128]{1,0:T(8,128)S(1)} %collective-permute-done.4.refs_3_), channel_id=1, source_target_pairs={{4,0},{8,4},{12,8},{16,12},{20,16},{24,20},{28,24},{0,28},{36,32},... | collective-permute-start | bytes 196616 | tf_op jit(solution)/shard_map/ppermute | solution.py:33
  20.7 4.3 %collective-permute-start.7 = (f32[128,128]{1,0:T(8,128)S(1)}, f32[128,128]{1,0:T(8,128)S(1)}, u32[]{:S(2)}, u32[]{:S(2)}) collective-permute-start(f32[128,128]{1,0:T(8,128)S(1)} %collective-permute-done.4.refs_3_), channel_id=1, source_target_pairs={{8,0},{12,4},{16,8},{20,12},{24,16},{28,20},{0,24},{4,28},{40,32},... | collective-permute-start | bytes 196616 | tf_op jit(solution)/shard_map/ppermute | solution.py:33
  20.8 5.1 %collective-permute-start.8 = (f32[128,128]{1,0:T(8,128)S(1)}, f32[128,128]{1,0:T(8,128)S(1)}, u32[]{:S(2)}, u32[]{:S(2)}) collective-permute-start(f32[128,128]{1,0:T(8,128)S(1)} %collective-permute-done.5.refs_4_), channel_id=1, source_target_pairs={{28,0},{0,4},{4,8},{8,12},{12,16},{16,20},{20,24},{24,28},{60,32},... | collective-permute-start | bytes 196616 | tf_op jit(solution)/shard_map/ppermute | solution.py:33
  26.2 8.3 %collective-permute-start.10 = (f32[2,2,152,128]{3,2,1,0:T(8,128)S(1)}, f32[2,2,152,128]{3,2,1,0:T(8,128)S(1)}, u32[]{:S(2)}, u32[]{:S(2)}) collective-permute-start(f32[2,2,152,128]{3,2,1,0:T(8,128)S(1)} %get-tuple-element.13.after_hbm.refs_1_), channel_id=1, source_target_pairs={{96,0},{100,4},{104,8},{108,12},{112,16},{116,20},{120,24},{124,28... | collective-permute-start | bytes 933896 | tf_op jit(solution)/shard_map/ppermute | solution.py:33
  26.7 7.8 %collective-permute-start.9 = (f32[2,2,152,128]{3,2,1,0:T(8,128)S(1)}, f32[2,2,152,128]{3,2,1,0:T(8,128)S(1)}, u32[]{:S(2)}, u32[]{:S(2)}) collective-permute-start(f32[2,2,152,128]{3,2,1,0:T(8,128)S(1)} %get-tuple-element.13.after_hbm.refs_1_), channel_id=1, source_target_pairs={{32,0},{36,4},{40,8},{44,12},{48,16},{52,20},{56,24},{60,28},{64,3... | collective-permute-start | bytes 933896 | tf_op jit(solution)/shard_map/ppermute | solution.py:33
  28.9 5.6 %collective-permute-start.11 = (f32[2,152,128]{2,1,0:T(8,128)S(1)}, f32[2,152,128]{2,1,0:T(8,128)S(1)}, u32[]{:S(2)}, u32[]{:S(2)}) collective-permute-start(f32[2,152,128]{2,1,0:T(8,128)S(1)} %get-tuple-element.14.refs_4_), channel_id=1, source_target_pairs={{128,0},{132,4},{136,8},{140,12},{144,16},{148,20},{152,24},{156,2... | collective-permute-start | bytes 466952 | tf_op jit(solution)/shard_map/ppermute | solution.py:33
  29.2 5.3 %copy-start = (f32[256,64]{1,0:T(8,128)S(1)}, f32[256,64]{1,0:T(8,128)}, u32[]{:S(2)}) copy-start(f32[256,64]{1,0:T(8,128)} %constant.8.clone.refs_6_) | copy-start | bytes 196612
  29.2 5.3 %copy-start.1 = (f32[2,128,128]{2,1,0:T(8,128)S(1)}, f32[2,128,128]{2,1,0:T(8,128)}, u32[]{:S(2)}) copy-start(f32[2,128,128]{2,1,0:T(8,128)} %constant.9.clone.refs_7_) | copy-start | bytes 393220
  29.2 5.3 %copy-start.2 = (f32[2,96,128]{2,1,0:T(8,128)S(1)}, f32[2,96,128]{2,1,0:T(8,128)}, u32[]{:S(2)}) copy-start(f32[2,96,128]{2,1,0:T(8,128)} %constant.10.clone.refs_8_) | copy-start | bytes 294916
  36.8 5.9 %collective-permute-start.12 = (f32[2,4,768]{2,1,0:T(4,128)S(1)}, f32[2,4,768]{2,1,0:T(4,128)S(1)}, u32[]{:S(2)}, u32[]{:S(2)}) collective-permute-start(f32[2,4,768]{2,1,0:T(4,128)S(1)} %get-tuple-element.16), channel_id=1, source_target_pairs={{0,1},{1,0},{2,3},{3,2},{4,5},{5,4},{6,7},{7,6},{8,9},{9,8},{10,11... | collective-permute-start | bytes 73736 | tf_op jit(solution)/shard_map/ppermute | solution.py:341
  42.8 2.5 %collective-permute-start.13 = (f32[4,768]{1,0:T(4,128)S(1)}, f32[4,768]{1,0:T(4,128)S(1)}, u32[]{:S(2)}, u32[]{:S(2)}) collective-permute-start(f32[4,768]{1,0:T(4,128)S(1)} %fusion), channel_id=1, source_target_pairs={{0,2},{1,3},{2,0},{3,1},{4,6},{5,7},{6,4},{7,5},{8,10},{9,11},{10,... | collective-permute-start | bytes 36872 | tf_op jit(solution)/shard_map/ppermute | solution.py:342

commit v4 on v3

--- a/solution.py
+++ b/solution.py
@@ -28,9 +28,11 @@
     pairs = []
     for i in range(XH * YS * ZS):
         a, b, c = i // (YS * ZS), i // ZS % YS, i % ZS
-        src = (a + dx) % XH * (YS * ZS) + (b + dy) % YS * ZS + (c + dz) % ZS
-        pairs.append((src, i))
-    return lax.ppermute(x, "tmpl", pairs)
+        for chan in range(4):
+            turn = -dz if chan % 2 == 0 else dz
+            src = (a + dx) % XH * (YS * ZS) + (b + dy) % YS * ZS + (c + turn) % ZS
+            pairs.append((src * 4 + chan, i * 4 + chan))
+    return lax.ppermute(x, ("tmpl", "chan"), pairs)
 
 
 def half_turn_fit():
@@ -133,13 +135,17 @@
 REST = CHANS - 128
 HELD = 3
 REST_AT = HELD * 32
-DENSE = REST_AT + 32
+DENSE = REST_AT + 24
 
 
 def put(j, ref, k, out_ref):
     out_ref[16 * j : 16 * j + 16, :] = ref[k, :, 0:128]
-    at = REST_AT + j // 4 * 16
-    out_ref[at : at + 16, 32 * (j % 4) : 32 * (j % 4) + REST] = ref[k, :, 128:CHANS]
+    if j < 4:
+        out_ref[REST_AT : REST_AT + 16, 32 * j : 32 * j + REST] = ref[k, :, 128:CHANS]
+        return
+    for half in range(2):
+        lanes = 64 * half + 32 * k
+        out_ref[DENSE - 8 : DENSE, lanes : lanes + REST] = ref[k, 8 * half : 8 * half + 8, 128:CHANS]
 
 
 def early_kernel(raw_ref, code_ref, own_ref, wide_ref, pair_ref):
@@ -184,11 +190,15 @@
 def pack_kernel(*refs):
     parts, one_ref, far_ref, held = refs[:8], refs[8], refs[9], refs[10]
     z = lax.axis_index("tmpl") % ZS
+    turn = 2 * (lax.axis_index("chan") % 2) - 1
     for part, dz in zip(parts, Z_ORDER):
-        at = pl.multiple_of(lax.rem(z + dz + ZS, ZS) * 16, 16)
-        for j in range(DENSE // 16):
+        at = pl.multiple_of(lax.rem(z + turn * dz + ZS, ZS) * 16, 16)
+        for j in range(REST_AT // 16 + 1):
             held[j, pl.ds(at, 16), :] = part[16 * j : 16 * j + 16, :]
-    rest = [held[j].T for j in range(REST_AT // 16, DENSE // 16)]
+        late = part[DENSE - 8 : DENSE, :]
+        held[REST_AT // 16 + 1, pl.ds(at, 8), :] = late
+        held[REST_AT // 16 + 1, pl.ds(at + 8, 8), :] = pltpu.roll(late, 64, 1)
+    rest = [held[j].T for j in range(REST_AT // 16, REST_AT // 16 + 2)]
     for j in range(2 * HELD):
         out = one_ref.at[j // 2, j % 2] if j < 4 else far_ref.at[j % 2]
         out[0:128, :] = held[j].T
@@ -218,7 +228,7 @@
         ),
         in_specs=[VMEM] * 8,
         out_specs=(VMEM, VMEM),
-        scratch_shapes=[pltpu.VMEM((DENSE // 16, 128, 128), jnp.float32)],
+        scratch_shapes=[pltpu.VMEM((REST_AT // 16 + 2, 128, 128), jnp.float32)],
         compiler_params=PARAMS,
     )(own, up, down, up2, down2, up3, up4, down3)
 
@@ -250,7 +260,8 @@
 
 def network_kernel(*refs):
     spec_ref, (one_ref, up_ref, down_ref, far_ref, other_far_ref) = refs[0], refs[1:6]
-    first_ref, twist_ref, last_ref, keep_ref, send_ref, data_ref, piece_ref = refs[6:]
+    first_ref, twist_ref, last_ref = refs[6:9]
+    out_refs, (data_ref, piece_ref) = refs[9:13], refs[13:]
     me = lax.axis_index("tmpl")
     x, y = me // (YS * ZS), me // ZS % YS
 
@@ -283,12 +294,10 @@
             acc[4 + m] = acc[4 + m] + (tr * d[1] + ti * d[0])
         return tuple(acc)
 
-    acc = lax.fori_loop(0, CHANS, channel, (jnp.zeros((8, 128), jnp.float32),) * 8, unroll=5)
+    acc = lax.fori_loop(0, CHANS, channel, (jnp.zeros((8, 128), jnp.float32),) * 8, unroll=15)
     to_lags(acc, first_ref, twist_ref, last_ref, piece_ref)
-    keep_ref[0] = piece_ref[0]
-    keep_ref[1] = piece_ref[2]
-    send_ref[0] = piece_ref[1]
-    send_ref[1] = piece_ref[3]
+    for j, out_ref in enumerate(out_refs):
+        out_ref[...] = piece_ref[j]
 
 
 def to_lags(acc, first_ref, twist_ref, last_ref, piece_ref):
@@ -316,12 +325,12 @@
 
 def network_part(spectra, blocks):
     lag_dev = LAGS // 4
-    shape = jax.ShapeDtypeStruct((2, TMPL, lag_dev), jnp.float32)
+    shape = jax.ShapeDtypeStruct((TMPL, lag_dev), jnp.float32)
     return pl.pallas_call(
         network_kernel,
-        out_shape=(shape, shape),
+        out_shape=(shape,) * 4,
         in_specs=[VMEM] * 9,
-        out_specs=(VMEM, VMEM),
+        out_specs=(VMEM,) * 4,
         scratch_shapes=[
             pltpu.VMEM((8, 2, ROWS, 128), jnp.float32),
             pltpu.VMEM((4, TMPL, lag_dev), jnp.float32),
@@ -337,10 +346,9 @@
     one, far = gather_xz(dense, from_offset(raw, dx=1), from_offset(raw, dy=2))
     blocks = gather_xy(one, far)
     spectra = template_part(tmpl_spec, wide, one)
-    keep, send = network_part(spectra, blocks)
-    got = lax.ppermute(send, "chan", [(i, i ^ 1) for i in range(4)])
-    other = lax.ppermute(keep[1] + got[1], "chan", [(i, i ^ 2) for i in range(4)])
-    return keep[0] + got[0] + other
+    pieces = network_part(spectra, blocks)
+    got = [lax.ppermute(pieces[j], "chan", [(i, i ^ j) for i in range(4)]) for j in (3, 2, 1)]
+    return pieces[0] + got[2] + (got[1] + got[0])
 
 
 def solution(mesh):

time: 46.1 us -> 45.2 us (0.980)
  waiting for transfers between devices: 7.92 us -> 6.47 us
  starting transfers between devices: 28.4 us -> 29 us
    ppermute x14 -> x15, waiting for transfers between devices: 7.92 us -> 6.47 us  [the longest x12 4.67 us: from_offset(): return lax.ppermute(x, ('tmpl', 'chan'), pairs)]
    ppermute x14 -> x15, starting transfers between devices: 28.4 us -> 29 us  [the longest x12 22.8 us: from_offset(): return lax.ppermute(x, ('tmpl', 'chan'), pairs)]
  transfers between devices with their start and end apart: 14 -> 15, of which waited for: 6 -> 6; matrix products, arithmetic and copies ran while one was open for 2% -> 2% of each run, Pallas kernels for 11% -> 11%
where the time goes in v4:
time: 45.2 us; the launch traced here: 45.1 us
  starting transfers between devices  29 us (64%)
  Pallas kernels  7.41 us (16%)
  waiting for transfers between devices  6.47 us (14%)
  other arithmetic  1.31 us (3%)
  local copies, waits for them, and re-layouts  0.77 us (2%)
    ppermute x12, starting transfers between devices, from_offset(): return lax.ppermute(x, ('tmpl', 'chan'), pairs)  22.8 us
    ppermute x3, starting transfers between devices, on_device(): lax.ppermute(pieces[j], 'chan', [(i, i ^ j) for i in range(4)])  6.22 us
    ppermute x12, waiting for transfers between devices, from_offset(): return lax.ppermute(x, ('tmpl', 'chan'), pairs)  4.67 us
    pallas_call x1, Pallas kernels, template_part(): pl.pallas_call(template_kernel, out_shape=jax.ShapeDtypeStruct((CHANS, 2,...  4.07 us
    pallas_call x1, Pallas kernels, network_part(): pl.pallas_call(network_kernel, out_shape=(shape,) * 4, in_specs=[VMEM] *...  2.18 us
    ppermute x3, waiting for transfers between devices, on_device(): lax.ppermute(pieces[j], 'chan', [(i, i ^ j) for i in range(4)])  1.8 us
  transfers between devices with their start and end apart: 15, of which 6 were waited for; matrix products, arithmetic and copies ran while one was open for 2% of the time, Pallas kernels for 11%

profile of v4, /device:TPU:1, one launch (start us, length us, event | category | flops | bytes accessed | tf_op | source)
XLA Modules:
  0.0 45.1 jit_solution(17948132493262342167)
XLA Ops:
  0.0 3.6 %collective-permute-start = (f32[2,16,150]{2,1,0:T(8,128)}, f32[2,16,150]{2,1,0:T(8,128)S(1)}, u32[]{:S(2)}, u32[]{:S(2)}) collective-permute-start(f32[2,16,150]{2,1,0:T(8,128)} %bitcast.6), channel_id=1, source_target_pairs={{128,0},{129,1},{130,2},{131,3},{132,4},{133,5},{134,6},{135,7},{1... | collective-permute-start | bytes 57608 | tf_op jit(solution)/shard_map/ppermute | solution.py:35
  3.6 2.9 %collective-permute-start.1 = (f32[2,16,150]{2,1,0:T(8,128)}, f32[2,16,150]{2,1,0:T(8,128)S(1)}, u32[]{:S(2)}, u32[]{:S(2)}) collective-permute-start(f32[2,16,150]{2,1,0:T(8,128)} %bitcast.7), channel_id=1, source_target_pairs={{64,0},{65,1},{66,2},{67,3},{68,4},{69,5},{70,6},{71,7},{72,8},{73... | collective-permute-start | bytes 57608 | tf_op jit(solution)/shard_map/ppermute | solution.py:35
  6.5 0.7 %add_convert_fusion.code_ref = f32[4,150]{1,0:T(4,128)S(1)} fusion(s32[4,150]{1,0:T(4,128)} %param.9, s32[4,150]{1,0:T(4,128)} %param.10), kind=kLoop, calls=%fused_computation.1 | loop fusion | flops 1800 | bytes 7200 | tf_op jit(solution)/shard_map/convert_element_type | solution.py:344
  7.2 0.8 %copy-done.3 = f32[2,150,16]{1,2,0:T(8,128)S(1)} copy-done((f32[2,150,16]{1,2,0:T(8,128)S(1)}, f32[2,150,16]{1,2,0:T(8,128)}, u32[]{:S(2)}) %copy-start.3) | copy-done | bytes 19224
  8.0 0.8 %shard_map.73 = (f32[120,128]{1,0:T(8,128)S(1)}, f32[150,3,8,128]{3,2,1,0:T(8,128)S(1)}) custom-call(f32[2,16,150]{2,1,0:T(8,128)S(1)} %bitcast.8, f32[4,150]{1,0:T(4,128)S(1)} %add_convert_fusion.code_ref), custom_call_target="tpu_custom_call" | custom-call | tf_op jit(solution)/shard_map/pallas_call | solution.py:167
  8.7 0.0 collective-permute-done.1.far_ref
  8.8 0.1 shard_map.74.refs_0_
  8.8 6.0 %collective-permute-start.4 = (f32[120,128]{1,0:T(8,128)S(1)}, f32[120,128]{1,0:T(8,128)S(1)}, u32[]{:S(2)}, u32[]{:S(2)}) collective-permute-start(f32[120,128]{1,0:T(8,128)S(1)} %shard_map.74.refs_0_), channel_id=1, source_target_pairs={{24,0},{9,1},{26,2},{11,3},{28,4},{13,5},{30,6},{15,7},{0,8},{17,9... | collective-permute-start | bytes 184328 | tf_op jit(solution)/shard_map/ppermute | solution.py:35
  14.9 3.1 %collective-permute-start.2 = (f32[120,128]{1,0:T(8,128)S(1)}, f32[120,128]{1,0:T(8,128)S(1)}, u32[]{:S(2)}, u32[]{:S(2)}) collective-permute-start(f32[120,128]{1,0:T(8,128)S(1)} %shard_map.74.refs_0_), channel_id=1, source_target_pairs={{28,0},{5,1},{30,2},{7,3},{0,4},{9,5},{2,6},{11,7},{4,8},{13,9},{6... | collective-permute-start | bytes 184328 | tf_op jit(solution)/shard_map/ppermute | solution.py:35
  18.0 0.0 collective-permute-start.3
  18.0 0.0 collective-permute-done.4.refs_3_
  18.0 2.7 %collective-permute-start.6 = (f32[120,128]{1,0:T(8,128)S(1)}, f32[120,128]{1,0:T(8,128)S(1)}, u32[]{:S(2)}, u32[]{:S(2)}) collective-permute-start(f32[120,128]{1,0:T(8,128)S(1)} %collective-permute-done.4.refs_3_), channel_id=1, source_target_pairs={{28,0},{5,1},{30,2},{7,3},{0,4},{9,5},{2,6},{11,7},{4,8},{13,9},{6... | collective-permute-start | bytes 184328 | tf_op jit(solution)/shard_map/ppermute | solution.py:35
  20.7 0.0 collective-permute-start.7
  20.7 0.0 collective-permute-done.5.refs_4_
  20.7 1.5 %collective-permute-start.8 = (f32[120,128]{1,0:T(8,128)S(1)}, f32[120,128]{1,0:T(8,128)S(1)}, u32[]{:S(2)}, u32[]{:S(2)}) collective-permute-start(f32[120,128]{1,0:T(8,128)S(1)} %collective-permute-done.5.refs_4_), channel_id=1, source_target_pairs={{4,0},{29,1},{6,2},{31,3},{8,4},{1,5},{10,6},{3,7},{12,8},{5,9},{1... | collective-permute-start | bytes 184328 | tf_op jit(solution)/shard_map/ppermute | solution.py:35
  22.2 0.0 collective-permute-done.2.refs_1_
  22.2 0.1 collective-permute-done.3.refs_2_
  22.3 2.8 %collective-permute-done.7.refs_6_ = f32[120,128]{1,0:T(8,128)S(1)} collective-permute-done((f32[120,128]{1,0:T(8,128)S(1)}, f32[120,128]{1,0:T(8,128)S(1)}, u32[]{:S(2)}, u32[]{:S(2)}) %collective-permute-start.7) | collective-permute-done | bytes 61472 | tf_op jit(solution)/shard_map/ppermute | solution.py:35
  25.1 0.5 %collective-permute-done.8.refs_7_ = f32[120,128]{1,0:T(8,128)S(1)} collective-permute-done((f32[120,128]{1,0:T(8,128)S(1)}, f32[120,128]{1,0:T(8,128)S(1)}, u32[]{:S(2)}, u32[]{:S(2)}) %collective-permute-start.8) | collective-permute-done | bytes 61472 | tf_op jit(solution)/shard_map/ppermute | solution.py:35
  25.6 0.3 shard_map.75
  25.9 0.7 %collective-permute-start.10 = (f32[2,2,152,128]{3,2,1,0:T(8,128)S(1)}, f32[2,2,152,128]{3,2,1,0:T(8,128)S(1)}, u32[]{:S(2)}, u32[]{:S(2)}) collective-permute-start(f32[2,2,152,128]{3,2,1,0:T(8,128)S(1)} %get-tuple-element.15.after_hbm.refs_1_), channel_id=1, source_target_pairs={{96,0},{97,1},{98,2},{99,3},{100,4},{101,5},{102,6},{103,7},{104,8... | collective-permute-start | bytes 933896 | tf_op jit(solution)/shard_map/ppermute | solution.py:35
  26.6 2.0 %collective-permute-start.9 = (f32[2,2,152,128]{3,2,1,0:T(8,128)S(1)}, f32[2,2,152,128]{3,2,1,0:T(8,128)S(1)}, u32[]{:S(2)}, u32[]{:S(2)}) collective-permute-start(f32[2,2,152,128]{3,2,1,0:T(8,128)S(1)} %get-tuple-element.15.after_hbm.refs_1_), channel_id=1, source_target_pairs={{32,0},{33,1},{34,2},{35,3},{36,4},{37,5},{38,6},{39,7},{40,8},{41... | collective-permute-start | bytes 933896 | tf_op jit(solution)/shard_map/ppermute | solution.py:35
  28.6 0.2 collective-permute-start.11
  28.9 4.1 %shard_map.76.refs_0_ = f32[150,2,4,8,128]{4,3,2,1,0:T(8,128)S(1)} custom-call(f32[2,150,4,8,128]{4,3,2,1,0:T(8,128)} %bitcast.9, f32[150,3,8,128]{3,2,1,0:T(8,128)S(1)} %get-tuple-element.13.wide_ref, f32[2,2,152,128]{3,2,1,0:T(8,128)S(1)} %get-tuple-element.15.after_hbm.refs_1_), custom_call_target="tpu_custom_call" | custom-call | tf_op jit(solution)/shard_map/pallas_call | solution.py:121
  32.9 1.3 %collective-permute-done.11.refs_5_ = f32[2,152,128]{2,1,0:T(8,128)S(1)} collective-permute-done((f32[2,152,128]{2,1,0:T(8,128)S(1)}, f32[2,152,128]{2,1,0:T(8,128)S(1)}, u32[]{:S(2)}, u32[]{:S(2)}) %collective-permute-start.11) | collective-permute-done | bytes 155680 | tf_op jit(solution)/shard_map/ppermute | solution.py:35
  34.3 2.2 %shard_map.77 = (f32[4,768]{1,0:T(4,128)S(1)}, f32[4,768]{1,0:T(4,128)S(1)}, f32[4,768]{1,0:T(4,128)S(1)}, f32[4,768]{1,0:T(4,128)S(1)}) custom-call(f32[150,2,4,8,128]{4,3,2,1,0:T(8,128)S(1)} %shard_map.76.refs_0_, f32[2,2,152,128]{3,2,1,0:T(8,128)S(1)} %get-tuple-element.15.after_hbm.refs_1_, f32[2,2,152,128]{3,2,1,0:T(8,128)S(1)} %collective-permute-done.9.refs_2_, ...), custom_call_target="tpu_custom_call" | custom-call | tf_op jit(solution)/shard_map/pallas_call | solution.py:329
  36.4 4.5 %collective-permute-start.12 = (f32[4,768]{1,0:T(4,128)S(1)}, f32[4,768]{1,0:T(4,128)S(1)}, u32[]{:S(2)}, u32[]{:S(2)}) collective-permute-start(f32[4,768]{1,0:T(4,128)S(1)} %get-tuple-element.18), channel_id=1, source_target_pairs={{0,1},{1,0},{2,3},{3,2},{4,5},{5,4},{6,7},{7,6},{8,9},{9,8},{10,11... | collective-permute-start | bytes 36872 | tf_op jit(solution)/shard_map/ppermute | solution.py:350
  40.9 0.3 collective-permute-start.13
  41.3 1.4 %collective-permute-start.14 = (f32[4,768]{1,0:T(4,128)S(1)}, f32[4,768]{1,0:T(4,128)S(1)}, u32[]{:S(2)}, u32[]{:S(2)}) collective-permute-start(f32[4,768]{1,0:T(4,128)S(1)} %get-tuple-element.20), channel_id=1, source_target_pairs={{0,3},{1,2},{2,1},{3,0},{4,7},{5,6},{6,5},{7,4},{8,11},{9,10},{10,... | collective-permute-start | bytes 36872 | tf_op jit(solution)/shard_map/ppermute | solution.py:350
  42.7 0.8 %collective-permute-done.13 = f32[4,768]{1,0:T(4,128)S(1)} collective-permute-done((f32[4,768]{1,0:T(4,128)S(1)}, f32[4,768]{1,0:T(4,128)S(1)}, u32[]{:S(2)}, u32[]{:S(2)}) %collective-permute-start.13) | collective-permute-done | bytes 12320 | tf_op jit(solution)/shard_map/ppermute | solution.py:350
  43.5 1.0 %collective-permute-done.14 = f32[4,768]{1,0:T(4,128)S(1)} collective-permute-done((f32[4,768]{1,0:T(4,128)S(1)}, f32[4,768]{1,0:T(4,128)S(1)}, u32[]{:S(2)}, u32[]{:S(2)}) %collective-permute-start.14) | collective-permute-done | bytes 12320 | tf_op jit(solution)/shard_map/ppermute | solution.py:350
  44.5 0.6 %add_add_fusion = f32[4,768]{1,0:T(4,128)} fusion(f32[4,768]{1,0:T(4,128)S(1)} %collective-permute-done.13, f32[4,768]{1,0:T(4,128)S(1)} %collective-permute-done.14, f32[4,768]{1,0:T(4,128)S(1)} %get-tuple-element.17, f32[4,768]{1,0:T(4,128)S(1)} %collective-permute-done.12), kind=kLoop, calls=%fused_computation | loop fusion | flops 9216 | bytes 61440 | tf_op jit(solution)/shard_map/add | solution.py:351
  (13 shorter events, 0.0 us)
Async XLA Ops:
  0.0 8.7 %collective-permute-start = (f32[2,16,150]{2,1,0:T(8,128)}, f32[2,16,150]{2,1,0:T(8,128)S(1)}, u32[]{:S(2)}, u32[]{:S(2)}) collective-permute-start(f32[2,16,150]{2,1,0:T(8,128)} %bitcast.6), channel_id=1, source_target_pairs={{128,0},{129,1},{130,2},{131,3},{132,4},{133,5},{134,6},{135,7},{1... | collective-permute-start | bytes 57608 | tf_op jit(solution)/shard_map/ppermute | solution.py:35
  3.6 5.2 %collective-permute-start.1 = (f32[2,16,150]{2,1,0:T(8,128)}, f32[2,16,150]{2,1,0:T(8,128)S(1)}, u32[]{:S(2)}, u32[]{:S(2)}) collective-permute-start(f32[2,16,150]{2,1,0:T(8,128)} %bitcast.7), channel_id=1, source_target_pairs={{64,0},{65,1},{66,2},{67,3},{68,4},{69,5},{70,6},{71,7},{72,8},{73... | collective-permute-start | bytes 57608 | tf_op jit(solution)/shard_map/ppermute | solution.py:35
  7.2 0.8 %copy-start.3 = (f32[2,150,16]{1,2,0:T(8,128)S(1)}, f32[2,150,16]{1,2,0:T(8,128)}, u32[]{:S(2)}) copy-start(f32[2,150,16]{1,2,0:T(8,128)} %param.7) | copy-start | bytes 57604
  8.8 9.2 %collective-permute-start.4 = (f32[120,128]{1,0:T(8,128)S(1)}, f32[120,128]{1,0:T(8,128)S(1)}, u32[]{:S(2)}, u32[]{:S(2)}) collective-permute-start(f32[120,128]{1,0:T(8,128)S(1)} %shard_map.74.refs_0_), channel_id=1, source_target_pairs={{24,0},{9,1},{26,2},{11,3},{28,4},{13,5},{30,6},{15,7},{0,8},{17,9... | collective-permute-start | bytes 184328 | tf_op jit(solution)/shard_map/ppermute | solution.py:35
  14.9 5.8 %collective-permute-start.5 = (f32[120,128]{1,0:T(8,128)S(1)}, f32[120,128]{1,0:T(8,128)S(1)}, u32[]{:S(2)}, u32[]{:S(2)}) collective-permute-start(f32[120,128]{1,0:T(8,128)S(1)} %shard_map.74.refs_0_), channel_id=1, source_target_pairs={{8,0},{25,1},{10,2},{27,3},{12,4},{29,5},{14,6},{31,7},{16,8},{1,9... | collective-permute-start | bytes 184328 | tf_op jit(solution)/shard_map/ppermute | solution.py:35
  14.9 7.3 %collective-permute-start.2 = (f32[120,128]{1,0:T(8,128)S(1)}, f32[120,128]{1,0:T(8,128)S(1)}, u32[]{:S(2)}, u32[]{:S(2)}) collective-permute-start(f32[120,128]{1,0:T(8,128)S(1)} %shard_map.74.refs_0_), channel_id=1, source_target_pairs={{28,0},{5,1},{30,2},{7,3},{0,4},{9,5},{2,6},{11,7},{4,8},{13,9},{6... | collective-permute-start | bytes 184328 | tf_op jit(solution)/shard_map/ppermute | solution.py:35
  18.0 4.3 %collective-permute-start.3 = (f32[120,128]{1,0:T(8,128)S(1)}, f32[120,128]{1,0:T(8,128)S(1)}, u32[]{:S(2)}, u32[]{:S(2)}) collective-permute-start(f32[120,128]{1,0:T(8,128)S(1)} %shard_map.74.refs_0_), channel_id=1, source_target_pairs={{4,0},{29,1},{6,2},{31,3},{8,4},{1,5},{10,6},{3,7},{12,8},{5,9},{1... | collective-permute-start | bytes 184328 | tf_op jit(solution)/shard_map/ppermute | solution.py:35
  18.0 4.3 %collective-permute-start.6 = (f32[120,128]{1,0:T(8,128)S(1)}, f32[120,128]{1,0:T(8,128)S(1)}, u32[]{:S(2)}, u32[]{:S(2)}) collective-permute-start(f32[120,128]{1,0:T(8,128)S(1)} %collective-permute-done.4.refs_3_), channel_id=1, source_target_pairs={{28,0},{5,1},{30,2},{7,3},{0,4},{9,5},{2,6},{11,7},{4,8},{13,9},{6... | collective-permute-start | bytes 184328 | tf_op jit(solution)/shard_map/ppermute | solution.py:35
  20.7 4.4 %collective-permute-start.7 = (f32[120,128]{1,0:T(8,128)S(1)}, f32[120,128]{1,0:T(8,128)S(1)}, u32[]{:S(2)}, u32[]{:S(2)}) collective-permute-start(f32[120,128]{1,0:T(8,128)S(1)} %collective-permute-done.4.refs_3_), channel_id=1, source_target_pairs={{24,0},{9,1},{26,2},{11,3},{28,4},{13,5},{30,6},{15,7},{0,8},{17,9... | collective-permute-start | bytes 184328 | tf_op jit(solution)/shard_map/ppermute | solution.py:35
  20.7 4.8 %collective-permute-start.8 = (f32[120,128]{1,0:T(8,128)S(1)}, f32[120,128]{1,0:T(8,128)S(1)}, u32[]{:S(2)}, u32[]{:S(2)}) collective-permute-start(f32[120,128]{1,0:T(8,128)S(1)} %collective-permute-done.5.refs_4_), channel_id=1, source_target_pairs={{4,0},{29,1},{6,2},{31,3},{8,4},{1,5},{10,6},{3,7},{12,8},{5,9},{1... | collective-permute-start | bytes 184328 | tf_op jit(solution)/shard_map/ppermute | solution.py:35
  25.9 8.3 %collective-permute-start.10 = (f32[2,2,152,128]{3,2,1,0:T(8,128)S(1)}, f32[2,2,152,128]{3,2,1,0:T(8,128)S(1)}, u32[]{:S(2)}, u32[]{:S(2)}) collective-permute-start(f32[2,2,152,128]{3,2,1,0:T(8,128)S(1)} %get-tuple-element.15.after_hbm.refs_1_), channel_id=1, source_target_pairs={{96,0},{97,1},{98,2},{99,3},{100,4},{101,5},{102,6},{103,7},{104,8... | collective-permute-start | bytes 933896 | tf_op jit(solution)/shard_map/ppermute | solution.py:35
  26.6 7.6 %collective-permute-start.9 = (f32[2,2,152,128]{3,2,1,0:T(8,128)S(1)}, f32[2,2,152,128]{3,2,1,0:T(8,128)S(1)}, u32[]{:S(2)}, u32[]{:S(2)}) collective-permute-start(f32[2,2,152,128]{3,2,1,0:T(8,128)S(1)} %get-tuple-element.15.after_hbm.refs_1_), channel_id=1, source_target_pairs={{32,0},{33,1},{34,2},{35,3},{36,4},{37,5},{38,6},{39,7},{40,8},{41... | collective-permute-start | bytes 933896 | tf_op jit(solution)/shard_map/ppermute | solution.py:35
  28.6 5.6 %collective-permute-start.11 = (f32[2,152,128]{2,1,0:T(8,128)S(1)}, f32[2,152,128]{2,1,0:T(8,128)S(1)}, u32[]{:S(2)}, u32[]{:S(2)}) collective-permute-start(f32[2,152,128]{2,1,0:T(8,128)S(1)} %get-tuple-element.16.refs_4_), channel_id=1, source_target_pairs={{128,0},{129,1},{130,2},{131,3},{132,4},{133,5},{134,6},{135,7},{1... | collective-permute-start | bytes 466952 | tf_op jit(solution)/shard_map/ppermute | solution.py:35
  28.9 5.4 %copy-start = (f32[256,64]{1,0:T(8,128)S(1)}, f32[256,64]{1,0:T(8,128)}, u32[]{:S(2)}) copy-start(f32[256,64]{1,0:T(8,128)} %constant.8.clone.refs_6_) | copy-start | bytes 196612
  28.9 5.4 %copy-start.1 = (f32[2,128,128]{2,1,0:T(8,128)S(1)}, f32[2,128,128]{2,1,0:T(8,128)}, u32[]{:S(2)}) copy-start(f32[2,128,128]{2,1,0:T(8,128)} %constant.9.clone.refs_7_) | copy-start | bytes 393220
  28.9 5.4 %copy-start.2 = (f32[2,96,128]{2,1,0:T(8,128)S(1)}, f32[2,96,128]{2,1,0:T(8,128)}, u32[]{:S(2)}) copy-start(f32[2,96,128]{2,1,0:T(8,128)} %constant.10.clone.refs_8_) | copy-start | bytes 294916
  36.4 6.2 %collective-permute-start.12 = (f32[4,768]{1,0:T(4,128)S(1)}, f32[4,768]{1,0:T(4,128)S(1)}, u32[]{:S(2)}, u32[]{:S(2)}) collective-permute-start(f32[4,768]{1,0:T(4,128)S(1)} %get-tuple-element.18), channel_id=1, source_target_pairs={{0,1},{1,0},{2,3},{3,2},{4,5},{5,4},{6,7},{7,6},{8,9},{9,8},{10,11... | collective-permute-start | bytes 36872 | tf_op jit(solution)/shard_map/ppermute | solution.py:350
  40.9 2.6 %collective-permute-start.13 = (f32[4,768]{1,0:T(4,128)S(1)}, f32[4,768]{1,0:T(4,128)S(1)}, u32[]{:S(2)}, u32[]{:S(2)}) collective-permute-start(f32[4,768]{1,0:T(4,128)S(1)} %get-tuple-element.19), channel_id=1, source_target_pairs={{0,2},{1,3},{2,0},{3,1},{4,6},{5,7},{6,4},{7,5},{8,10},{9,11},{10,... | collective-permute-start | bytes 36872 | tf_op jit(solution)/shard_map/ppermute | solution.py:350
  41.3 3.2 %collective-permute-start.14 = (f32[4,768]{1,0:T(4,128)S(1)}, f32[4,768]{1,0:T(4,128)S(1)}, u32[]{:S(2)}, u32[]{:S(2)}) collective-permute-start(f32[4,768]{1,0:T(4,128)S(1)} %get-tuple-element.20), channel_id=1, source_target_pairs={{0,3},{1,2},{2,1},{3,0},{4,7},{5,6},{6,5},{7,4},{8,11},{9,10},{10,... | collective-permute-start | bytes 36872 | tf_op jit(solution)/shard_map/ppermute | solution.py:350

commit v5 on v4

--- a/solution.py
+++ b/solution.py
@@ -19,7 +19,7 @@
 XH, YS, ZS = 2, 4, 8
 
 VMEM = pl.BlockSpec(memory_space=pltpu.VMEM)
-HIGH = lax.Precision.HIGHEST
+HIGH = lax.Precision.HIGH
 PARAMS = pltpu.CompilerParams(vmem_limit_bytes=16 << 20)
 LARGE = pltpu.CompilerParams(vmem_limit_bytes=45 << 20)
 
@@ -184,7 +184,7 @@
         put(4 + k, far_ref, k, out_ref)
 
 
-Z_ORDER = (0, 1, -1, 2, -2, 3, 4, -3)
+Z_ORDER = (0, -1, 1, 2, -2, 3, 4, -3)
 
 
 def pack_kernel(*refs):
@@ -230,7 +230,7 @@
         out_specs=(VMEM, VMEM),
         scratch_shapes=[pltpu.VMEM((REST_AT // 16 + 2, 128, 128), jnp.float32)],
         compiler_params=PARAMS,
-    )(own, up, down, up2, down2, up3, up4, down3)
+    )(own, down, up, up2, down2, up3, up4, down3)
 
 
 def gather_xy(one, far):

time: 45.2 us -> 44.7 us (0.989)
  transfers between devices with their start and end apart: 15 -> 15, of which waited for: 6 -> 5; matrix products, arithmetic and copies ran while one was open for 2% -> 2% of each run, Pallas kernels for 11% -> 11%
where the time goes in v5:
time: 44.7 us; the launch traced here: 44.5 us
  starting transfers between devices  28.8 us (64%)
  Pallas kernels  7.13 us (16%)
  waiting for transfers between devices  6.38 us (14%)
  other arithmetic  1.31 us (3%)
  local copies, waits for them, and re-layouts  0.77 us (2%)
    ppermute x12, starting transfers between devices, from_offset(): return lax.ppermute(x, ('tmpl', 'chan'), pairs)  22.8 us
    ppermute x3, starting transfers between devices, on_device(): lax.ppermute(pieces[j], 'chan', [(i, i ^ j) for i in range(4)])  6.02 us
    ppermute x12, waiting for transfers between devices, from_offset(): return lax.ppermute(x, ('tmpl', 'chan'), pairs)  4.58 us
    pallas_call x1, Pallas kernels, template_part(): pl.pallas_call(template_kernel, out_shape=jax.ShapeDtypeStruct((CHANS, 2,...  4.07 us
    pallas_call x1, Pallas kernels, network_part(): pl.pallas_call(network_kernel, out_shape=(shape,) * 4, in_specs=[VMEM] *...  1.91 us
    ppermute x3, waiting for transfers between devices, on_device(): lax.ppermute(pieces[j], 'chan', [(i, i ^ j) for i in range(4)])  1.8 us
  transfers between devices with their start and end apart: 15, of which 5 were waited for; matrix products, arithmetic and copies ran while one was open for 2% of the time, Pallas kernels for 11%

profile of v5, /device:TPU:1, one launch (start us, length us, event | category | flops | bytes accessed | tf_op | source)
XLA Modules:
  0.0 44.5 jit_solution(8301626582014207097)
XLA Ops:
  0.0 3.6 %collective-permute-start = (f32[2,16,150]{2,1,0:T(8,128)}, f32[2,16,150]{2,1,0:T(8,128)S(1)}, u32[]{:S(2)}, u32[]{:S(2)}) collective-permute-start(f32[2,16,150]{2,1,0:T(8,128)} %bitcast.6), channel_id=1, source_target_pairs={{128,0},{129,1},{130,2},{131,3},{132,4},{133,5},{134,6},{135,7},{1... | collective-permute-start | bytes 57608 | tf_op jit(solution)/shard_map/ppermute | solution.py:35
  3.6 2.9 %collective-permute-start.1 = (f32[2,16,150]{2,1,0:T(8,128)}, f32[2,16,150]{2,1,0:T(8,128)S(1)}, u32[]{:S(2)}, u32[]{:S(2)}) collective-permute-start(f32[2,16,150]{2,1,0:T(8,128)} %bitcast.7), channel_id=1, source_target_pairs={{64,0},{65,1},{66,2},{67,3},{68,4},{69,5},{70,6},{71,7},{72,8},{73... | collective-permute-start | bytes 57608 | tf_op jit(solution)/shard_map/ppermute | solution.py:35
  6.5 0.7 %add_convert_fusion.code_ref = f32[4,150]{1,0:T(4,128)S(1)} fusion(s32[4,150]{1,0:T(4,128)} %param.9, s32[4,150]{1,0:T(4,128)} %param.10), kind=kLoop, calls=%fused_computation.1 | loop fusion | flops 1800 | bytes 7200 | tf_op jit(solution)/shard_map/convert_element_type | solution.py:344
  7.2 0.8 %copy-done.3 = f32[2,150,16]{1,2,0:T(8,128)S(1)} copy-done((f32[2,150,16]{1,2,0:T(8,128)S(1)}, f32[2,150,16]{1,2,0:T(8,128)}, u32[]{:S(2)}) %copy-start.3) | copy-done | bytes 19224
  8.0 0.8 %shard_map.73 = (f32[120,128]{1,0:T(8,128)S(1)}, f32[150,3,8,128]{3,2,1,0:T(8,128)S(1)}) custom-call(f32[2,16,150]{2,1,0:T(8,128)S(1)} %bitcast.8, f32[4,150]{1,0:T(4,128)S(1)} %add_convert_fusion.code_ref), custom_call_target="tpu_custom_call" | custom-call | tf_op jit(solution)/shard_map/pallas_call | solution.py:167
  8.7 0.0 collective-permute-done.other_ref
  8.8 0.1 shard_map.74.refs_0_
  8.8 6.0 %collective-permute-start.4 = (f32[120,128]{1,0:T(8,128)S(1)}, f32[120,128]{1,0:T(8,128)S(1)}, u32[]{:S(2)}, u32[]{:S(2)}) collective-permute-start(f32[120,128]{1,0:T(8,128)S(1)} %shard_map.74.refs_0_), channel_id=1, source_target_pairs={{24,0},{9,1},{26,2},{11,3},{28,4},{13,5},{30,6},{15,7},{0,8},{17,9... | collective-permute-start | bytes 184328 | tf_op jit(solution)/shard_map/ppermute | solution.py:35
  14.9 0.7 %collective-permute-start.2 = (f32[120,128]{1,0:T(8,128)S(1)}, f32[120,128]{1,0:T(8,128)S(1)}, u32[]{:S(2)}, u32[]{:S(2)}) collective-permute-start(f32[120,128]{1,0:T(8,128)S(1)} %shard_map.74.refs_0_), channel_id=1, source_target_pairs={{4,0},{29,1},{6,2},{31,3},{8,4},{1,5},{10,6},{3,7},{12,8},{5,9},{1... | collective-permute-start | bytes 184328 | tf_op jit(solution)/shard_map/ppermute | solution.py:35
  15.6 2.4 %collective-permute-start.3 = (f32[120,128]{1,0:T(8,128)S(1)}, f32[120,128]{1,0:T(8,128)S(1)}, u32[]{:S(2)}, u32[]{:S(2)}) collective-permute-start(f32[120,128]{1,0:T(8,128)S(1)} %shard_map.74.refs_0_), channel_id=1, source_target_pairs={{28,0},{5,1},{30,2},{7,3},{0,4},{9,5},{2,6},{11,7},{4,8},{13,9},{6... | collective-permute-start | bytes 184328 | tf_op jit(solution)/shard_map/ppermute | solution.py:35
  18.0 1.7 %collective-permute-start.6 = (f32[120,128]{1,0:T(8,128)S(1)}, f32[120,128]{1,0:T(8,128)S(1)}, u32[]{:S(2)}, u32[]{:S(2)}) collective-permute-start(f32[120,128]{1,0:T(8,128)S(1)} %collective-permute-done.4.refs_3_), channel_id=1, source_target_pairs={{28,0},{5,1},{30,2},{7,3},{0,4},{9,5},{2,6},{11,7},{4,8},{13,9},{6... | collective-permute-start | bytes 184328 | tf_op jit(solution)/shard_map/ppermute | solution.py:35
  19.7 1.0 %collective-permute-start.7 = (f32[120,128]{1,0:T(8,128)S(1)}, f32[120,128]{1,0:T(8,128)S(1)}, u32[]{:S(2)}, u32[]{:S(2)}) collective-permute-start(f32[120,128]{1,0:T(8,128)S(1)} %collective-permute-done.4.refs_3_), channel_id=1, source_target_pairs={{24,0},{9,1},{26,2},{11,3},{28,4},{13,5},{30,6},{15,7},{0,8},{17,9... | collective-permute-start | bytes 184328 | tf_op jit(solution)/shard_map/ppermute | solution.py:35
  20.7 0.0 collective-permute-done.5.refs_4_
  20.7 1.5 %collective-permute-start.8 = (f32[120,128]{1,0:T(8,128)S(1)}, f32[120,128]{1,0:T(8,128)S(1)}, u32[]{:S(2)}, u32[]{:S(2)}) collective-permute-start(f32[120,128]{1,0:T(8,128)S(1)} %collective-permute-done.5.refs_4_), channel_id=1, source_target_pairs={{4,0},{29,1},{6,2},{31,3},{8,4},{1,5},{10,6},{3,7},{12,8},{5,9},{1... | collective-permute-start | bytes 184328 | tf_op jit(solution)/shard_map/ppermute | solution.py:35
  22.2 0.0 collective-permute-done.2.refs_1_
  22.2 0.0 collective-permute-done.3.refs_2_
  22.2 0.0 collective-permute-done.6.refs_5_
  22.2 2.2 %collective-permute-done.7.refs_6_ = f32[120,128]{1,0:T(8,128)S(1)} collective-permute-done((f32[120,128]{1,0:T(8,128)S(1)}, f32[120,128]{1,0:T(8,128)S(1)}, u32[]{:S(2)}, u32[]{:S(2)}) %collective-permute-start.7) | collective-permute-done | bytes 61472 | tf_op jit(solution)/shard_map/ppermute | solution.py:35
  24.4 1.1 %collective-permute-done.8.refs_7_ = f32[120,128]{1,0:T(8,128)S(1)} collective-permute-done((f32[120,128]{1,0:T(8,128)S(1)}, f32[120,128]{1,0:T(8,128)S(1)}, u32[]{:S(2)}, u32[]{:S(2)}) %collective-permute-start.8) | collective-permute-done | bytes 61472 | tf_op jit(solution)/shard_map/ppermute | solution.py:35
  25.5 0.3 shard_map.75
  25.8 1.1 %collective-permute-start.10 = (f32[2,2,152,128]{3,2,1,0:T(8,128)S(1)}, f32[2,2,152,128]{3,2,1,0:T(8,128)S(1)}, u32[]{:S(2)}, u32[]{:S(2)}) collective-permute-start(f32[2,2,152,128]{3,2,1,0:T(8,128)S(1)} %get-tuple-element.15.after_hbm.refs_1_), channel_id=1, source_target_pairs={{96,0},{97,1},{98,2},{99,3},{100,4},{101,5},{102,6},{103,7},{104,8... | collective-permute-start | bytes 933896 | tf_op jit(solution)/shard_map/ppermute | solution.py:35
  26.9 1.7 %collective-permute-start.9 = (f32[2,2,152,128]{3,2,1,0:T(8,128)S(1)}, f32[2,2,152,128]{3,2,1,0:T(8,128)S(1)}, u32[]{:S(2)}, u32[]{:S(2)}) collective-permute-start(f32[2,2,152,128]{3,2,1,0:T(8,128)S(1)} %get-tuple-element.15.after_hbm.refs_1_), channel_id=1, source_target_pairs={{32,0},{33,1},{34,2},{35,3},{36,4},{37,5},{38,6},{39,7},{40,8},{41... | collective-permute-start | bytes 933896 | tf_op jit(solution)/shard_map/ppermute | solution.py:35
  28.5 0.2 collective-permute-start.11
  28.8 4.1 %shard_map.76.refs_0_ = f32[150,2,4,8,128]{4,3,2,1,0:T(8,128)S(1)} custom-call(f32[2,150,4,8,128]{4,3,2,1,0:T(8,128)} %bitcast.9, f32[150,3,8,128]{3,2,1,0:T(8,128)S(1)} %get-tuple-element.13.wide_ref, f32[2,2,152,128]{3,2,1,0:T(8,128)S(1)} %get-tuple-element.15.after_hbm.refs_1_), custom_call_target="tpu_custom_call" | custom-call | tf_op jit(solution)/shard_map/pallas_call | solution.py:121
  32.9 1.3 %collective-permute-done.11.refs_5_ = f32[2,152,128]{2,1,0:T(8,128)S(1)} collective-permute-done((f32[2,152,128]{2,1,0:T(8,128)S(1)}, f32[2,152,128]{2,1,0:T(8,128)S(1)}, u32[]{:S(2)}, u32[]{:S(2)}) %collective-permute-start.11) | collective-permute-done | bytes 155680 | tf_op jit(solution)/shard_map/ppermute | solution.py:35
  34.2 1.9 %shard_map.77 = (f32[4,768]{1,0:T(4,128)S(1)}, f32[4,768]{1,0:T(4,128)S(1)}, f32[4,768]{1,0:T(4,128)S(1)}, f32[4,768]{1,0:T(4,128)S(1)}) custom-call(f32[150,2,4,8,128]{4,3,2,1,0:T(8,128)S(1)} %shard_map.76.refs_0_, f32[2,2,152,128]{3,2,1,0:T(8,128)S(1)} %get-tuple-element.15.after_hbm.refs_1_, f32[2,2,152,128]{3,2,1,0:T(8,128)S(1)} %collective-permute-done.9.refs_2_, ...), custom_call_target="tpu_custom_call" | custom-call | tf_op jit(solution)/shard_map/pallas_call | solution.py:329
  36.1 4.3 %collective-permute-start.12 = (f32[4,768]{1,0:T(4,128)S(1)}, f32[4,768]{1,0:T(4,128)S(1)}, u32[]{:S(2)}, u32[]{:S(2)}) collective-permute-start(f32[4,768]{1,0:T(4,128)S(1)} %get-tuple-element.18), channel_id=1, source_target_pairs={{0,1},{1,0},{2,3},{3,2},{4,5},{5,4},{6,7},{7,6},{8,9},{9,8},{10,11... | collective-permute-start | bytes 36872 | tf_op jit(solution)/shard_map/ppermute | solution.py:350
  40.4 0.3 collective-permute-start.13
  40.7 1.4 %collective-permute-start.14 = (f32[4,768]{1,0:T(4,128)S(1)}, f32[4,768]{1,0:T(4,128)S(1)}, u32[]{:S(2)}, u32[]{:S(2)}) collective-permute-start(f32[4,768]{1,0:T(4,128)S(1)} %get-tuple-element.20), channel_id=1, source_target_pairs={{0,3},{1,2},{2,1},{3,0},{4,7},{5,6},{6,5},{7,4},{8,11},{9,10},{10,... | collective-permute-start | bytes 36872 | tf_op jit(solution)/shard_map/ppermute | solution.py:350
  42.1 0.8 %collective-permute-done.13 = f32[4,768]{1,0:T(4,128)S(1)} collective-permute-done((f32[4,768]{1,0:T(4,128)S(1)}, f32[4,768]{1,0:T(4,128)S(1)}, u32[]{:S(2)}, u32[]{:S(2)}) %collective-permute-start.13) | collective-permute-done | bytes 12320 | tf_op jit(solution)/shard_map/ppermute | solution.py:350
  42.9 1.0 %collective-permute-done.14 = f32[4,768]{1,0:T(4,128)S(1)} collective-permute-done((f32[4,768]{1,0:T(4,128)S(1)}, f32[4,768]{1,0:T(4,128)S(1)}, u32[]{:S(2)}, u32[]{:S(2)}) %collective-permute-start.14) | collective-permute-done | bytes 12320 | tf_op jit(solution)/shard_map/ppermute | solution.py:350
  43.9 0.6 %add_add_fusion = f32[4,768]{1,0:T(4,128)} fusion(f32[4,768]{1,0:T(4,128)S(1)} %collective-permute-done.13, f32[4,768]{1,0:T(4,128)S(1)} %collective-permute-done.14, f32[4,768]{1,0:T(4,128)S(1)} %get-tuple-element.17, f32[4,768]{1,0:T(4,128)S(1)} %collective-permute-done.12), kind=kLoop, calls=%fused_computation | loop fusion | flops 9216 | bytes 61440 | tf_op jit(solution)/shard_map/add | solution.py:351
  (13 shorter events, 0.0 us)
Async XLA Ops:
  0.0 8.7 %collective-permute-start = (f32[2,16,150]{2,1,0:T(8,128)}, f32[2,16,150]{2,1,0:T(8,128)S(1)}, u32[]{:S(2)}, u32[]{:S(2)}) collective-permute-start(f32[2,16,150]{2,1,0:T(8,128)} %bitcast.6), channel_id=1, source_target_pairs={{128,0},{129,1},{130,2},{131,3},{132,4},{133,5},{134,6},{135,7},{1... | collective-permute-start | bytes 57608 | tf_op jit(solution)/shard_map/ppermute | solution.py:35
  3.6 5.2 %collective-permute-start.1 = (f32[2,16,150]{2,1,0:T(8,128)}, f32[2,16,150]{2,1,0:T(8,128)S(1)}, u32[]{:S(2)}, u32[]{:S(2)}) collective-permute-start(f32[2,16,150]{2,1,0:T(8,128)} %bitcast.7), channel_id=1, source_target_pairs={{64,0},{65,1},{66,2},{67,3},{68,4},{69,5},{70,6},{71,7},{72,8},{73... | collective-permute-start | bytes 57608 | tf_op jit(solution)/shard_map/ppermute | solution.py:35
  7.2 0.8 %copy-start.3 = (f32[2,150,16]{1,2,0:T(8,128)S(1)}, f32[2,150,16]{1,2,0:T(8,128)}, u32[]{:S(2)}) copy-start(f32[2,150,16]{1,2,0:T(8,128)} %param.7) | copy-start | bytes 57604
  8.8 9.2 %collective-permute-start.4 = (f32[120,128]{1,0:T(8,128)S(1)}, f32[120,128]{1,0:T(8,128)S(1)}, u32[]{:S(2)}, u32[]{:S(2)}) collective-permute-start(f32[120,128]{1,0:T(8,128)S(1)} %shard_map.74.refs_0_), channel_id=1, source_target_pairs={{24,0},{9,1},{26,2},{11,3},{28,4},{13,5},{30,6},{15,7},{0,8},{17,9... | collective-permute-start | bytes 184328 | tf_op jit(solution)/shard_map/ppermute | solution.py:35
  14.9 5.8 %collective-permute-start.5 = (f32[120,128]{1,0:T(8,128)S(1)}, f32[120,128]{1,0:T(8,128)S(1)}, u32[]{:S(2)}, u32[]{:S(2)}) collective-permute-start(f32[120,128]{1,0:T(8,128)S(1)} %shard_map.74.refs_0_), channel_id=1, source_target_pairs={{8,0},{25,1},{10,2},{27,3},{12,4},{29,5},{14,6},{31,7},{16,8},{1,9... | collective-permute-start | bytes 184328 | tf_op jit(solution)/shard_map/ppermute | solution.py:35
  14.9 7.3 %collective-permute-start.2 = (f32[120,128]{1,0:T(8,128)S(1)}, f32[120,128]{1,0:T(8,128)S(1)}, u32[]{:S(2)}, u32[]{:S(2)}) collective-permute-start(f32[120,128]{1,0:T(8,128)S(1)} %shard_map.74.refs_0_), channel_id=1, source_target_pairs={{4,0},{29,1},{6,2},{31,3},{8,4},{1,5},{10,6},{3,7},{12,8},{5,9},{1... | collective-permute-start | bytes 184328 | tf_op jit(solution)/shard_map/ppermute | solution.py:35
  15.6 6.6 %collective-permute-start.3 = (f32[120,128]{1,0:T(8,128)S(1)}, f32[120,128]{1,0:T(8,128)S(1)}, u32[]{:S(2)}, u32[]{:S(2)}) collective-permute-start(f32[120,128]{1,0:T(8,128)S(1)} %shard_map.74.refs_0_), channel_id=1, source_target_pairs={{28,0},{5,1},{30,2},{7,3},{0,4},{9,5},{2,6},{11,7},{4,8},{13,9},{6... | collective-permute-start | bytes 184328 | tf_op jit(solution)/shard_map/ppermute | solution.py:35
  18.0 4.2 %collective-permute-start.6 = (f32[120,128]{1,0:T(8,128)S(1)}, f32[120,128]{1,0:T(8,128)S(1)}, u32[]{:S(2)}, u32[]{:S(2)}) collective-permute-start(f32[120,128]{1,0:T(8,128)S(1)} %collective-permute-done.4.refs_3_), channel_id=1, source_target_pairs={{28,0},{5,1},{30,2},{7,3},{0,4},{9,5},{2,6},{11,7},{4,8},{13,9},{6... | collective-permute-start | bytes 184328 | tf_op jit(solution)/shard_map/ppermute | solution.py:35
  19.7 4.6 %collective-permute-start.7 = (f32[120,128]{1,0:T(8,128)S(1)}, f32[120,128]{1,0:T(8,128)S(1)}, u32[]{:S(2)}, u32[]{:S(2)}) collective-permute-start(f32[120,128]{1,0:T(8,128)S(1)} %collective-permute-done.4.refs_3_), channel_id=1, source_target_pairs={{24,0},{9,1},{26,2},{11,3},{28,4},{13,5},{30,6},{15,7},{0,8},{17,9... | collective-permute-start | bytes 184328 | tf_op jit(solution)/shard_map/ppermute | solution.py:35
  20.7 4.8 %collective-permute-start.8 = (f32[120,128]{1,0:T(8,128)S(1)}, f32[120,128]{1,0:T(8,128)S(1)}, u32[]{:S(2)}, u32[]{:S(2)}) collective-permute-start(f32[120,128]{1,0:T(8,128)S(1)} %collective-permute-done.5.refs_4_), channel_id=1, source_target_pairs={{4,0},{29,1},{6,2},{31,3},{8,4},{1,5},{10,6},{3,7},{12,8},{5,9},{1... | collective-permute-start | bytes 184328 | tf_op jit(solution)/shard_map/ppermute | solution.py:35
  25.8 8.3 %collective-permute-start.10 = (f32[2,2,152,128]{3,2,1,0:T(8,128)S(1)}, f32[2,2,152,128]{3,2,1,0:T(8,128)S(1)}, u32[]{:S(2)}, u32[]{:S(2)}) collective-permute-start(f32[2,2,152,128]{3,2,1,0:T(8,128)S(1)} %get-tuple-element.15.after_hbm.refs_1_), channel_id=1, source_target_pairs={{96,0},{97,1},{98,2},{99,3},{100,4},{101,5},{102,6},{103,7},{104,8... | collective-permute-start | bytes 933896 | tf_op jit(solution)/shard_map/ppermute | solution.py:35
  26.9 7.3 %collective-permute-start.9 = (f32[2,2,152,128]{3,2,1,0:T(8,128)S(1)}, f32[2,2,152,128]{3,2,1,0:T(8,128)S(1)}, u32[]{:S(2)}, u32[]{:S(2)}) collective-permute-start(f32[2,2,152,128]{3,2,1,0:T(8,128)S(1)} %get-tuple-element.15.after_hbm.refs_1_), channel_id=1, source_target_pairs={{32,0},{33,1},{34,2},{35,3},{36,4},{37,5},{38,6},{39,7},{40,8},{41... | collective-permute-start | bytes 933896 | tf_op jit(solution)/shard_map/ppermute | solution.py:35
  28.5 5.6 %collective-permute-start.11 = (f32[2,152,128]{2,1,0:T(8,128)S(1)}, f32[2,152,128]{2,1,0:T(8,128)S(1)}, u32[]{:S(2)}, u32[]{:S(2)}) collective-permute-start(f32[2,152,128]{2,1,0:T(8,128)S(1)} %get-tuple-element.16.refs_4_), channel_id=1, source_target_pairs={{128,0},{129,1},{130,2},{131,3},{132,4},{133,5},{134,6},{135,7},{1... | collective-permute-start | bytes 466952 | tf_op jit(solution)/shard_map/ppermute | solution.py:35
  28.8 5.4 %copy-start = (f32[256,64]{1,0:T(8,128)S(1)}, f32[256,64]{1,0:T(8,128)}, u32[]{:S(2)}) copy-start(f32[256,64]{1,0:T(8,128)} %constant.8.clone.refs_6_) | copy-start | bytes 196612
  28.8 5.4 %copy-start.1 = (f32[2,128,128]{2,1,0:T(8,128)S(1)}, f32[2,128,128]{2,1,0:T(8,128)}, u32[]{:S(2)}) copy-start(f32[2,128,128]{2,1,0:T(8,128)} %constant.9.clone.refs_7_) | copy-start | bytes 393220
  28.8 5.4 %copy-start.2 = (f32[2,96,128]{2,1,0:T(8,128)S(1)}, f32[2,96,128]{2,1,0:T(8,128)}, u32[]{:S(2)}) copy-start(f32[2,96,128]{2,1,0:T(8,128)} %constant.10.clone.refs_8_) | copy-start | bytes 294916
  36.1 6.0 %collective-permute-start.12 = (f32[4,768]{1,0:T(4,128)S(1)}, f32[4,768]{1,0:T(4,128)S(1)}, u32[]{:S(2)}, u32[]{:S(2)}) collective-permute-start(f32[4,768]{1,0:T(4,128)S(1)} %get-tuple-element.18), channel_id=1, source_target_pairs={{0,1},{1,0},{2,3},{3,2},{4,5},{5,4},{6,7},{7,6},{8,9},{9,8},{10,11... | collective-permute-start | bytes 36872 | tf_op jit(solution)/shard_map/ppermute | solution.py:350
  40.4 2.6 %collective-permute-start.13 = (f32[4,768]{1,0:T(4,128)S(1)}, f32[4,768]{1,0:T(4,128)S(1)}, u32[]{:S(2)}, u32[]{:S(2)}) collective-permute-start(f32[4,768]{1,0:T(4,128)S(1)} %get-tuple-element.19), channel_id=1, source_target_pairs={{0,2},{1,3},{2,0},{3,1},{4,6},{5,7},{6,4},{7,5},{8,10},{9,11},{10,... | collective-permute-start | bytes 36872 | tf_op jit(solution)/shard_map/ppermute | solution.py:350
  40.7 3.2 %collective-permute-start.14 = (f32[4,768]{1,0:T(4,128)S(1)}, f32[4,768]{1,0:T(4,128)S(1)}, u32[]{:S(2)}, u32[]{:S(2)}) collective-permute-start(f32[4,768]{1,0:T(4,128)S(1)} %get-tuple-element.20), channel_id=1, source_target_pairs={{0,3},{1,2},{2,1},{3,0},{4,7},{5,6},{6,5},{7,4},{8,11},{9,10},{10,... | collective-permute-start | bytes 36872 | tf_op jit(solution)/shard_map/ppermute | solution.py:350

commit v6 on v5

--- a/solution.py
+++ b/solution.py
@@ -29,7 +29,7 @@
     for i in range(XH * YS * ZS):
         a, b, c = i // (YS * ZS), i // ZS % YS, i % ZS
         for chan in range(4):
-            turn = -dz if chan % 2 == 0 else dz
+            turn = -dz
             src = (a + dx) % XH * (YS * ZS) + (b + dy) % YS * ZS + (c + turn) % ZS
             pairs.append((src * 4 + chan, i * 4 + chan))
     return lax.ppermute(x, ("tmpl", "chan"), pairs)
@@ -190,7 +190,7 @@
 def pack_kernel(*refs):
     parts, one_ref, far_ref, held = refs[:8], refs[8], refs[9], refs[10]
     z = lax.axis_index("tmpl") % ZS
-    turn = 2 * (lax.axis_index("chan") % 2) - 1
+    turn = -1
     for part, dz in zip(parts, Z_ORDER):
         at = pl.multiple_of(lax.rem(z + turn * dz + ZS, ZS) * 16, 16)
         for j in range(REST_AT // 16 + 1):
@@ -347,8 +347,8 @@
     blocks = gather_xy(one, far)
     spectra = template_part(tmpl_spec, wide, one)
     pieces = network_part(spectra, blocks)
-    got = [lax.ppermute(pieces[j], "chan", [(i, i ^ j) for i in range(4)]) for j in (3, 2, 1)]
-    return pieces[0] + got[2] + (got[1] + got[0])
+    got = [lax.ppermute(pieces[j], "chan", [(i, i ^ j) for i in range(4)]) for j in (1, 2, 3)]
+    return pieces[0] + got[0] + (got[1] + got[2])
 
 
 def solution(mesh):

time: 44.7 us -> 44.1 us (0.987)
  starting transfers between devices: 28.8 us -> 27.8 us
    ppermute x12, starting transfers between devices: 22.8 us -> 21.2 us  [from_offset(): return lax.ppermute(x, ('tmpl', 'chan'), pairs)]
    ppermute x3, starting transfers between devices: 6.02 us -> 6.66 us  [on_device(): lax.ppermute(pieces[j], 'chan', [(i, i ^ j) for i in range(4)])]
  transfers between devices with their start and end apart: 15 -> 15, of which waited for: 5 -> 6; matrix products, arithmetic and copies ran while one was open for 2% -> 2% of each run, Pallas kernels for 11% -> 11%
where the time goes in v6:
time: 44.1 us; the launch traced here: 43.9 us
  starting transfers between devices  27.8 us (63%)
  Pallas kernels  7.13 us (16%)
  waiting for transfers between devices  6.78 us (15%)
  other arithmetic  1.31 us (3%)
  local copies, waits for them, and re-layouts  0.77 us (2%)
    ppermute x12, starting transfers between devices, from_offset(): return lax.ppermute(x, ('tmpl', 'chan'), pairs)  21.2 us
    ppermute x3, starting transfers between devices, on_device(): lax.ppermute(pieces[j], 'chan', [(i, i ^ j) for i in range(4)])  6.66 us
    ppermute x12, waiting for transfers between devices, from_offset(): return lax.ppermute(x, ('tmpl', 'chan'), pairs)  4.98 us
    pallas_call x1, Pallas kernels, template_part(): pl.pallas_call(template_kernel, out_shape=jax.ShapeDtypeStruct((CHANS, 2,...  4.07 us
    pallas_call x1, Pallas kernels, network_part(): pl.pallas_call(network_kernel, out_shape=(shape,) * 4, in_specs=[VMEM] *...  1.91 us
    ppermute x3, waiting for transfers between devices, on_device(): lax.ppermute(pieces[j], 'chan', [(i, i ^ j) for i in range(4)])  1.8 us
  transfers between devices with their start and end apart: 15, of which 6 were waited for; matrix products, arithmetic and copies ran while one was open for 2% of the time, Pallas kernels for 11%

profile of v6, /device:TPU:1, one launch (start us, length us, event | category | flops | bytes accessed | tf_op | source)
XLA Modules:
  0.0 43.9 jit_solution(8621497692623620918)
XLA Ops:
  0.0 3.6 %collective-permute-start = (f32[2,16,150]{2,1,0:T(8,128)}, f32[2,16,150]{2,1,0:T(8,128)S(1)}, u32[]{:S(2)}, u32[]{:S(2)}) collective-permute-start(f32[2,16,150]{2,1,0:T(8,128)} %bitcast.6), channel_id=1, source_target_pairs={{128,0},{129,1},{130,2},{131,3},{132,4},{133,5},{134,6},{135,7},{1... | collective-permute-start | bytes 57608 | tf_op jit(solution)/shard_map/ppermute | solution.py:35
  3.6 2.9 %collective-permute-start.1 = (f32[2,16,150]{2,1,0:T(8,128)}, f32[2,16,150]{2,1,0:T(8,128)S(1)}, u32[]{:S(2)}, u32[]{:S(2)}) collective-permute-start(f32[2,16,150]{2,1,0:T(8,128)} %bitcast.7), channel_id=1, source_target_pairs={{64,0},{65,1},{66,2},{67,3},{68,4},{69,5},{70,6},{71,7},{72,8},{73... | collective-permute-start | bytes 57608 | tf_op jit(solution)/shard_map/ppermute | solution.py:35
  6.5 0.7 %add_convert_fusion.code_ref = f32[4,150]{1,0:T(4,128)S(1)} fusion(s32[4,150]{1,0:T(4,128)} %param.9, s32[4,150]{1,0:T(4,128)} %param.10), kind=kLoop, calls=%fused_computation.1 | loop fusion | flops 1800 | bytes 7200 | tf_op jit(solution)/shard_map/convert_element_type | solution.py:344
  7.2 0.8 %copy-done.3 = f32[2,150,16]{1,2,0:T(8,128)S(1)} copy-done((f32[2,150,16]{1,2,0:T(8,128)S(1)}, f32[2,150,16]{1,2,0:T(8,128)}, u32[]{:S(2)}) %copy-start.3) | copy-done | bytes 19224
  8.0 0.8 %shard_map.73 = (f32[120,128]{1,0:T(8,128)S(1)}, f32[150,3,8,128]{3,2,1,0:T(8,128)S(1)}) custom-call(f32[2,16,150]{2,1,0:T(8,128)S(1)} %bitcast.8, f32[4,150]{1,0:T(4,128)S(1)} %add_convert_fusion.code_ref), custom_call_target="tpu_custom_call" | custom-call | tf_op jit(solution)/shard_map/pallas_call | solution.py:167
  8.7 0.0 collective-permute-done.1.far_ref
  8.8 0.1 shard_map.74.refs_0_
  8.8 3.0 %collective-permute-start.4 = (f32[120,128]{1,0:T(8,128)S(1)}, f32[120,128]{1,0:T(8,128)S(1)}, u32[]{:S(2)}, u32[]{:S(2)}) collective-permute-start(f32[120,128]{1,0:T(8,128)S(1)} %shard_map.74.refs_0_), channel_id=1, source_target_pairs={{24,0},{25,1},{26,2},{27,3},{28,4},{29,5},{30,6},{31,7},{0,8},{1,9... | collective-permute-start | bytes 184328 | tf_op jit(solution)/shard_map/ppermute | solution.py:35
  11.8 3.1 %collective-permute-start.5 = (f32[120,128]{1,0:T(8,128)S(1)}, f32[120,128]{1,0:T(8,128)S(1)}, u32[]{:S(2)}, u32[]{:S(2)}) collective-permute-start(f32[120,128]{1,0:T(8,128)S(1)} %shard_map.74.refs_0_), channel_id=1, source_target_pairs={{8,0},{9,1},{10,2},{11,3},{12,4},{13,5},{14,6},{15,7},{16,8},{17,9... | collective-permute-start | bytes 184328 | tf_op jit(solution)/shard_map/ppermute | solution.py:35
  15.0 1.8 %collective-permute-start.2 = (f32[120,128]{1,0:T(8,128)S(1)}, f32[120,128]{1,0:T(8,128)S(1)}, u32[]{:S(2)}, u32[]{:S(2)}) collective-permute-start(f32[120,128]{1,0:T(8,128)S(1)} %shard_map.74.refs_0_), channel_id=1, source_target_pairs={{4,0},{5,1},{6,2},{7,3},{8,4},{9,5},{10,6},{11,7},{12,8},{13,9},{1... | collective-permute-start | bytes 184328 | tf_op jit(solution)/shard_map/ppermute | solution.py:35
  16.8 1.1 %collective-permute-start.6 = (f32[120,128]{1,0:T(8,128)S(1)}, f32[120,128]{1,0:T(8,128)S(1)}, u32[]{:S(2)}, u32[]{:S(2)}) collective-permute-start(f32[120,128]{1,0:T(8,128)S(1)} %collective-permute-done.4.refs_3_), channel_id=1, source_target_pairs={{28,0},{29,1},{30,2},{31,3},{0,4},{1,5},{2,6},{3,7},{4,8},{5,9},{6... | collective-permute-start | bytes 184328 | tf_op jit(solution)/shard_map/ppermute | solution.py:35
  17.9 2.0 %collective-permute-start.7 = (f32[120,128]{1,0:T(8,128)S(1)}, f32[120,128]{1,0:T(8,128)S(1)}, u32[]{:S(2)}, u32[]{:S(2)}) collective-permute-start(f32[120,128]{1,0:T(8,128)S(1)} %collective-permute-done.4.refs_3_), channel_id=1, source_target_pairs={{24,0},{25,1},{26,2},{27,3},{28,4},{29,5},{30,6},{31,7},{0,8},{1,9... | collective-permute-start | bytes 184328 | tf_op jit(solution)/shard_map/ppermute | solution.py:35
  19.9 0.6 %collective-permute-start.8 = (f32[120,128]{1,0:T(8,128)S(1)}, f32[120,128]{1,0:T(8,128)S(1)}, u32[]{:S(2)}, u32[]{:S(2)}) collective-permute-start(f32[120,128]{1,0:T(8,128)S(1)} %collective-permute-done.5.refs_4_), channel_id=1, source_target_pairs={{4,0},{5,1},{6,2},{7,3},{8,4},{9,5},{10,6},{11,7},{12,8},{13,9},{1... | collective-permute-start | bytes 184328 | tf_op jit(solution)/shard_map/ppermute | solution.py:35
  20.6 0.5 %collective-permute-done.3.refs_2_ = f32[120,128]{1,0:T(8,128)S(1)} collective-permute-done((f32[120,128]{1,0:T(8,128)S(1)}, f32[120,128]{1,0:T(8,128)S(1)}, u32[]{:S(2)}, u32[]{:S(2)}) %collective-permute-start.3) | collective-permute-done | bytes 61472 | tf_op jit(solution)/shard_map/ppermute | solution.py:35
  21.1 0.7 %collective-permute-done.6.refs_5_ = f32[120,128]{1,0:T(8,128)S(1)} collective-permute-done((f32[120,128]{1,0:T(8,128)S(1)}, f32[120,128]{1,0:T(8,128)S(1)}, u32[]{:S(2)}, u32[]{:S(2)}) %collective-permute-start.6) | collective-permute-done | bytes 61472 | tf_op jit(solution)/shard_map/ppermute | solution.py:35
  21.7 2.5 %collective-permute-done.7.refs_6_ = f32[120,128]{1,0:T(8,128)S(1)} collective-permute-done((f32[120,128]{1,0:T(8,128)S(1)}, f32[120,128]{1,0:T(8,128)S(1)}, u32[]{:S(2)}, u32[]{:S(2)}) %collective-permute-start.7) | collective-permute-done | bytes 61472 | tf_op jit(solution)/shard_map/ppermute | solution.py:35
  24.2 0.0 collective-permute-done.8.refs_7_
  24.3 0.3 shard_map.75
  24.6 0.3 collective-permute-start.10
  24.8 2.5 %collective-permute-start.9 = (f32[2,2,152,128]{3,2,1,0:T(8,128)S(1)}, f32[2,2,152,128]{3,2,1,0:T(8,128)S(1)}, u32[]{:S(2)}, u32[]{:S(2)}) collective-permute-start(f32[2,2,152,128]{3,2,1,0:T(8,128)S(1)} %get-tuple-element.15.after_hbm.refs_1_), channel_id=1, source_target_pairs={{32,0},{33,1},{34,2},{35,3},{36,4},{37,5},{38,6},{39,7},{40,8},{41... | collective-permute-start | bytes 933896 | tf_op jit(solution)/shard_map/ppermute | solution.py:35
  27.3 0.2 collective-permute-start.11
  27.5 4.1 %shard_map.76.refs_0_ = f32[150,2,4,8,128]{4,3,2,1,0:T(8,128)S(1)} custom-call(f32[2,150,4,8,128]{4,3,2,1,0:T(8,128)} %bitcast.9, f32[150,3,8,128]{3,2,1,0:T(8,128)S(1)} %get-tuple-element.13.wide_ref, f32[2,2,152,128]{3,2,1,0:T(8,128)S(1)} %get-tuple-element.15.after_hbm.refs_1_), custom_call_target="tpu_custom_call" | custom-call | tf_op jit(solution)/shard_map/pallas_call | solution.py:121
  31.6 1.3 %collective-permute-done.11.refs_5_ = f32[2,152,128]{2,1,0:T(8,128)S(1)} collective-permute-done((f32[2,152,128]{2,1,0:T(8,128)S(1)}, f32[2,152,128]{2,1,0:T(8,128)S(1)}, u32[]{:S(2)}, u32[]{:S(2)}) %collective-permute-start.11) | collective-permute-done | bytes 155680 | tf_op jit(solution)/shard_map/ppermute | solution.py:35
  32.9 0.0 collective-permute-done.10.refs_3_
  32.9 0.0 collective-permute-done.9.refs_2_
  32.9 1.9 %shard_map.77 = (f32[4,768]{1,0:T(4,128)S(1)}, f32[4,768]{1,0:T(4,128)S(1)}, f32[4,768]{1,0:T(4,128)S(1)}, f32[4,768]{1,0:T(4,128)S(1)}) custom-call(f32[150,2,4,8,128]{4,3,2,1,0:T(8,128)S(1)} %shard_map.76.refs_0_, f32[2,2,152,128]{3,2,1,0:T(8,128)S(1)} %get-tuple-element.15.after_hbm.refs_1_, f32[2,2,152,128]{3,2,1,0:T(8,128)S(1)} %collective-permute-done.9.refs_2_, ...), custom_call_target="tpu_custom_call" | custom-call | tf_op jit(solution)/shard_map/pallas_call | solution.py:329
  34.8 4.9 %collective-permute-start.12 = (f32[4,768]{1,0:T(4,128)S(1)}, f32[4,768]{1,0:T(4,128)S(1)}, u32[]{:S(2)}, u32[]{:S(2)}) collective-permute-start(f32[4,768]{1,0:T(4,128)S(1)} %get-tuple-element.18), channel_id=1, source_target_pairs={{0,1},{1,0},{2,3},{3,2},{4,5},{5,4},{6,7},{7,6},{8,9},{9,8},{10,11... | collective-permute-start | bytes 36872 | tf_op jit(solution)/shard_map/ppermute | solution.py:350
  39.8 0.3 collective-permute-start.13
  40.1 1.4 %collective-permute-start.14 = (f32[4,768]{1,0:T(4,128)S(1)}, f32[4,768]{1,0:T(4,128)S(1)}, u32[]{:S(2)}, u32[]{:S(2)}) collective-permute-start(f32[4,768]{1,0:T(4,128)S(1)} %get-tuple-element.20), channel_id=1, source_target_pairs={{0,3},{1,2},{2,1},{3,0},{4,7},{5,6},{6,5},{7,4},{8,11},{9,10},{10,... | collective-permute-start | bytes 36872 | tf_op jit(solution)/shard_map/ppermute | solution.py:350
  41.5 0.8 %collective-permute-done.13 = f32[4,768]{1,0:T(4,128)S(1)} collective-permute-done((f32[4,768]{1,0:T(4,128)S(1)}, f32[4,768]{1,0:T(4,128)S(1)}, u32[]{:S(2)}, u32[]{:S(2)}) %collective-permute-start.13) | collective-permute-done | bytes 12320 | tf_op jit(solution)/shard_map/ppermute | solution.py:350
  42.3 1.0 %collective-permute-done.14 = f32[4,768]{1,0:T(4,128)S(1)} collective-permute-done((f32[4,768]{1,0:T(4,128)S(1)}, f32[4,768]{1,0:T(4,128)S(1)}, u32[]{:S(2)}, u32[]{:S(2)}) %collective-permute-start.14) | collective-permute-done | bytes 12320 | tf_op jit(solution)/shard_map/ppermute | solution.py:350
  43.3 0.6 %add_add_fusion = f32[4,768]{1,0:T(4,128)} fusion(f32[4,768]{1,0:T(4,128)S(1)} %collective-permute-done.13, f32[4,768]{1,0:T(4,128)S(1)} %collective-permute-done.14, f32[4,768]{1,0:T(4,128)S(1)} %get-tuple-element.17, f32[4,768]{1,0:T(4,128)S(1)} %collective-permute-done.12), kind=kLoop, calls=%fused_computation | loop fusion | flops 9216 | bytes 61440 | tf_op jit(solution)/shard_map/add | solution.py:351
  (13 shorter events, 0.0 us)
Async XLA Ops:
  0.0 8.7 %collective-permute-start = (f32[2,16,150]{2,1,0:T(8,128)}, f32[2,16,150]{2,1,0:T(8,128)S(1)}, u32[]{:S(2)}, u32[]{:S(2)}) collective-permute-start(f32[2,16,150]{2,1,0:T(8,128)} %bitcast.6), channel_id=1, source_target_pairs={{128,0},{129,1},{130,2},{131,3},{132,4},{133,5},{134,6},{135,7},{1... | collective-permute-start | bytes 57608 | tf_op jit(solution)/shard_map/ppermute | solution.py:35
  3.6 5.2 %collective-permute-start.1 = (f32[2,16,150]{2,1,0:T(8,128)}, f32[2,16,150]{2,1,0:T(8,128)S(1)}, u32[]{:S(2)}, u32[]{:S(2)}) collective-permute-start(f32[2,16,150]{2,1,0:T(8,128)} %bitcast.7), channel_id=1, source_target_pairs={{64,0},{65,1},{66,2},{67,3},{68,4},{69,5},{70,6},{71,7},{72,8},{73... | collective-permute-start | bytes 57608 | tf_op jit(solution)/shard_map/ppermute | solution.py:35
  7.2 0.8 %copy-start.3 = (f32[2,150,16]{1,2,0:T(8,128)S(1)}, f32[2,150,16]{1,2,0:T(8,128)}, u32[]{:S(2)}) copy-start(f32[2,150,16]{1,2,0:T(8,128)} %param.7) | copy-start | bytes 57604
  8.8 8.0 %collective-permute-start.4 = (f32[120,128]{1,0:T(8,128)S(1)}, f32[120,128]{1,0:T(8,128)S(1)}, u32[]{:S(2)}, u32[]{:S(2)}) collective-permute-start(f32[120,128]{1,0:T(8,128)S(1)} %shard_map.74.refs_0_), channel_id=1, source_target_pairs={{24,0},{25,1},{26,2},{27,3},{28,4},{29,5},{30,6},{31,7},{0,8},{1,9... | collective-permute-start | bytes 184328 | tf_op jit(solution)/shard_map/ppermute | solution.py:35
  11.8 8.1 %collective-permute-start.5 = (f32[120,128]{1,0:T(8,128)S(1)}, f32[120,128]{1,0:T(8,128)S(1)}, u32[]{:S(2)}, u32[]{:S(2)}) collective-permute-start(f32[120,128]{1,0:T(8,128)S(1)} %shard_map.74.refs_0_), channel_id=1, source_target_pairs={{8,0},{9,1},{10,2},{11,3},{12,4},{13,5},{14,6},{15,7},{16,8},{17,9... | collective-permute-start | bytes 184328 | tf_op jit(solution)/shard_map/ppermute | solution.py:35
  15.0 5.6 %collective-permute-start.2 = (f32[120,128]{1,0:T(8,128)S(1)}, f32[120,128]{1,0:T(8,128)S(1)}, u32[]{:S(2)}, u32[]{:S(2)}) collective-permute-start(f32[120,128]{1,0:T(8,128)S(1)} %shard_map.74.refs_0_), channel_id=1, source_target_pairs={{4,0},{5,1},{6,2},{7,3},{8,4},{9,5},{10,6},{11,7},{12,8},{13,9},{1... | collective-permute-start | bytes 184328 | tf_op jit(solution)/shard_map/ppermute | solution.py:35
  16.8 4.3 %collective-permute-start.3 = (f32[120,128]{1,0:T(8,128)S(1)}, f32[120,128]{1,0:T(8,128)S(1)}, u32[]{:S(2)}, u32[]{:S(2)}) collective-permute-start(f32[120,128]{1,0:T(8,128)S(1)} %shard_map.74.refs_0_), channel_id=1, source_target_pairs={{28,0},{29,1},{30,2},{31,3},{0,4},{1,5},{2,6},{3,7},{4,8},{5,9},{6... | collective-permute-start | bytes 184328 | tf_op jit(solution)/shard_map/ppermute | solution.py:35
  16.8 4.9 %collective-permute-start.6 = (f32[120,128]{1,0:T(8,128)S(1)}, f32[120,128]{1,0:T(8,128)S(1)}, u32[]{:S(2)}, u32[]{:S(2)}) collective-permute-start(f32[120,128]{1,0:T(8,128)S(1)} %collective-permute-done.4.refs_3_), channel_id=1, source_target_pairs={{28,0},{29,1},{30,2},{31,3},{0,4},{1,5},{2,6},{3,7},{4,8},{5,9},{6... | collective-permute-start | bytes 184328 | tf_op jit(solution)/shard_map/ppermute | solution.py:35
  17.9 6.4 %collective-permute-start.7 = (f32[120,128]{1,0:T(8,128)S(1)}, f32[120,128]{1,0:T(8,128)S(1)}, u32[]{:S(2)}, u32[]{:S(2)}) collective-permute-start(f32[120,128]{1,0:T(8,128)S(1)} %collective-permute-done.4.refs_3_), channel_id=1, source_target_pairs={{24,0},{25,1},{26,2},{27,3},{28,4},{29,5},{30,6},{31,7},{0,8},{1,9... | collective-permute-start | bytes 184328 | tf_op jit(solution)/shard_map/ppermute | solution.py:35
  19.9 4.3 %collective-permute-start.8 = (f32[120,128]{1,0:T(8,128)S(1)}, f32[120,128]{1,0:T(8,128)S(1)}, u32[]{:S(2)}, u32[]{:S(2)}) collective-permute-start(f32[120,128]{1,0:T(8,128)S(1)} %collective-permute-done.5.refs_4_), channel_id=1, source_target_pairs={{4,0},{5,1},{6,2},{7,3},{8,4},{9,5},{10,6},{11,7},{12,8},{13,9},{1... | collective-permute-start | bytes 184328 | tf_op jit(solution)/shard_map/ppermute | solution.py:35
  24.6 8.3 %collective-permute-start.10 = (f32[2,2,152,128]{3,2,1,0:T(8,128)S(1)}, f32[2,2,152,128]{3,2,1,0:T(8,128)S(1)}, u32[]{:S(2)}, u32[]{:S(2)}) collective-permute-start(f32[2,2,152,128]{3,2,1,0:T(8,128)S(1)} %get-tuple-element.15.after_hbm.refs_1_), channel_id=1, source_target_pairs={{96,0},{97,1},{98,2},{99,3},{100,4},{101,5},{102,6},{103,7},{104,8... | collective-permute-start | bytes 933896 | tf_op jit(solution)/shard_map/ppermute | solution.py:35
  24.8 8.1 %collective-permute-start.9 = (f32[2,2,152,128]{3,2,1,0:T(8,128)S(1)}, f32[2,2,152,128]{3,2,1,0:T(8,128)S(1)}, u32[]{:S(2)}, u32[]{:S(2)}) collective-permute-start(f32[2,2,152,128]{3,2,1,0:T(8,128)S(1)} %get-tuple-element.15.after_hbm.refs_1_), channel_id=1, source_target_pairs={{32,0},{33,1},{34,2},{35,3},{36,4},{37,5},{38,6},{39,7},{40,8},{41... | collective-permute-start | bytes 933896 | tf_op jit(solution)/shard_map/ppermute | solution.py:35
  27.3 5.6 %collective-permute-start.11 = (f32[2,152,128]{2,1,0:T(8,128)S(1)}, f32[2,152,128]{2,1,0:T(8,128)S(1)}, u32[]{:S(2)}, u32[]{:S(2)}) collective-permute-start(f32[2,152,128]{2,1,0:T(8,128)S(1)} %get-tuple-element.16.refs_4_), channel_id=1, source_target_pairs={{128,0},{129,1},{130,2},{131,3},{132,4},{133,5},{134,6},{135,7},{1... | collective-permute-start | bytes 466952 | tf_op jit(solution)/shard_map/ppermute | solution.py:35
  27.5 5.4 %copy-start = (f32[256,64]{1,0:T(8,128)S(1)}, f32[256,64]{1,0:T(8,128)}, u32[]{:S(2)}) copy-start(f32[256,64]{1,0:T(8,128)} %constant.8.clone.refs_6_) | copy-start | bytes 196612
  27.5 5.4 %copy-start.1 = (f32[2,128,128]{2,1,0:T(8,128)S(1)}, f32[2,128,128]{2,1,0:T(8,128)}, u32[]{:S(2)}) copy-start(f32[2,128,128]{2,1,0:T(8,128)} %constant.9.clone.refs_7_) | copy-start | bytes 393220
  27.5 5.4 %copy-start.2 = (f32[2,96,128]{2,1,0:T(8,128)S(1)}, f32[2,96,128]{2,1,0:T(8,128)}, u32[]{:S(2)}) copy-start(f32[2,96,128]{2,1,0:T(8,128)} %constant.10.clone.refs_8_) | copy-start | bytes 294916
  34.8 6.7 %collective-permute-start.12 = (f32[4,768]{1,0:T(4,128)S(1)}, f32[4,768]{1,0:T(4,128)S(1)}, u32[]{:S(2)}, u32[]{:S(2)}) collective-permute-start(f32[4,768]{1,0:T(4,128)S(1)} %get-tuple-element.18), channel_id=1, source_target_pairs={{0,1},{1,0},{2,3},{3,2},{4,5},{5,4},{6,7},{7,6},{8,9},{9,8},{10,11... | collective-permute-start | bytes 36872 | tf_op jit(solution)/shard_map/ppermute | solution.py:350
  39.8 2.6 %collective-permute-start.13 = (f32[4,768]{1,0:T(4,128)S(1)}, f32[4,768]{1,0:T(4,128)S(1)}, u32[]{:S(2)}, u32[]{:S(2)}) collective-permute-start(f32[4,768]{1,0:T(4,128)S(1)} %get-tuple-element.19), channel_id=1, source_target_pairs={{0,2},{1,3},{2,0},{3,1},{4,6},{5,7},{6,4},{7,5},{8,10},{9,11},{10,... | collective-permute-start | bytes 36872 | tf_op jit(solution)/shard_map/ppermute | solution.py:350
  40.1 3.2 %collective-permute-start.14 = (f32[4,768]{1,0:T(4,128)S(1)}, f32[4,768]{1,0:T(4,128)S(1)}, u32[]{:S(2)}, u32[]{:S(2)}) collective-permute-start(f32[4,768]{1,0:T(4,128)S(1)} %get-tuple-element.20), channel_id=1, source_target_pairs={{0,3},{1,2},{2,1},{3,0},{4,7},{5,6},{6,5},{7,4},{8,11},{9,10},{10,... | collective-permute-start | bytes 36872 | tf_op jit(solution)/shard_map/ppermute | solution.py:350
